TPU v7x, 512 devices: a whole 4x8x8 slice. The times are simulated.
512 devices in a mesh: space: 32 (over y_lo, x, core), member: 16 (over z, y_hi).
Axes of the slice: x: 4, y: 8 (y_hi: 2, y_lo: 4; y = y_hi * 4 + y_lo), z: 8, core: 2. Of those that a mesh axis runs over, the one named last changes fastest.
Arguments:
- anomalies: bfloat16 [256, 256, 256], P('member', 'space'), may hold values from -6 to 6
- loc_blocks: bfloat16 [5, 256, 256], replicated, may hold values from -2 to 2
- tile_reach: int32 [256], P('space'), may hold values from 1 to 4, as said below
- obs_var: float32 [256, 256], P('space', 'member'), may hold values from 0.5 to 2
- innovations: float32 [2, 256, 256], P(None, 'space', 'member'), may hold values from -40 to 40
Outputs:
- increment: float32 [2, 256, 256], P(None, 'space', 'member')
- residual: float32 [2, 256, 256], P(None, 'space', 'member')
Inputs may be any that keep to these rules, and one draw needn't show every extreme that they name: `tile_reach`: some tile has reach 4 and some tile has reach 1.
All inputs are finite; a program needn't handle non-finite values.
Results may differ from a plain program's by a relative error of at most 0.02.
Values may be sent and summed in bfloat16 or wider, within the bound.
No kernel may reach another device: no remote copies, remote signals or barrier semaphores. Data moves between devices by JAX's collectives and lax.ppermute only.
A program may use at most 64 MiB of HBM per device.

v0:
```python
import jax
import jax.numpy as jnp
from jax import lax
from jax.sharding import PartitionSpec as P

W = 4
ITERS = 3


epsilon = 1e-06


def from_behind(block, axis, distance):
    devices = range(lax.axis_size(axis))
    route = [((i - distance) % len(devices), i) for i in devices]
    return lax.ppermute(block, axis, route)


def apply_block(tiles_in, matrix, transposed):
    flattened = tiles_in.reshape(-1, tiles_in.shape[-1])
    if transposed:
        result = lax.dot_general(
            flattened, matrix, (((1,), (1,)), ((), ())), preferred_element_type=jnp.float32
        )
    else:
        result = jnp.dot(flattened, matrix, preferred_element_type=jnp.float32)
    return result.reshape(tiles_in.shape)


def residual_norms(residual):
    return lax.psum(jnp.sum(residual * residual, axis=(1, 2)), ("space", "member"))


def on_device(anomalies, loc_blocks, tile_reach, obs_var, innovations):
    local_tiles = anomalies.shape[1]
    members = anomalies.shape[0] * lax.axis_size("member")
    spread = anomalies.astype(jnp.float32)
    active = (jnp.arange(W + 1, dtype=jnp.int32)[None, :] <= tile_reach[:, None]).astype(
        jnp.bfloat16
    )
    gate_values = active.astype(jnp.float32)
    increment = jnp.zeros(innovations.shape, jnp.float32)
    residual = innovations
    direction = innovations
    norm_now = residual_norms(residual)
    for iteration in range(ITERS):
        full_field = lax.all_gather(direction, "member", axis=2, tiled=True)
        weighted = (spread[:, None] * full_field[None]).astype(jnp.bfloat16)
        spilled = jnp.zeros(weighted.shape[:2] + (local_tiles + W, weighted.shape[3]), jnp.float32)
        for covariance_offset in range(W + 1):
            gated_rows = weighted * active[:, covariance_offset][None, None, :, None]
            covariance_product = apply_block(gated_rows, loc_blocks[covariance_offset], False)
            spilled = spilled + jnp.pad(
                covariance_product,
                ((0, 0), (0, 0), (covariance_offset, W - covariance_offset), (0, 0)),
            )
        arrived = from_behind(spilled[:, :, local_tiles:].astype(jnp.bfloat16), "space", 1).astype(
            jnp.float32
        )
        forward = spilled[:, :, :local_tiles] + jnp.pad(
            arrived, ((0, 0), (0, 0), (0, local_tiles - W), (0, 0))
        )
        forward = forward.astype(jnp.bfloat16)
        leading = from_behind(forward[:, :, :W], "space", -1)
        joined_next = jnp.concatenate([forward, leading], axis=2)
        backward = jnp.zeros(
            joined_next.shape[:2] + (local_tiles, joined_next.shape[3]), jnp.float32
        )
        for offset in range(W + 1):
            product = apply_block(
                joined_next[:, :, offset : offset + local_tiles], loc_blocks[offset], True
            )
            backward = backward + product * gate_values[:, offset][None, None, :, None]
        partial_value = jnp.sum(spread[:, None] * backward, axis=0) / (members - 1)
        totals = lax.psum(partial_value, "member")
        slice_width = totals.shape[2] // lax.axis_size("member")
        totals = lax.dynamic_slice_in_dim(
            totals, lax.axis_index("member") * slice_width, slice_width, 2
        )
        image_field, forward = (totals + obs_var[None] * direction, forward)
        curvature = lax.psum(jnp.sum(direction * image_field, axis=(1, 2)), ("space", "member"))
        step_length = norm_now / curvature
        increment = increment + step_length[:, None, None] * direction
        residual = residual - step_length[:, None, None] * image_field
        if iteration + 1 < ITERS:
            norm_next = residual_norms(residual)
            direction = residual + (norm_next / (norm_now + epsilon))[:, None, None] * direction
            norm_now = norm_next
    return (increment, residual)


def solution(mesh):
    in_specs = (
        P("member", "space", None),
        P(),
        P("space"),
        P("space", "member"),
        P(None, "space", "member"),
    )
    out_specs = (P(None, "space", "member"), P(None, "space", "member"))
    return jax.shard_map(
        on_device, mesh=mesh, in_specs=in_specs, out_specs=out_specs, check_vma=False
    )
```

profile of v0, /device:TPU:1, one launch (start us, length us, event | category | flops | bytes accessed | tf_op | source)
XLA Modules:
  0.0 964.9 jit_solution(11051883178069162289)
XLA Ops:
  0.7 0.7 fusion.193
  1.5 0.9 convert_element_type.135
  2.3 55.8 %all_gather.9 = f32[2,8,256]{1,0,2:T(2,128)S(1)} all-gather(f32[2,8,16]{1,0,2:T(2,128)S(1)} %copy.22), channel_id=1, replica_groups=mesh['space'=32,'member'=16] {'member'}, dimensions={2}, use_global_device_ids=true | all-gather | bytes 17408 | tf_op jit(solution)/shard_map/all_gather | solution.py:47
  59.7 10.6 %collective-permute-start = (bf16[16,2,4,256]{3,2,1,0:T(4,128)(2,1)S(1)}, bf16[16,2,4,256]{3,2,1,0:T(4,128)(2,1)S(1)}, u32[]{:S(2)}, u32[]{:S(2)}) collective-permute-start(bf16[16,2,4,256]{3,2,1,0:T(4,128)(2,1)S(1)} %slice.435), channel_id=1, source_target_pairs={{496,0},{0,16},{16,32},{32,48},{48,64},{64,80},{80,96},{96,112},{1... | collective-permute-start | bytes 196616 | tf_op jit(solution)/shard_map/ppermute | solution.py:16
  70.3 1.3 collective-permute-done
  71.7 7.1 collective-permute-start.1
  80.6 77.5 %psum.64 = f32[2,8,256]{2,1,0:T(8,128)S(1)} all-reduce(f32[2,8,256]{2,1,0:T(8,128)S(1)} %broadcast_multiply_fusion.2), channel_id=1, replica_groups=mesh['space'=32,'member'=16] {'member'}, use_global_device_ids=true, to_apply=%region_3.4 | all-reduce | flops 4096 | bytes 32768 | tf_op jit(solution)/shard_map/psum | solution.py:75
  158.3 106.5 %all-reduce.18 = (f32[2]{0:T(128)S(1)}, f32[2]{0:T(128)S(1)}) all-reduce(f32[2]{0:T(128)S(1)} %get-tuple-element.5, f32[2]{0:T(128)S(1)} %get-tuple-element.4), channel_id=1, replica_groups=mesh['space'=32,'member'=16] {'space','member'}, use_global_device_ids=true, to_apply=%region_1.0 | all-reduce | flops 4 | bytes 32 | tf_op jit(solution)/shard_map/psum | solution.py:31
  265.0 95.5 %psum.66 = f32[2]{0:T(128)S(1)} all-reduce(f32[2]{0:T(128)S(1)} %multiply_reduce_fusion.3), channel_id=1, replica_groups=mesh['space'=32,'member'=16] {'space','member'}, use_global_device_ids=true, to_apply=%region_7.8 | all-reduce | flops 2 | bytes 16 | tf_op jit(solution)/shard_map/psum | solution.py:31
  360.6 46.4 %all_gather.10 = f32[2,8,256]{1,0,2:T(2,128)S(1)} all-gather(f32[2,8,16]{1,0,2:T(2,128)S(1)} %copy.24), channel_id=1, replica_groups=mesh['space'=32,'member'=16] {'member'}, dimensions={2}, use_global_device_ids=true | all-gather | bytes 17408 | tf_op jit(solution)/shard_map/all_gather | solution.py:47
  408.6 10.6 %collective-permute-start.2 = (bf16[16,2,4,256]{3,2,1,0:T(4,128)(2,1)S(1)}, bf16[16,2,4,256]{3,2,1,0:T(4,128)(2,1)S(1)}, u32[]{:S(2)}, u32[]{:S(2)}) collective-permute-start(bf16[16,2,4,256]{3,2,1,0:T(4,128)(2,1)S(1)} %slice.434), channel_id=1, source_target_pairs={{496,0},{0,16},{16,32},{32,48},{48,64},{64,80},{80,96},{96,112},{1... | collective-permute-start | bytes 196616 | tf_op jit(solution)/shard_map/ppermute | solution.py:16
  419.2 1.3 collective-permute-done.2
  420.6 7.5 collective-permute-start.3
  429.9 77.7 %psum.67 = f32[2,8,256]{2,1,0:T(8,128)S(1)} all-reduce(f32[2,8,256]{2,1,0:T(8,128)S(1)} %broadcast_multiply_fusion.1), channel_id=1, replica_groups=mesh['space'=32,'member'=16] {'member'}, use_global_device_ids=true, to_apply=%region_9.10 | all-reduce | flops 4096 | bytes 32768 | tf_op jit(solution)/shard_map/psum | solution.py:75
  507.7 106.6 %psum.68 = f32[2]{0:T(128)S(1)} all-reduce(f32[2]{0:T(128)S(1)} %multiply_reduce_fusion.2), channel_id=1, replica_groups=mesh['space'=32,'member'=16] {'space','member'}, use_global_device_ids=true, to_apply=%region_11.12 | all-reduce | flops 2 | bytes 16 | tf_op jit(solution)/shard_map/psum | solution.py:81
  614.5 95.5 %psum.69 = f32[2]{0:T(128)S(1)} all-reduce(f32[2]{0:T(128)S(1)} %get-tuple-element.8), channel_id=1, replica_groups=mesh['space'=32,'member'=16] {'space','member'}, use_global_device_ids=true, to_apply=%region_13.14 | all-reduce | flops 2 | bytes 16 | tf_op jit(solution)/shard_map/psum | solution.py:31
  710.1 45.7 %all_gather.11 = f32[2,8,256]{1,0,2:T(2,128)S(1)} all-gather(f32[2,8,16]{1,0,2:T(2,128)S(1)} %copy.26), channel_id=1, replica_groups=mesh['space'=32,'member'=16] {'member'}, dimensions={2}, use_global_device_ids=true | all-gather | bytes 17408 | tf_op jit(solution)/shard_map/all_gather | solution.py:47
  757.4 10.9 %collective-permute-start.4 = (bf16[16,2,4,256]{3,2,1,0:T(4,128)(2,1)S(1)}, bf16[16,2,4,256]{3,2,1,0:T(4,128)(2,1)S(1)}, u32[]{:S(2)}, u32[]{:S(2)}) collective-permute-start(bf16[16,2,4,256]{3,2,1,0:T(4,128)(2,1)S(1)} %slice.433), channel_id=1, source_target_pairs={{496,0},{0,16},{16,32},{32,48},{48,64},{64,80},{80,96},{96,112},{1... | collective-permute-start | bytes 196616 | tf_op jit(solution)/shard_map/ppermute | solution.py:16
  768.3 1.3 collective-permute-done.4
  769.7 7.4 collective-permute-start.5
  777.3 0.7 collective-permute-done.5
  778.9 78.4 %psum.70 = f32[2,8,256]{2,1,0:T(8,128)S(1)} all-reduce(f32[2,8,256]{2,1,0:T(8,128)S(1)} %broadcast_multiply_fusion), channel_id=1, replica_groups=mesh['space'=32,'member'=16] {'member'}, use_global_device_ids=true, to_apply=%region_15.16 | all-reduce | flops 4096 | bytes 32768 | tf_op jit(solution)/shard_map/psum | solution.py:75
  857.5 106.7 %psum.71 = f32[2]{0:T(128)S(1)} all-reduce(f32[2]{0:T(128)S(1)} %multiply_reduce_fusion), channel_id=1, replica_groups=mesh['space'=32,'member'=16] {'space','member'}, use_global_device_ids=true, to_apply=%region_17.18 | all-reduce | flops 2 | bytes 16 | tf_op jit(solution)/shard_map/psum | solution.py:81
  964.2 0.7 multiply_subtract_fusion
  (73 shorter events, 10.7 us)
Async XLA Ops:
  0.6 0.8 copy-start.1
  0.6 57.6 %copy-start = (bf16[5,256,256]{2,1,0:T(8,128)(2,1)S(1)}, bf16[5,256,256]{2,1,0:T(8,128)(2,1)}, u32[]{:S(2)}) copy-start(bf16[5,256,256]{2,1,0:T(8,128)(2,1)} %param.6) | copy-start | bytes 1966084
  59.7 11.9 %collective-permute-start = (bf16[16,2,4,256]{3,2,1,0:T(4,128)(2,1)S(1)}, bf16[16,2,4,256]{3,2,1,0:T(4,128)(2,1)S(1)}, u32[]{:S(2)}, u32[]{:S(2)}) collective-permute-start(bf16[16,2,4,256]{3,2,1,0:T(4,128)(2,1)S(1)} %slice.435), channel_id=1, source_target_pairs={{496,0},{0,16},{16,32},{32,48},{48,64},{64,80},{80,96},{96,112},{1... | collective-permute-start | bytes 196616 | tf_op jit(solution)/shard_map/ppermute | solution.py:16
  71.7 8.0 collective-permute-start.1
  80.6 77.6 %copy-start.2 = (f32[8,16]{1,0:T(8,128)S(1)}, f32[8,16]{1,0:T(8,128)}, u32[]{:S(2)}) copy-start(f32[8,16]{1,0:T(8,128)} %param.8) | copy-start | bytes 1540
  408.6 11.9 %collective-permute-start.2 = (bf16[16,2,4,256]{3,2,1,0:T(4,128)(2,1)S(1)}, bf16[16,2,4,256]{3,2,1,0:T(4,128)(2,1)S(1)}, u32[]{:S(2)}, u32[]{:S(2)}) collective-permute-start(bf16[16,2,4,256]{3,2,1,0:T(4,128)(2,1)S(1)} %slice.434), channel_id=1, source_target_pairs={{496,0},{0,16},{16,32},{32,48},{48,64},{64,80},{80,96},{96,112},{1... | collective-permute-start | bytes 196616 | tf_op jit(solution)/shard_map/ppermute | solution.py:16
  420.6 8.4 collective-permute-start.3
  757.4 12.3 %collective-permute-start.4 = (bf16[16,2,4,256]{3,2,1,0:T(4,128)(2,1)S(1)}, bf16[16,2,4,256]{3,2,1,0:T(4,128)(2,1)S(1)}, u32[]{:S(2)}, u32[]{:S(2)}) collective-permute-start(bf16[16,2,4,256]{3,2,1,0:T(4,128)(2,1)S(1)} %slice.433), channel_id=1, source_target_pairs={{496,0},{0,16},{16,32},{32,48},{48,64},{64,80},{80,96},{96,112},{1... | collective-permute-start | bytes 196616 | tf_op jit(solution)/shard_map/ppermute | solution.py:16
  769.7 8.2 collective-permute-start.5
where the time goes:
time: 966 us; the launch traced here: 965 us
  blocking collectives  892 us (92%)
  starting transfers between devices  54 us (6%)
    psum x3, blocking collectives, residual_norms(): lax.psum(jnp.sum(residual * residual, axis=(1, 2)), ('space', 'member'))  297 us
    psum x3, blocking collectives, on_device(): totals = lax.psum(partial_value, 'member')  234 us
    psum x2, blocking collectives, on_device(): lax.psum(jnp.sum(direction * image_field, axis=(1, 2)), ('space', 'member'))  213 us
    all_gather x3, blocking collectives, on_device(): full_field = lax.all_gather(direction, 'member', axis=2, tiled=True)  148 us
    ppermute x6, starting transfers between devices, from_behind(): return lax.ppermute(block, axis, route)  54 us
  transfers between devices with their start and end apart: 6, of which 6 were waited for; matrix products, arithmetic and copies ran while one was open for 0% of the time, Pallas kernels for 0%

commit v1 on v0

v1 whole, which is shorter than its diff:
```python
import jax
import jax.numpy as jnp
from jax import lax
from jax.experimental import pallas as pl
from jax.experimental.pallas import tpu as pltpu
from jax.sharding import PartitionSpec as P

W = 4
ITERS = 3
EPSILON = 1e-6
SCALE = 2.0**-8

VM = pl.BlockSpec(memory_space=pltpu.VMEM)
SM = pl.BlockSpec(memory_space=pltpu.SMEM)

BASE = [0, 5, 9, 12, 14]
BASE_T = [0, 15, 19, 22, 24]
N_TABLE = 26


def from_behind(block, axis, distance):
    n = lax.axis_size(axis)
    return lax.ppermute(block, axis, [((i - distance) % n, i) for i in range(n)])


def row_products(a, b):
    return lax.dot_general(a, b, (((1,), (1,)), ((), ())), preferred_element_type=jnp.float32)


def table_kernel(loc_ref, t_ref):
    k = 0
    for d in range(W + 1):
        total = None
        for o in range(W + 1 - d):
            p = row_products(loc_ref[o + d], loc_ref[o])
            total = p if total is None else total + p
            t_ref[k] = total
            k += 1
    for d in range(1, W + 1):
        total = None
        for o in range(W + 1 - d):
            p = row_products(loc_ref[o], loc_ref[o + d])
            total = p if total is None else total + p
            t_ref[k] = total
            k += 1
    t_ref[k] = jnp.zeros(t_ref.shape[1:], jnp.float32)


def make_tables(loc_blocks):
    return pl.pallas_call(
        table_kernel,
        out_shape=jax.ShapeDtypeStruct((N_TABLE,) + loc_blocks.shape[1:], jnp.float32),
        in_specs=[VM],
        out_specs=VM,
        compiler_params=pltpu.CompilerParams(vmem_limit_bytes=20 << 20),
    )(loc_blocks)


def apply_kernel(reach_ref, own_ref, left_ref, right_ref, t_ref, v_ref, obs_ref, y_ref, xs):
    for w in range(4):
        xs[w] = left_ref[:, 1 + w].reshape(256, 256)
        xs[4 + w] = own_ref[:, w].reshape(256, 256)
        xs[8 + w] = own_ref[:, 5 + w].reshape(256, 256)
        xs[12 + w] = right_ref[:, w].reshape(256, 256)

    def tile(w, carry):
        rows = xs[w + W].T
        reach_w = reach_ref[w + W]
        acc = [jnp.zeros((256, 128), jnp.float32) for _ in range(2)]
        for shift in range(-W, W + 1):
            d = abs(shift)
            other = w + W + shift
            covariance = jnp.dot(rows, xs[other], preferred_element_type=jnp.float32)
            reach_o = reach_ref[other]
            if shift >= 0:
                last, base = jnp.minimum(reach_o, reach_w - d), BASE[d]
            else:
                last, base = jnp.minimum(reach_w, reach_o - d), BASE_T[d]
            entry = jnp.where(last >= 0, base + last, N_TABLE - 1)
            block = covariance * t_ref[entry]
            for f in range(2):
                p = block * v_ref[f, pl.ds(other, 1), :]
                acc[f] = acc[f] + (p[:, :128] + p[:, 128:])
        for f in range(2):
            row = jnp.sum(acc[f].T, axis=0, keepdims=True)
            y_ref[f, pl.ds(w, 1), :] = (
                row * (1.0 / 255.0) + obs_ref[pl.ds(w, 1), :] * v_ref[f, pl.ds(w + W, 1), :]
            ) * SCALE
        return carry

    lax.fori_loop(0, 8, tile, 0)


def apply_operator(reach, own, left, right, table, v, obs):
    return pl.pallas_call(
        apply_kernel,
        out_shape=jax.ShapeDtypeStruct((2, 8, 256), jnp.float32),
        in_specs=[SM] + [VM] * 6,
        out_specs=VM,
        scratch_shapes=[pltpu.VMEM((16, 256, 256), jnp.bfloat16)],
        compiler_params=pltpu.CompilerParams(vmem_limit_bytes=30 << 20),
    )(reach, own, left, right, table, v, obs)


def moments_kernel(p0_ref, p1_ref, p2_ref, p3_ref, m_ref):
    p = [p0_ref, p1_ref, p2_ref, p3_ref]
    lane = lax.broadcasted_iota(jnp.int32, (1, 128), 1)
    out = jnp.zeros((1, 128), jnp.float32)
    for k in range(2 * ITERS):
        for f in range(2):
            value = jnp.sum(p[k // 2][f] * p[(k + 1) // 2][f], keepdims=True)
            out = out + jnp.where(lane == 2 * k + f, value, 0.0)
    m_ref[...] = out


def local_moments(p):
    return pl.pallas_call(
        moments_kernel,
        out_shape=jax.ShapeDtypeStruct((1, 128), jnp.float32),
        in_specs=[VM] * 4,
        out_specs=VM,
    )(*p)


def poly_add(a, b):
    n = max(len(a), len(b))
    out = []
    for i in range(n):
        if i >= len(a):
            out.append(b[i])
        elif i >= len(b):
            out.append(a[i])
        else:
            out.append(a[i] + b[i])
    return out


def poly_dot(a, b, moment):
    total = None
    for i, x in enumerate(a):
        for j, y in enumerate(b):
            if x is None or y is None:
                continue
            term = x * y * moment[i + j]
            total = term if total is None else total + term
    return total


def finish_kernel(m_ref, p0_ref, p1_ref, p2_ref, p3_ref, inc_ref, res_ref):
    p = [p0_ref, p1_ref, p2_ref, p3_ref]
    lane = lax.broadcasted_iota(jnp.int32, (1, 128), 1)
    sums = jnp.sum(m_ref[...], axis=0, keepdims=True)
    one = jnp.ones((1, 1), jnp.float32)
    zero = jnp.zeros((1, 1), jnp.float32)
    for f in range(2):
        moment = [
            jnp.sum(jnp.where(lane == 2 * k + f, sums, 0.0), axis=1, keepdims=True)
            for k in range(2 * ITERS)
        ]
        residual, direction, increment = [one], [one], []
        norm_now = moment[0]
        for iteration in range(ITERS):
            image = [None] + direction
            step = norm_now / poly_dot(direction, image, moment)
            increment = poly_add(increment, [step * c for c in direction])
            residual = poly_add(residual, [zero] + [-step * c for c in direction])
            if iteration + 1 < ITERS:
                norm_next = poly_dot(residual, residual, moment)
                ratio = norm_next / (norm_now + EPSILON)
                direction = poly_add(residual, [ratio * c for c in direction])
                norm_now = norm_next
        inc_ref[f] = sum(c * p[i][f] for i, c in enumerate(increment)) * SCALE
        res_ref[f] = sum(c * p[i][f] for i, c in enumerate(residual))


def finish(m, p):
    shape = jax.ShapeDtypeStruct(p[0].shape, jnp.float32)
    return pl.pallas_call(
        finish_kernel,
        out_shape=(shape, shape),
        in_specs=[VM] * 5,
        out_specs=(VM, VM),
    )(m, *p)


def three_pieces(x):
    high = lax.reduce_precision(x, 8, 7)
    rest = x - high
    middle = lax.reduce_precision(rest, 8, 7)
    return jnp.stack([high, middle, rest - middle]).astype(jnp.bfloat16)


def on_device(anomalies, loc_blocks, tile_reach, obs_var, innovations):
    table = make_tables(loc_blocks)
    mine = jnp.concatenate([innovations, obs_var[None]])
    extra = jnp.concatenate([three_pieces(mine).reshape(-1), tile_reach.astype(jnp.bfloat16)])
    extra = jnp.pad(extra, (0, 4096 - extra.shape[0])).reshape(1, 16, 256)
    by_tile = anomalies.transpose(1, 0, 2)
    chunk = jnp.concatenate([by_tile[:4], extra, by_tile[4:]])
    own = lax.all_to_all(jnp.broadcast_to(chunk[None], (16,) + chunk.shape), "member", 0, 0)
    left = from_behind(own[:, 4:], "space", 1)
    right = from_behind(own[:, :5], "space", -1)
    extras = jnp.stack([left[:, 0], own[:, 4], right[:, 4]]).reshape(3, 16, 4096)
    reaches = extras[:, 0, 1152:1160].astype(jnp.int32)
    reach = jnp.concatenate([reaches[0, 4:], reaches[1], reaches[2, :4]])
    pieces = extras[:, :, :1152].astype(jnp.float32).reshape(3, 16, 3, 3, 8, 16)
    values = pieces[:, :, 0] + (pieces[:, :, 1] + pieces[:, :, 2])
    values = values.transpose(0, 2, 3, 1, 4).reshape(3, 3, 8, 256)
    obs = values[1, 2]
    v = jnp.concatenate([values[0, :2, 4:], values[1, :2], values[2, :2, :4]], axis=1)
    p = [values[1, :2]]
    for power in range(ITERS):
        if power:
            before = from_behind(p[-1][:, 4:], "space", 1)
            after = from_behind(p[-1][:, :4], "space", -1)
            v = jnp.concatenate([before, p[-1], after], axis=1)
        p.append(apply_operator(reach, own, left, right, table, v, obs))
    m = local_moments(p)
    m = lax.all_to_all(jnp.broadcast_to(m, (32, 128)), "space", 0, 0, tiled=True)
    increment, residual = finish(m, p)
    start = lax.axis_index("member") * 16
    return (
        lax.dynamic_slice_in_dim(increment, start, 16, 2),
        lax.dynamic_slice_in_dim(residual, start, 16, 2),
    )


def solution(mesh):
    in_specs = (
        P("member", "space", None),
        P(),
        P("space"),
        P("space", "member"),
        P(None, "space", "member"),
    )
    out_specs = (P(None, "space", "member"), P(None, "space", "member"))
    return jax.shard_map(
        on_device, mesh=mesh, in_specs=in_specs, out_specs=out_specs, check_vma=False
    )
```

time: 966 us -> 145 us (0.15)
  blocking collectives: 892 us -> 45.1 us
  Pallas kernels: 0 us -> 25.1 us
  local copies, waits for them, and re-layouts: 0.69 us -> 17.7 us
  starting transfers between devices: 54 us -> 37.6 us
    psum x8 -> x0, blocking collectives: 744 us -> none  [the longest x3 297 us: residual_norms(): lax.psum(jnp.sum(residual * residual, axis=(1, 2)), ('space', 'member'))]
    all_gather x3 -> x0, blocking collectives: 148 us -> none  [on_device(): full_field = lax.all_gather(direction, 'member', axis=2, tiled=True)]
    all_to_all x0 -> x1, blocking collectives: none -> 45.1 us  [on_device(): lax.all_to_all(jnp.broadcast_to(chunk[None], (16,) + chunk.shape), 'membe...]
    ppermute x6, starting transfers between devices: 54 us -> 24.3 us  [from_behind(): lax.ppermute(block, axis, [((i - distance) % n, i) for i in range(n)])]
    pallas_call x0 -> x6, Pallas kernels: none -> 25.1 us  [the longest x3 21.1 us: apply_operator(): pl.pallas_call(apply_kernel, out_shape=jax.ShapeDtypeStruct((2, 8, 256),...]
    all_to_all x0 -> x1, starting transfers between devices: none -> 13.2 us  [on_device(): lax.all_to_all(jnp.broadcast_to(m, (32, 128)), 'space', 0, 0, tiled=True)]
  transfers between devices with their start and end apart: 6 -> 7, of which waited for: 6 -> 5; matrix products, arithmetic and copies ran while one was open for 0% -> 1% of each run, Pallas kernels for 0% -> 1%
where the time goes in v1:
time: 145 us; the launch traced here: 144 us
  blocking collectives  45.1 us (31%)
  starting transfers between devices  37.6 us (26%)
  Pallas kernels  25.1 us (17%)
  local copies, waits for them, and re-layouts  17.7 us (12%)
  waiting for transfers between devices  14.4 us (10%)
  other arithmetic  3.48 us (2%)
    all_to_all x1, blocking collectives, on_device(): lax.all_to_all(jnp.broadcast_to(chunk[None], (16,) + chunk.shape), 'membe...  45.1 us
    ppermute x6, starting transfers between devices, from_behind(): lax.ppermute(block, axis, [((i - distance) % n, i) for i in range(n)])  24.3 us
    pallas_call x3, Pallas kernels, apply_operator(): pl.pallas_call(apply_kernel, out_shape=jax.ShapeDtypeStruct((2, 8, 256),...  21.1 us
    all_to_all x1, starting transfers between devices, on_device(): lax.all_to_all(jnp.broadcast_to(m, (32, 128)), 'space', 0, 0, tiled=True)  13.2 us
    unnamed x19, local copies, waits for them, and re-layouts  8.31 us
    all_to_all x1, waiting for transfers between devices, on_device(): lax.all_to_all(jnp.broadcast_to(m, (32, 128)), 'space', 0, 0, tiled=True)  7.31 us
    ppermute x6, waiting for transfers between devices, from_behind(): lax.ppermute(block, axis, [((i - distance) % n, i) for i in range(n)])  7.14 us
  transfers between devices with their start and end apart: 7, of which 5 were waited for; matrix products, arithmetic and copies ran while one was open for 1% of the time, Pallas kernels for 1%

profile of v1, /device:TPU:1, one launch (start us, length us, event | category | flops | bytes accessed | tf_op | source)
XLA Modules:
  0.0 144.3 jit_solution(18281746877065471821)
XLA Ops:
  2.2 0.9 fusion.8
  3.3 45.1 %all_to_all.13.own_ref = bf16[16,9,16,256]{3,2,1,0:T(8,128)(2,1)S(1)} all-to-all(bf16[16,9,16,256]{3,2,1,0:T(8,128)(2,1)S(1)} %broadcast_in_dim.4), channel_id=1, replica_groups=mesh['space'=32,'member'=16] {'member'}, dimensions={0} | all-to-all | bytes 2359296 | tf_op jit(solution)/shard_map/all_to_all | solution.py:200
  49.4 6.0 %collective-permute-start = (bf16[16,5,16,256]{3,2,1,0:T(8,128)(2,1)}, bf16[16,5,16,256]{3,2,1,0:T(8,128)(2,1)S(1)}, u32[]{:S(2)}, u32[]{:S(2)}) collective-permute-start(bf16[16,5,16,256]{3,2,1,0:T(8,128)(2,1)} %get-tuple-element.10), channel_id=1, source_target_pairs={{496,0},{0,16},{16,32},{32,48},{48,64},{64,80},{80,96},{96,112},{1... | collective-permute-start | bytes 1966088 | tf_op jit(solution)/shard_map/ppermute | solution.py:23
  55.4 1.9 %collective-permute-start.1 = (bf16[16,5,16,256]{3,2,1,0:T(8,128)(2,1)S(1)}, bf16[16,5,16,256]{3,2,1,0:T(8,128)(2,1)S(1)}, u32[]{:S(2)}, u32[]{:S(2)}) collective-permute-start(bf16[16,5,16,256]{3,2,1,0:T(8,128)(2,1)S(1)} %get-tuple-element.9), channel_id=1, source_target_pairs={{16,0},{32,16},{48,32},{64,48},{80,64},{96,80},{112,96},{128,112},... | collective-permute-start | bytes 1966088 | tf_op jit(solution)/shard_map/ppermute | solution.py:23
  57.4 1.0 shard_map.68.t_ref
  58.4 2.8 %copy-done = f32[26,256,256]{2,1,0:T(8,128)} copy-done((f32[26,256,256]{2,1,0:T(8,128)}, f32[26,256,256]{2,1,0:T(8,128)S(1)}, u32[]{:S(2)}) %copy-start) | copy-done | bytes 6815768
  61.3 1.9 %collective-permute-done.left_ref = bf16[16,5,16,256]{3,2,1,0:T(8,128)(2,1)S(1)} collective-permute-done((bf16[16,5,16,256]{3,2,1,0:T(8,128)(2,1)}, bf16[16,5,16,256]{3,2,1,0:T(8,128)(2,1)S(1)}, u32[]{:S(2)}, u32[]{:S(2)}) %collective-permute-start) | collective-permute-done | bytes 655392 | tf_op jit(solution)/shard_map/ppermute | solution.py:23
  64.0 3.6 %collective-permute-done.1.right_ref = bf16[16,5,16,256]{3,2,1,0:T(8,128)(2,1)S(1)} collective-permute-done((bf16[16,5,16,256]{3,2,1,0:T(8,128)(2,1)S(1)}, bf16[16,5,16,256]{3,2,1,0:T(8,128)(2,1)S(1)}, u32[]{:S(2)}, u32[]{:S(2)}) %collective-permute-start.1) | collective-permute-done | bytes 655392 | tf_op jit(solution)/shard_map/ppermute | solution.py:23
  70.0 1.9 %reshape.139 = f32[3,16,3,3,8,16]{5,4,3,2,1,0:T(8,128)} reshape(f32[3,16,1152]{2,1,0:T(8,128)S(1)} %slice_convert_fusion) | data formatting | bytes 442368 | tf_op jit(solution)/shard_map/reshape | solution.py:206
  71.8 1.5 %fusion.6 = (f32[3,16,1,3,8,16]{5,4,3,2,1,0:T(8,128)S(1)}, f32[3,16,1,3,8,16]{5,4,3,2,1,0:T(8,128)S(1)}, f32[3,16,1,3,8,16]{5,4,3,2,1,0:T(8,128)S(1)}) fusion(f32[3,16,3,3,8,16]{5,4,3,2,1,0:T(8,128)} %reshape.139), kind=kLoop, calls=%fused_computation.34 | loop fusion | bytes 442368 | tf_op jit(solution)/shard_map/slice | solution.py:207
  74.8 2.9 %copy-done.1 = f32[26,256,256]{2,1,0:T(8,128)S(1)} copy-done((f32[26,256,256]{2,1,0:T(8,128)S(1)}, f32[26,256,256]{2,1,0:T(8,128)}, u32[]{:S(2)}) %copy-start.1) | copy-done | bytes 6815768
  77.7 7.0 %shard_map.69.p1_ref = f32[2,8,256]{2,1,0:T(8,128)S(1)} custom-call(s32[16]{0:T(128)S(1)} %pad_add_fusion.reach_ref, bf16[16,9,16,256]{3,2,1,0:T(8,128)(2,1)S(1)} %all_to_all.13.own_ref, bf16[16,5,16,256]{3,2,1,0:T(8,128)(2,1)S(1)} %collective-permute-done.left_ref, bf16[16,5,16,256]{3,2,1,0:T(8,128)(2,1)S(1)} %collective-permute-done.1.right_ref, ...), custom_call_target="tpu_custom_call" | custom-call | tf_op jit(solution)/shard_map/pallas_call | solution.py:95
  84.8 1.9 %collective-permute-start.2 = (f32[2,4,256]{2,1,0:T(4,128)S(1)}, f32[2,4,256]{2,1,0:T(4,128)S(1)}, u32[]{:S(2)}, u32[]{:S(2)}) collective-permute-start(f32[2,4,256]{2,1,0:T(4,128)S(1)} %get-tuple-element.17), channel_id=1, source_target_pairs={{496,0},{0,16},{16,32},{32,48},{48,64},{64,80},{80,96},{96,112},{1... | collective-permute-start | bytes 24584 | tf_op jit(solution)/shard_map/ppermute | solution.py:23
  86.7 4.3 %collective-permute-start.3 = (f32[2,4,256]{2,1,0:T(4,128)S(1)}, f32[2,4,256]{2,1,0:T(4,128)S(1)}, u32[]{:S(2)}, u32[]{:S(2)}) collective-permute-start(f32[2,4,256]{2,1,0:T(4,128)S(1)} %get-tuple-element.18), channel_id=1, source_target_pairs={{16,0},{32,16},{48,32},{64,48},{80,64},{96,80},{112,96},{128,112},... | collective-permute-start | bytes 24584 | tf_op jit(solution)/shard_map/ppermute | solution.py:23
  91.8 7.0 %shard_map.70.p2_ref = f32[2,8,256]{2,1,0:T(8,128)S(1)} custom-call(s32[16]{0:T(128)S(1)} %pad_add_fusion.reach_ref, bf16[16,9,16,256]{3,2,1,0:T(8,128)(2,1)S(1)} %all_to_all.13.own_ref, bf16[16,5,16,256]{3,2,1,0:T(8,128)(2,1)S(1)} %collective-permute-done.left_ref, bf16[16,5,16,256]{3,2,1,0:T(8,128)(2,1)S(1)} %collective-permute-done.1.right_ref, ...), custom_call_target="tpu_custom_call" | custom-call | tf_op jit(solution)/shard_map/pallas_call | solution.py:95
  98.9 1.9 %collective-permute-start.4 = (f32[2,4,256]{2,1,0:T(4,128)S(1)}, f32[2,4,256]{2,1,0:T(4,128)S(1)}, u32[]{:S(2)}, u32[]{:S(2)}) collective-permute-start(f32[2,4,256]{2,1,0:T(4,128)S(1)} %get-tuple-element.15), channel_id=1, source_target_pairs={{496,0},{0,16},{16,32},{32,48},{48,64},{64,80},{80,96},{96,112},{1... | collective-permute-start | bytes 24584 | tf_op jit(solution)/shard_map/ppermute | solution.py:23
  100.8 8.3 %collective-permute-start.5 = (f32[2,4,256]{2,1,0:T(4,128)S(1)}, f32[2,4,256]{2,1,0:T(4,128)S(1)}, u32[]{:S(2)}, u32[]{:S(2)}) collective-permute-start(f32[2,4,256]{2,1,0:T(4,128)S(1)} %get-tuple-element.16), channel_id=1, source_target_pairs={{16,0},{32,16},{48,32},{64,48},{80,64},{96,80},{112,96},{128,112},... | collective-permute-start | bytes 24584 | tf_op jit(solution)/shard_map/ppermute | solution.py:23
  109.9 7.0 %shard_map.71.p3_ref = f32[2,8,256]{2,1,0:T(8,128)S(1)} custom-call(s32[16]{0:T(128)S(1)} %pad_add_fusion.reach_ref, bf16[16,9,16,256]{3,2,1,0:T(8,128)(2,1)S(1)} %all_to_all.13.own_ref, bf16[16,5,16,256]{3,2,1,0:T(8,128)(2,1)S(1)} %collective-permute-done.left_ref, bf16[16,5,16,256]{3,2,1,0:T(8,128)(2,1)S(1)} %collective-permute-done.1.right_ref, ...), custom_call_target="tpu_custom_call" | custom-call | tf_op jit(solution)/shard_map/pallas_call | solution.py:95
  117.6 1.4 shard_map.72
  119.0 1.3 broadcast_in_dim.5
  120.2 13.2 %all-to-all-start.1 = ((f32[32,1,128]{2,1,0:T(1,128)}), f32[32,1,128]{2,1,0:T(1,128)S(1)}, u32[]{:S(2)}, u32[]{:S(2)}) async-start(f32[32,1,128]{2,1,0:T(1,128)} %broadcast_in_dim.5), calls=%async_computation.1 | async-start | bytes 32768 | tf_op jit(solution)/shard_map/all_to_all | solution.py:219
  133.5 7.3 %all-to-all-done.1 = f32[32,1,128]{2,1,0:T(1,128)S(1)} async-done(((f32[32,1,128]{2,1,0:T(1,128)}), f32[32,1,128]{2,1,0:T(1,128)S(1)}, u32[]{:S(2)}, u32[]{:S(2)}) %all-to-all-start.1) | async-done | bytes 16416 | tf_op jit(solution)/shard_map/all_to_all | solution.py:219
  141.4 1.5 %shard_map.73 = (f32[2,8,256]{2,1,0:T(8,128)}, f32[2,8,256]{2,1,0:T(8,128)}) custom-call(f32[32,128]{1,0:T(8,128)} %bitcast.36, f32[2,8,256]{2,1,0:T(8,128)} %copy-done.6, f32[2,8,256]{2,1,0:T(8,128)} %copy-done.3, f32[2,8,256]{2,1,0:T(8,128)} %copy-done.4, f32[2,8,256]{2,1,0:T(8,128)} %copy-done.5), custom_call_target="tpu_custom_call" | custom-call | tf_op jit(solution)/shard_map/pallas_call | solution.py:178
  142.9 1.4 constant_dynamic-slice_fusion
  (53 shorter events, 10.0 us)
Async XLA Ops:
  48.4 8.9 %copy-start.2 = (bf16[5,256,256]{2,1,0:T(8,128)(2,1)S(1)}, bf16[5,256,256]{2,1,0:T(8,128)(2,1)}, u32[]{:S(2)}) copy-start(bf16[5,256,256]{2,1,0:T(8,128)(2,1)} %loc_ref.1) | copy-start | bytes 1966084
  49.4 13.9 %collective-permute-start = (bf16[16,5,16,256]{3,2,1,0:T(8,128)(2,1)}, bf16[16,5,16,256]{3,2,1,0:T(8,128)(2,1)S(1)}, u32[]{:S(2)}, u32[]{:S(2)}) collective-permute-start(bf16[16,5,16,256]{3,2,1,0:T(8,128)(2,1)} %get-tuple-element.10), channel_id=1, source_target_pairs={{496,0},{0,16},{16,32},{32,48},{48,64},{64,80},{80,96},{96,112},{1... | collective-permute-start | bytes 1966088 | tf_op jit(solution)/shard_map/ppermute | solution.py:23
  55.4 12.2 %collective-permute-start.1 = (bf16[16,5,16,256]{3,2,1,0:T(8,128)(2,1)S(1)}, bf16[16,5,16,256]{3,2,1,0:T(8,128)(2,1)S(1)}, u32[]{:S(2)}, u32[]{:S(2)}) collective-permute-start(bf16[16,5,16,256]{3,2,1,0:T(8,128)(2,1)S(1)} %get-tuple-element.9), channel_id=1, source_target_pairs={{16,0},{32,16},{48,32},{64,48},{80,64},{96,80},{112,96},{128,112},... | collective-permute-start | bytes 1966088 | tf_op jit(solution)/shard_map/ppermute | solution.py:23
  58.4 2.8 %copy-start = (f32[26,256,256]{2,1,0:T(8,128)}, f32[26,256,256]{2,1,0:T(8,128)S(1)}, u32[]{:S(2)}) copy-start(f32[26,256,256]{2,1,0:T(8,128)S(1)} %shard_map.68.t_ref) | copy-start | bytes 20447236
  73.9 10.9 %copy-start.6 = (f32[2,8,256]{2,1,0:T(8,128)}, f32[2,8,256]{2,1,0:T(8,128)S(1)}, u32[]{:S(2)}) copy-start(f32[2,8,256]{2,1,0:T(8,128)S(1)} %slice_bitcast_fusion.p0_ref) | copy-start | bytes 49156
  74.8 2.9 %copy-start.1 = (f32[26,256,256]{2,1,0:T(8,128)S(1)}, f32[26,256,256]{2,1,0:T(8,128)}, u32[]{:S(2)}) copy-start(f32[26,256,256]{2,1,0:T(8,128)} %copy-done) | copy-start | bytes 20447236
  84.8 14.1 %copy-start.3 = (f32[2,8,256]{2,1,0:T(8,128)}, f32[2,8,256]{2,1,0:T(8,128)S(1)}, u32[]{:S(2)}) copy-start(f32[2,8,256]{2,1,0:T(8,128)S(1)} %shard_map.69.p1_ref) | copy-start | bytes 49156
  84.8 6.2 %collective-permute-start.2 = (f32[2,4,256]{2,1,0:T(4,128)S(1)}, f32[2,4,256]{2,1,0:T(4,128)S(1)}, u32[]{:S(2)}, u32[]{:S(2)}) collective-permute-start(f32[2,4,256]{2,1,0:T(4,128)S(1)} %get-tuple-element.17), channel_id=1, source_target_pairs={{496,0},{0,16},{16,32},{32,48},{48,64},{64,80},{80,96},{96,112},{1... | collective-permute-start | bytes 24584 | tf_op jit(solution)/shard_map/ppermute | solution.py:23
  86.7 5.1 %collective-permute-start.3 = (f32[2,4,256]{2,1,0:T(4,128)S(1)}, f32[2,4,256]{2,1,0:T(4,128)S(1)}, u32[]{:S(2)}, u32[]{:S(2)}) collective-permute-start(f32[2,4,256]{2,1,0:T(4,128)S(1)} %get-tuple-element.18), channel_id=1, source_target_pairs={{16,0},{32,16},{48,32},{64,48},{80,64},{96,80},{112,96},{128,112},... | collective-permute-start | bytes 24584 | tf_op jit(solution)/shard_map/ppermute | solution.py:23
  98.9 18.1 %copy-start.4 = (f32[2,8,256]{2,1,0:T(8,128)}, f32[2,8,256]{2,1,0:T(8,128)S(1)}, u32[]{:S(2)}) copy-start(f32[2,8,256]{2,1,0:T(8,128)S(1)} %shard_map.70.p2_ref) | copy-start | bytes 49156
  98.9 10.2 %collective-permute-start.4 = (f32[2,4,256]{2,1,0:T(4,128)S(1)}, f32[2,4,256]{2,1,0:T(4,128)S(1)}, u32[]{:S(2)}, u32[]{:S(2)}) collective-permute-start(f32[2,4,256]{2,1,0:T(4,128)S(1)} %get-tuple-element.15), channel_id=1, source_target_pairs={{496,0},{0,16},{16,32},{32,48},{48,64},{64,80},{80,96},{96,112},{1... | collective-permute-start | bytes 24584 | tf_op jit(solution)/shard_map/ppermute | solution.py:23
  100.8 9.1 %collective-permute-start.5 = (f32[2,4,256]{2,1,0:T(4,128)S(1)}, f32[2,4,256]{2,1,0:T(4,128)S(1)}, u32[]{:S(2)}, u32[]{:S(2)}) collective-permute-start(f32[2,4,256]{2,1,0:T(4,128)S(1)} %get-tuple-element.16), channel_id=1, source_target_pairs={{16,0},{32,16},{48,32},{64,48},{80,64},{96,80},{112,96},{128,112},... | collective-permute-start | bytes 24584 | tf_op jit(solution)/shard_map/ppermute | solution.py:23
  117.0 0.6 copy-start.5
  120.2 20.6 %all-to-all-start.1 = ((f32[32,1,128]{2,1,0:T(1,128)}), f32[32,1,128]{2,1,0:T(1,128)S(1)}, u32[]{:S(2)}, u32[]{:S(2)}) async-start(f32[32,1,128]{2,1,0:T(1,128)} %broadcast_in_dim.5), calls=%async_computation.1 | async-start | bytes 32768 | tf_op jit(solution)/shard_map/all_to_all | solution.py:219
  140.8 0.6 copy-start.7

commit v2 on v0

v2 whole, which is shorter than its diff:
```python
import jax
import jax.numpy as jnp
from jax import lax
from jax.experimental import pallas as pl
from jax.experimental.pallas import tpu as pltpu
from jax.sharding import PartitionSpec as P

W = 4
ITERS = 3
EPSILON = 1e-6
SCALE = 2.0**-8
MIB = 1 << 20

VM = pl.BlockSpec(memory_space=pltpu.VMEM)
SM = pl.BlockSpec(memory_space=pltpu.SMEM)

FIELDS = 128
PART = 144
CHUNK = 272

BASE = [0, 5, 9, 12, 14]
BASE_T = [0, 15, 19, 22, 24]
N_TABLE = 26

INNER = [(w, s) for w in range(8) for s in range(-W, W + 1) if 0 <= w + s < 8]
OUTER = [(w, s) for w in range(8) for s in range(-W, W + 1) if not 0 <= w + s < 8]


def params(mib):
    return pltpu.CompilerParams(vmem_limit_bytes=mib * MIB)


def pair_swap(block, offset):
    n, m = lax.axis_size("space"), lax.axis_size("member")
    route = []
    for i in range(n):
        j = i + 1 if (i + offset) % 2 == 0 else i - 1
        for k in range(m):
            route.append((i * m + k, (j % n) * m + (k if 0 <= j < n else k ^ 1)))
    return lax.ppermute(block, ("space", "member"), route)


def pack_kernel(anomalies_ref, reach_ref, obs_ref, innovations_ref, chunk_ref):
    x = anomalies_ref[...].astype(jnp.float32)
    rows = []
    for t in range(8):
        tile = x[:, t, :]
        rows += [tile[:, :128], tile[:, 128:]]
    lane = lax.broadcasted_iota(jnp.int32, (1, 128), 1)
    lines = []
    for a in range(3):
        block = innovations_ref[a] if a < 2 else obs_ref[...]
        wide = jnp.concatenate([block, jnp.zeros((8, 112), jnp.float32)], axis=1)
        line = wide[0:1]
        for t in range(1, 8):
            line = line + pltpu.roll(wide[t : t + 1], 16 * t, 1)
        lines.append(line)
    values = jnp.concatenate(lines, axis=0)
    high = values.astype(jnp.bfloat16).astype(jnp.float32)
    rest = values - high
    middle = rest.astype(jnp.bfloat16).astype(jnp.float32)
    reach = jnp.zeros((1, 128), jnp.float32)
    for t in range(8):
        reach = reach + jnp.where(lane == t, reach_ref[t].astype(jnp.float32), 0.0)
    fields = jnp.concatenate(
        [high, middle, rest - middle, reach, jnp.zeros((6, 128), jnp.float32)], axis=0
    )
    chunk = jnp.concatenate(rows[:8] + [fields] + rows[8:], axis=0).astype(jnp.bfloat16)
    for k in range(16):
        chunk_ref[k] = chunk


def pack(anomalies, tile_reach, obs_var, innovations):
    return pl.pallas_call(
        pack_kernel,
        out_shape=jax.ShapeDtypeStruct((16, CHUNK, 128), jnp.bfloat16),
        in_specs=[VM, SM, VM, VM],
        out_specs=VM,
        compiler_params=params(8),
    )(anomalies, tile_reach, obs_var, innovations)


def swap_blocks(x):
    row = lax.broadcasted_iota(jnp.int32, (8, 128), 0)
    block = lax.broadcasted_iota(jnp.int32, (8, 128), 1) // 16
    for bit in (1, 2, 4):
        r, b = (row & bit) != 0, (block & bit) != 0
        up = pltpu.roll(pltpu.roll(x, 8 - bit, 0), 16 * bit, 1)
        down = pltpu.roll(pltpu.roll(x, bit, 0), 128 - 16 * bit, 1)
        x = jnp.where(r == b, x, jnp.where(b, up, down))
    return x


def unpack_fields(lines):
    lines = lines.astype(jnp.float32)
    out = []
    for a in range(3):
        value = lines[:, a] + (lines[:, 3 + a] + lines[:, 6 + a])
        out.append(jnp.concatenate([swap_blocks(value[:8]), swap_blocks(value[8:])], axis=1))
    return out


def row_products(a, b):
    return lax.dot_general(a, b, (((1,), (1,)), ((), ())), preferred_element_type=jnp.float32)


def tile_of(ref, row):
    return jnp.concatenate(
        [
            ref[:, pl.ds(row, 16), :].reshape(256, 128),
            ref[:, pl.ds(row + 16, 16), :].reshape(256, 128),
        ],
        axis=1,
    )


def table_entry(shift, reach_w, reach_o):
    d = abs(shift)
    if shift >= 0:
        last, base = jnp.minimum(reach_o, reach_w - d), BASE[d]
    else:
        last, base = jnp.minimum(reach_w, reach_o - d), BASE_T[d]
    return jnp.where(last >= 0, base + last, N_TABLE - 1)


def inner_kernel(reach_ref, loc_ref, own_ref, t_ref, h_ref, xs):
    for w in range(8):
        xs[w] = tile_of(own_ref, 32 * w + (16 if w >= 4 else 0))
    factor = SCALE / 255.0
    k = 0
    for d in range(W + 1):
        total = None
        for o in range(W + 1 - d):
            p = row_products(loc_ref[o + d], loc_ref[o])
            total = p if total is None else total + p
            t_ref[k] = total * factor
            k += 1
    for d in range(1, W + 1):
        total = None
        for o in range(W + 1 - d):
            p = row_products(loc_ref[o], loc_ref[o + d])
            total = p if total is None else total + p
            t_ref[k] = total * factor
            k += 1
    t_ref[k] = jnp.zeros(t_ref.shape[1:], jnp.float32)

    def tile(w, start):
        rows = xs[w].T
        for shift in range(-W, W + 1):
            other = w + shift

            @pl.when((other >= 0) & (other < 8))
            def _():
                entry = table_entry(shift, reach_ref[w], reach_ref[other])
                covariance = jnp.dot(rows, xs[other], preferred_element_type=jnp.float32)
                h_ref[w * 8 + other] = covariance * t_ref[entry]

        return start

    lax.fori_loop(0, 8, tile, 0)


def inner_blocks(reach, loc_blocks, own):
    return pl.pallas_call(
        inner_kernel,
        out_shape=(
            jax.ShapeDtypeStruct((N_TABLE, 256, 256), jnp.float32),
            jax.ShapeDtypeStruct((64, 256, 256), jnp.float32),
        ),
        in_specs=[SM, VM, VM],
        out_specs=(VM, VM),
        scratch_shapes=[pltpu.VMEM((8, 256, 256), jnp.bfloat16)],
        compiler_params=params(30),
        cost_estimate=pl.CostEstimate(
            flops=77 * 2 * 256**3, bytes_accessed=28 * MIB, transcendentals=0
        ),
    )(reach, loc_blocks, own)


def add_products(acc, block, v_rows):
    for f in range(2):
        p = block * v_rows[f]
        p = p[:, :128] + p[:, 128:]
        acc[f] = p if acc[f] is None else acc[f] + p


def row_sums(parts):
    return jnp.sum(jnp.concatenate(parts, axis=0).T, axis=0, keepdims=True)


ROWS = 64


def apply_blocks(inner_ref, outer_ref, v_ref, obs_ref, y):
    for w in range(8):
        done = [[], []]
        for c in range(0, 256, ROWS):
            acc = [None, None]
            for shift in range(-W, W + 1):
                other = w + shift
                if 0 <= other < 8:
                    block = inner_ref[w * 8 + other, c : c + ROWS, :]
                else:
                    block = outer_ref[OUTER.index((w, shift)), c : c + ROWS, :]
                rows = [v_ref[f, other + W : other + W + 1, :] for f in range(2)]
                add_products(acc, block, rows)
            for f in range(2):
                done[f].append(acc[f])
        for f in range(2):
            y[f, w : w + 1, :] = row_sums(done[f]) + (obs_ref[w : w + 1, :] * SCALE) * v_ref[
                f, w + W : w + W + 1, :
            ]


def set_sends(even, p, a_ref, b_ref):
    for f in range(2):
        low, high = p[f, :W], p[f, W:]
        a_ref[f] = jnp.where(even, high, low)
        b_ref[f] = jnp.where(even, low, high)


def first_kernel(
    reach_ref, own_ref, a_ref, b_ref, t_ref, inner_ref,
    outer_ref, p0_ref, obs_ref, p1_ref, send_a_ref, send_b_ref,
    xs, v, lines,
):
    even = lax.axis_index("space") % 2 == 0
    a_low, b_low = jnp.where(even, 0, 16), jnp.where(even, 16, 0)
    for w in range(8):
        xs[w + W] = tile_of(own_ref, 32 * w + (16 if w >= 4 else 0))
    for w in range(W):
        xs[jnp.where(even, 12, 0) + w] = tile_of(a_ref, pl.multiple_of(a_low + 32 * w, 16))
        xs[jnp.where(even, 0, 12) + w] = tile_of(b_ref, pl.multiple_of(b_low + 32 * w, 16))
    a_at = pl.multiple_of(jnp.where(even, 128, 0), 16)
    b_at = pl.multiple_of(jnp.where(even, 0, 128), 16)
    lines[0] = a_ref[:, pl.ds(a_at, 16), :]
    lines[1] = b_ref[:, pl.ds(b_at, 16), :]
    a_fields, b_fields = unpack_fields(lines[0]), unpack_fields(lines[1])
    own_fields = unpack_fields(own_ref[:, FIELDS : FIELDS + 16, :])
    for f in range(2):
        v[f, :W] = jnp.where(even, b_fields[f], a_fields[f])[W:]
        v[f, W : W + 8] = own_fields[f]
        v[f, W + 8 :] = jnp.where(even, a_fields[f], b_fields[f])[:W]
        p0_ref[f] = own_fields[f]
    obs_ref[...] = own_fields[2]

    lane = lax.broadcasted_iota(jnp.int32, (1, 128), 1)
    reach_a = lines[0, 0, 9:10, :].astype(jnp.float32)
    reach_b = lines[1, 0, 9:10, :].astype(jnp.float32)
    reach_left = jnp.where(even, reach_b, reach_a)
    reach_right = jnp.where(even, reach_a, reach_b)

    def reach_of(tile):
        if 0 <= tile < 8:
            return reach_ref[tile]
        line, at = (reach_left, tile + 8) if tile < 0 else (reach_right, tile - 8)
        return jnp.sum(jnp.where(lane == at, line, 0.0)).astype(jnp.int32)

    reach = {tile: reach_of(tile) for tile in range(-W, 8 + W)}
    for w in range(8):
        rows = xs[w + W].T
        for shift in range(-W, W + 1):
            if (w, shift) not in OUTER:
                continue
            entry = table_entry(shift, reach[w], reach[w + shift])
            covariance = jnp.dot(rows, xs[w + shift + W], preferred_element_type=jnp.float32)
            outer_ref[OUTER.index((w, shift))] = covariance * t_ref[entry]
    apply_blocks(inner_ref, outer_ref, v, obs_ref, p1_ref)
    set_sends(even, p1_ref, send_a_ref, send_b_ref)


FIELD = jax.ShapeDtypeStruct((2, 8, 256), jnp.float32)
HALO = jax.ShapeDtypeStruct((2, W, 256), jnp.float32)


def first_application(reach, own, a, b, table, inner):
    return pl.pallas_call(
        first_kernel,
        out_shape=(
            jax.ShapeDtypeStruct((len(OUTER), 256, 256), jnp.float32),
            FIELD,
            jax.ShapeDtypeStruct((8, 256), jnp.float32),
            FIELD,
            HALO,
            HALO,
        ),
        in_specs=[SM] + [VM] * 5,
        out_specs=(VM,) * 6,
        scratch_shapes=[
            pltpu.VMEM((16, 256, 256), jnp.bfloat16),
            pltpu.VMEM((2, 16, 256), jnp.float32),
            pltpu.VMEM((2, 16, 16, 128), jnp.bfloat16),
        ],
        compiler_params=params(36),
    )(reach, own, a, b, table, inner)


def fill_window(even, p_ref, a_ref, b_ref, v):
    for f in range(2):
        v[f, :W] = jnp.where(even, b_ref[f], a_ref[f])
        v[f, W : W + 8] = p_ref[f]
        v[f, W + 8 :] = jnp.where(even, a_ref[f], b_ref[f])


def next_kernel(
    p_ref, a_ref, b_ref, obs_ref, inner_ref, outer_ref, y_ref, send_a_ref, send_b_ref, v
):
    even = lax.axis_index("space") % 2 == 0
    fill_window(even, p_ref, a_ref, b_ref, v)
    apply_blocks(inner_ref, outer_ref, v, obs_ref, y_ref)
    set_sends(even, y_ref, send_a_ref, send_b_ref)


def next_application(p, a, b, obs, inner, outer):
    return pl.pallas_call(
        next_kernel,
        out_shape=(FIELD, HALO, HALO),
        in_specs=[VM] * 6,
        out_specs=(VM,) * 3,
        scratch_shapes=[pltpu.VMEM((2, 16, 256), jnp.float32)],
        compiler_params=params(30),
    )(p, a, b, obs, inner, outer)


def two_sum(a, b):
    s = a + b
    t = s - a
    return s, (a - (s - t)) + (b - t)


def halves(a):
    c = a * 4097.0
    high = c - (c - a)
    return high, a - high


def two_product(a, b):
    p = a * b
    ah, al = halves(a)
    bh, bl = halves(b)
    return p, ((ah * bh - p) + ah * bl + al * bh) + al * bl


def pair_add(x, y):
    s, e = two_sum(x[0], y[0])
    e = e + (x[1] + y[1])
    high = s + e
    return high, e - (high - s)


def pair_times(x, y):
    p, e = two_product(x[0], y[0])
    return p, e + (x[0] * y[1] + x[1] * y[0])


def last_kernel(
    p_ref, a_ref, b_ref, obs_ref, inner_ref, outer_ref, p0_ref, p1_ref, y_ref, m_ref, v
):
    even = lax.axis_index("space") % 2 == 0
    fill_window(even, p_ref, a_ref, b_ref, v)
    apply_blocks(inner_ref, outer_ref, v, obs_ref, y_ref)
    powers = [p0_ref, p1_ref, p_ref, y_ref]
    row = lax.broadcasted_iota(jnp.int32, (8, 128), 0)
    lane = lax.broadcasted_iota(jnp.int32, (8, 128), 1)
    sums = []
    for f in range(2):
        packed = [jnp.zeros((8, 128), jnp.float32)] * 2
        for k in range(2 * ITERS):
            p, e = two_product(powers[k // 2][f], powers[(k + 1) // 2][f])
            total = pair_add((p[:, :128], e[:, :128]), (p[:, 128:], e[:, 128:]))
            for shift in (4, 2, 1):
                total = pair_add(total, [pltpu.roll(x, shift, 0) for x in total])
            packed = [jnp.where(row == k, x, y) for x, y in zip(total, packed)]
        for shift in (64, 32, 16, 8, 4, 2, 1):
            packed = pair_add(packed, [pltpu.roll(x, shift, 1) for x in packed])
        sums.append(packed)
    high = jnp.where(lane < 32, sums[0][0], sums[1][0])
    low = jnp.where(lane < 96, sums[0][1], sums[1][1])
    out = jnp.where(lane < 64, high, low)
    for k in range(32):
        m_ref[k] = out


def last_application(p, a, b, obs, inner, outer, p0, p1):
    return pl.pallas_call(
        last_kernel,
        out_shape=(FIELD, jax.ShapeDtypeStruct((32, 8, 128), jnp.float32)),
        in_specs=[VM] * 8,
        out_specs=(VM,) * 2,
        scratch_shapes=[pltpu.VMEM((2, 16, 256), jnp.float32)],
        compiler_params=params(30),
    )(p, a, b, obs, inner, outer, p0, p1)


def square_dot(poly, moment):
    total = None
    for k in range(2 * len(poly) - 1):
        coefficient = None
        for i in range(len(poly)):
            j = k - i
            if i > j or j >= len(poly):
                continue
            term = two_product(poly[i], poly[j])
            if i != j:
                term = (2.0 * term[0], 2.0 * term[1])
            coefficient = term if coefficient is None else pair_add(coefficient, term)
        term = pair_times(coefficient, moment[k])
        total = term if total is None else pair_add(total, term)
    return total[0] + total[1]


def finish_kernel(m_ref, p0_ref, p1_ref, p2_ref, p3_ref, inc_ref, res_ref):
    member = lax.axis_index("member")
    s = m_ref[0]
    e = jnp.zeros((8, 128), jnp.float32)
    for k in range(1, 32):
        s, t = two_sum(s, m_ref[k])
        e = e + t
    low = e + pltpu.roll(s, 64, 1)
    moment = [(s[k : k + 1], low[k : k + 1]) for k in range(2 * ITERS)]
    one = jnp.ones((1, 128), jnp.float32)
    residual, direction, increment = [one], [one], []
    norm_now = moment[0][0] + moment[0][1]
    for iteration in range(ITERS):
        step = norm_now / square_dot(direction, moment[1:])
        moved = [step * c for c in direction]
        increment = [x + y for x, y in zip(increment, moved)] + moved[len(increment) :]
        residual = residual[:1] + [
            (residual[i + 1] if i + 1 < len(residual) else 0.0) - c for i, c in enumerate(moved)
        ]
        if iteration + 1 < ITERS:
            norm_next = square_dot(residual, moment)
            ratio = norm_next / (norm_now + EPSILON)
            grown = [ratio * c for c in direction]
            direction = [x + y for x, y in zip(residual, grown)] + residual[len(grown) :]
            norm_now = norm_next
    shift = (128 - (member % 8) * 16) % 128
    upper = member >= 8
    powers = [p0_ref, p1_ref, p2_ref, p3_ref]
    for f in range(2):
        at = 32 * f
        mine = [
            pltpu.roll(jnp.where(upper, p[f, :, 128:], p[f, :, :128]), shift, 1) for p in powers
        ]
        inc = sum(c[:, at : at + 1] * x for c, x in zip(increment, mine)) * SCALE
        res = sum(c[:, at : at + 1] * x for c, x in zip(residual, mine))
        inc_ref[f] = inc[:, :16]
        res_ref[f] = res[:, :16]


def finish(m, p):
    shape = jax.ShapeDtypeStruct((2, 8, 16), jnp.float32)
    return pl.pallas_call(
        finish_kernel,
        out_shape=(shape, shape),
        in_specs=[VM] * 5,
        out_specs=(VM, VM),
        compiler_params=params(8),
    )(m, *p)


def on_device(anomalies, loc_blocks, tile_reach, obs_var, innovations):
    chunk = pack(anomalies, tile_reach, obs_var, innovations)
    own = lax.all_to_all(chunk, "member", 0, 0)
    odd = lax.axis_index("space") % 2
    to_a = lax.dynamic_slice_in_dim(own, 128 * (1 - odd), PART, 1)
    to_b = lax.dynamic_slice_in_dim(own, 128 * odd, PART, 1)
    a, b = pair_swap(to_a, 0), pair_swap(to_b, 1)
    table, inner = inner_blocks(tile_reach, loc_blocks, own)
    outer, p0, obs, p1, to_a, to_b = first_application(tile_reach, own, a, b, table, inner)
    a, b = pair_swap(to_a, 0), pair_swap(to_b, 1)
    p2, to_a, to_b = next_application(p1, a, b, obs, inner, outer)
    a, b = pair_swap(to_a, 0), pair_swap(to_b, 1)
    p3, m = last_application(p2, a, b, obs, inner, outer, p0, p1)
    m = lax.all_to_all(m, "space", 0, 0)
    return finish(m, [p0, p1, p2, p3])


def solution(mesh):
    in_specs = (
        P("member", "space", None),
        P(),
        P("space"),
        P("space", "member"),
        P(None, "space", "member"),
    )
    out_specs = (P(None, "space", "member"), P(None, "space", "member"))
    return jax.shard_map(
        on_device, mesh=mesh, in_specs=in_specs, out_specs=out_specs, check_vma=False
    )
```

time: 966 us -> 145 us (0.15)
  the two profiles are of different devices: /device:TPU:1 before, /device:TPU:129 now
where the time goes in v2:
time: 145 us; the launch traced here: 144 us
  Pallas kernels  38.1 us (26%)
  starting transfers between devices  37.3 us (26%)
  waiting for transfers between devices  32.5 us (22%)
  blocking collectives  26.7 us (18%)
  local copies, waits for them, and re-layouts  8.72 us (6%)
    all_to_all x1, blocking collectives, on_device(): m = lax.all_to_all(m, 'space', 0, 0)  26.7 us
    all_to_all x1, waiting for transfers between devices, on_device(): own = lax.all_to_all(chunk, 'member', 0, 0)  26.6 us
    ppermute x6, starting transfers between devices, pair_swap(): return lax.ppermute(block, ('space', 'member'), route)  23.5 us
    pallas_call x1, Pallas kernels, inner_blocks(): pl.pallas_call(inner_kernel, out_shape=(jax.ShapeDtypeStruct((N_TABLE, 25...  17.8 us
    all_to_all x1, starting transfers between devices, on_device(): own = lax.all_to_all(chunk, 'member', 0, 0)  13.8 us
    pallas_call x1, Pallas kernels, first_application(): pl.pallas_call(first_kernel, out_shape=(jax.ShapeDtypeStruct((len(OUTER),...  10.8 us
    unnamed x14, local copies, waits for them, and re-layouts  8.65 us
    ppermute x6, waiting for transfers between devices, pair_swap(): return lax.ppermute(block, ('space', 'member'), route)  5.89 us
  transfers between devices with their start and end apart: 7, of which 3 were waited for; matrix products, arithmetic and copies ran while one was open for 0% of the time, Pallas kernels for 12%

profile of v2, /device:TPU:129, one launch (start us, length us, event | category | flops | bytes accessed | tf_op | source)
XLA Modules:
  0.0 144.0 jit_solution(1192454779646309410)
XLA Ops:
  0.6 0.8 copy-done.1
  1.5 0.7 copy-done.2
  2.2 0.7 copy-done.3
  2.9 0.7 copy-done.4
  3.5 1.7 %shard_map.68 = bf16[16,272,128]{2,1,0:T(8,128)(2,1)} custom-call(bf16[16,8,256]{2,1,0:T(8,128)(2,1)S(1)} %copy-done.1, s32[8]{0:T(128)S(1)} %copy-done.4, f32[8,16]{1,0:T(8,128)S(1)} %copy-done.3, f32[2,8,16]{2,1,0:T(8,128)S(1)} %copy-done.2), custom_call_target="tpu_custom_call" | custom-call | tf_op jit(solution)/shard_map/pallas_call | solution.py:74
  5.2 13.8 %all-to-all-start = ((bf16[16,272,128]{2,1,0:T(8,128)(2,1)}), bf16[16,272,128]{2,1,0:T(8,128)(2,1)S(1)}, u32[]{:S(2)}, u32[]{:S(2)}) async-start(bf16[16,272,128]{2,1,0:T(8,128)(2,1)} %shard_map.68), calls=%async_computation | async-start | bytes 2228224 | tf_op jit(solution)/shard_map/all_to_all | solution.py:464
  19.0 26.6 %all-to-all-done.own_ref = bf16[16,272,128]{2,1,0:T(8,128)(2,1)S(1)} async-done(((bf16[16,272,128]{2,1,0:T(8,128)(2,1)}), bf16[16,272,128]{2,1,0:T(8,128)(2,1)S(1)}, u32[]{:S(2)}, u32[]{:S(2)}) %all-to-all-start) | async-done | bytes 1114144 | tf_op jit(solution)/shard_map/all_to_all | solution.py:464
  45.6 0.1 constant_dynamic-slice_fusion
  45.7 5.8 %collective-permute-start.1 = (bf16[16,144,128]{2,1,0:T(8,128)(2,1)S(1)}, bf16[16,144,128]{2,1,0:T(8,128)(2,1)S(1)}, u32[]{:S(2)}, u32[]{:S(2)}) collective-permute-start(bf16[16,144,128]{2,1,0:T(8,128)(2,1)S(1)} %get-tuple-element.28), channel_id=1, source_target_pairs={{0,497},{1,496},{2,499},{3,498},{4,501},{5,500},{6,503},{7,502},{8... | collective-permute-start | bytes 1769480 | tf_op jit(solution)/shard_map/ppermute | solution.py:40
  51.4 6.1 %collective-permute-start = (bf16[16,144,128]{2,1,0:T(8,128)(2,1)S(1)}, bf16[16,144,128]{2,1,0:T(8,128)(2,1)S(1)}, u32[]{:S(2)}, u32[]{:S(2)}) collective-permute-start(bf16[16,144,128]{2,1,0:T(8,128)(2,1)S(1)} %get-tuple-element.29), channel_id=1, source_target_pairs={{0,16},{1,17},{2,18},{3,19},{4,20},{5,21},{6,22},{7,23},{8,24},{9,... | collective-permute-start | bytes 1769480 | tf_op jit(solution)/shard_map/ppermute | solution.py:40
  57.6 17.8 %shard_map.69 = (f32[26,256,256]{2,1,0:T(8,128)S(1)}, f32[64,256,256]{2,1,0:T(8,128)}) custom-call(s32[8]{0:T(128)S(1)} %copy-done.5, bf16[5,256,256]{2,1,0:T(8,128)(2,1)S(1)} %copy-done.6, bf16[16,272,128]{2,1,0:T(8,128)(2,1)S(1)} %all-to-all-done.own_ref), custom_call_target="tpu_custom_call" | custom-call | flops 2583691264 | bytes 29360128 | tf_op jit(solution)/shard_map/pallas_call | solution.py:164
  75.4 10.8 %shard_map.70 = (f32[20,256,256]{2,1,0:T(8,128)S(1)}, f32[2,8,256]{2,1,0:T(8,128)S(1)}, f32[8,256]{1,0:T(8,128)S(1)}, f32[2,8,256]{2,1,0:T(8,128)S(1)}, f32[2,4,...) custom-call(s32[8]{0:T(128)S(1)} %copy-done.5, bf16[16,272,128]{2,1,0:T(8,128)(2,1)S(1)} %all-to-all-done.own_ref, ...), custom_call_target="tpu_custom_call" | custom-call | tf_op jit(solution)/shard_map/pallas_call | solution.py:277
  86.2 1.9 %collective-permute-start.2 = (f32[2,4,256]{2,1,0:T(4,128)S(1)}, f32[2,4,256]{2,1,0:T(4,128)S(1)}, u32[]{:S(2)}, u32[]{:S(2)}) collective-permute-start(f32[2,4,256]{2,1,0:T(4,128)S(1)} %get-tuple-element.18), channel_id=1, source_target_pairs={{0,16},{1,17},{2,18},{3,19},{4,20},{5,21},{6,22},{7,23},{8,24},{9,... | collective-permute-start | bytes 24584 | tf_op jit(solution)/shard_map/ppermute | solution.py:40
  88.1 1.9 %collective-permute-start.3 = (f32[2,4,256]{2,1,0:T(4,128)S(1)}, f32[2,4,256]{2,1,0:T(4,128)S(1)}, u32[]{:S(2)}, u32[]{:S(2)}) collective-permute-start(f32[2,4,256]{2,1,0:T(4,128)S(1)} %get-tuple-element.19), channel_id=1, source_target_pairs={{0,497},{1,496},{2,499},{3,498},{4,501},{5,500},{6,503},{7,502},{8... | collective-permute-start | bytes 24584 | tf_op jit(solution)/shard_map/ppermute | solution.py:40
  90.1 3.0 %collective-permute-done.3.b_ref = f32[2,4,256]{2,1,0:T(4,128)S(1)} collective-permute-done((f32[2,4,256]{2,1,0:T(4,128)S(1)}, f32[2,4,256]{2,1,0:T(4,128)S(1)}, u32[]{:S(2)}, u32[]{:S(2)}) %collective-permute-start.3) | collective-permute-done | bytes 8224 | tf_op jit(solution)/shard_map/ppermute | solution.py:40
  93.1 5.8 %copy-done = f32[64,256,256]{2,1,0:T(8,128)S(1)} copy-done((f32[64,256,256]{2,1,0:T(8,128)S(1)}, f32[64,256,256]{2,1,0:T(8,128)}, u32[]{:S(2)}) %copy-start) | copy-done | bytes 16777240
  98.9 3.1 %shard_map.71 = (f32[2,8,256]{2,1,0:T(8,128)S(1)}, f32[2,4,256]{2,1,0:T(4,128)S(1)}, f32[2,4,256]{2,1,0:T(4,128)S(1)}) custom-call(f32[2,8,256]{2,1,0:T(8,128)S(1)} %get-tuple-element.17.p_ref.p1_ref, f32[2,4,256]{2,1,0:T(4,128)S(1)} %collective-permute-done.2.a_ref, f32[2,4,256]{2,1,0:T(4,128)S(1)} %collective-permute-done.3.b_ref, ...), custom_call_target="tpu_custom_call" | custom-call | tf_op jit(solution)/shard_map/pallas_call | solution.py:315
  101.9 5.7 %collective-permute-start.4 = (f32[2,4,256]{2,1,0:T(4,128)S(1)}, f32[2,4,256]{2,1,0:T(4,128)S(1)}, u32[]{:S(2)}, u32[]{:S(2)}) collective-permute-start(f32[2,4,256]{2,1,0:T(4,128)S(1)} %get-tuple-element.23), channel_id=1, source_target_pairs={{0,16},{1,17},{2,18},{3,19},{4,20},{5,21},{6,22},{7,23},{8,24},{9,... | collective-permute-start | bytes 24584 | tf_op jit(solution)/shard_map/ppermute | solution.py:40
  107.7 2.1 %collective-permute-start.5 = (f32[2,4,256]{2,1,0:T(4,128)S(1)}, f32[2,4,256]{2,1,0:T(4,128)S(1)}, u32[]{:S(2)}, u32[]{:S(2)}) collective-permute-start(f32[2,4,256]{2,1,0:T(4,128)S(1)} %get-tuple-element.24), channel_id=1, source_target_pairs={{0,497},{1,496},{2,499},{3,498},{4,501},{5,500},{6,503},{7,502},{8... | collective-permute-start | bytes 24584 | tf_op jit(solution)/shard_map/ppermute | solution.py:40
  109.8 0.0 collective-permute-done.4.a_ref
  109.8 2.9 %collective-permute-done.5.b_ref = f32[2,4,256]{2,1,0:T(4,128)S(1)} collective-permute-done((f32[2,4,256]{2,1,0:T(4,128)S(1)}, f32[2,4,256]{2,1,0:T(4,128)S(1)}, u32[]{:S(2)}, u32[]{:S(2)}) %collective-permute-start.5) | collective-permute-done | bytes 8224 | tf_op jit(solution)/shard_map/ppermute | solution.py:40
  112.6 3.7 %shard_map.72 = (f32[2,8,256]{2,1,0:T(8,128)S(1)}, f32[32,8,128]{2,1,0:T(8,128)S(1)}) custom-call(f32[2,8,256]{2,1,0:T(8,128)S(1)} %get-tuple-element.22.p_ref.p2_ref, f32[2,4,256]{2,1,0:T(4,128)S(1)} %collective-permute-done.4.a_ref, f32[2,4,256]{2,1,0:T(4,128)S(1)} %collective-permute-done.5.b_ref, f32[8,256]{1,0:T(8,128)S(1)} %get-tuple-element.20.obs_ref, ...), custom_call_target="tpu_custom_call" | custom-call | tf_op jit(solution)/shard_map/pallas_call | solution.py:385
  116.3 26.7 %all_to_all.10.m_ref = f32[32,8,128]{2,1,0:T(8,128)S(1)} all-to-all(f32[32,8,128]{2,1,0:T(8,128)S(1)} %get-tuple-element.26), channel_id=1, replica_groups=mesh['space'=32,'member'=16] {'space'}, dimensions={0} | all-to-all | bytes 262144 | tf_op jit(solution)/shard_map/all_to_all | solution.py:475
  143.0 1.0 shard_map.73
  (12 shorter events, 0.0 us)
Async XLA Ops:
  0.6 0.8 copy-start.1
  1.5 0.7 copy-start.2
  2.2 0.7 copy-start.3
  2.9 0.7 copy-start.4
  3.5 54.0 %copy-start.5 = (s32[8]{0:T(128)S(1)}, s32[8]{0:T(128)}, u32[]{:S(2)}) copy-start(s32[8]{0:T(128)} %reach_ref.5) | copy-start | bytes 100
  3.5 54.0 %copy-start.6 = (bf16[5,256,256]{2,1,0:T(8,128)(2,1)S(1)}, bf16[5,256,256]{2,1,0:T(8,128)(2,1)}, u32[]{:S(2)}) copy-start(bf16[5,256,256]{2,1,0:T(8,128)(2,1)} %loc_ref.1) | copy-start | bytes 1966084
  5.2 40.3 %all-to-all-start = ((bf16[16,272,128]{2,1,0:T(8,128)(2,1)}), bf16[16,272,128]{2,1,0:T(8,128)(2,1)S(1)}, u32[]{:S(2)}, u32[]{:S(2)}) async-start(bf16[16,272,128]{2,1,0:T(8,128)(2,1)} %shard_map.68), calls=%async_computation | async-start | bytes 2228224 | tf_op jit(solution)/shard_map/all_to_all | solution.py:464
  45.7 29.7 %collective-permute-start.1 = (bf16[16,144,128]{2,1,0:T(8,128)(2,1)S(1)}, bf16[16,144,128]{2,1,0:T(8,128)(2,1)S(1)}, u32[]{:S(2)}, u32[]{:S(2)}) collective-permute-start(bf16[16,144,128]{2,1,0:T(8,128)(2,1)S(1)} %get-tuple-element.28), channel_id=1, source_target_pairs={{0,497},{1,496},{2,499},{3,498},{4,501},{5,500},{6,503},{7,502},{8... | collective-permute-start | bytes 1769480 | tf_op jit(solution)/shard_map/ppermute | solution.py:40
  51.4 24.0 %collective-permute-start = (bf16[16,144,128]{2,1,0:T(8,128)(2,1)S(1)}, bf16[16,144,128]{2,1,0:T(8,128)(2,1)S(1)}, u32[]{:S(2)}, u32[]{:S(2)}) collective-permute-start(bf16[16,144,128]{2,1,0:T(8,128)(2,1)S(1)} %get-tuple-element.29), channel_id=1, source_target_pairs={{0,16},{1,17},{2,18},{3,19},{4,20},{5,21},{6,22},{7,23},{8,24},{9,... | collective-permute-start | bytes 1769480 | tf_op jit(solution)/shard_map/ppermute | solution.py:40
  86.2 3.9 %collective-permute-start.2 = (f32[2,4,256]{2,1,0:T(4,128)S(1)}, f32[2,4,256]{2,1,0:T(4,128)S(1)}, u32[]{:S(2)}, u32[]{:S(2)}) collective-permute-start(f32[2,4,256]{2,1,0:T(4,128)S(1)} %get-tuple-element.18), channel_id=1, source_target_pairs={{0,16},{1,17},{2,18},{3,19},{4,20},{5,21},{6,22},{7,23},{8,24},{9,... | collective-permute-start | bytes 24584 | tf_op jit(solution)/shard_map/ppermute | solution.py:40
  88.1 5.0 %collective-permute-start.3 = (f32[2,4,256]{2,1,0:T(4,128)S(1)}, f32[2,4,256]{2,1,0:T(4,128)S(1)}, u32[]{:S(2)}, u32[]{:S(2)}) collective-permute-start(f32[2,4,256]{2,1,0:T(4,128)S(1)} %get-tuple-element.19), channel_id=1, source_target_pairs={{0,497},{1,496},{2,499},{3,498},{4,501},{5,500},{6,503},{7,502},{8... | collective-permute-start | bytes 24584 | tf_op jit(solution)/shard_map/ppermute | solution.py:40
  93.1 5.8 %copy-start = (f32[64,256,256]{2,1,0:T(8,128)S(1)}, f32[64,256,256]{2,1,0:T(8,128)}, u32[]{:S(2)}) copy-start(f32[64,256,256]{2,1,0:T(8,128)} %get-tuple-element.16.inner_ref) | copy-start | bytes 50331652
  101.9 7.8 %collective-permute-start.4 = (f32[2,4,256]{2,1,0:T(4,128)S(1)}, f32[2,4,256]{2,1,0:T(4,128)S(1)}, u32[]{:S(2)}, u32[]{:S(2)}) collective-permute-start(f32[2,4,256]{2,1,0:T(4,128)S(1)} %get-tuple-element.23), channel_id=1, source_target_pairs={{0,16},{1,17},{2,18},{3,19},{4,20},{5,21},{6,22},{7,23},{8,24},{9,... | collective-permute-start | bytes 24584 | tf_op jit(solution)/shard_map/ppermute | solution.py:40
  107.7 5.0 %collective-permute-start.5 = (f32[2,4,256]{2,1,0:T(4,128)S(1)}, f32[2,4,256]{2,1,0:T(4,128)S(1)}, u32[]{:S(2)}, u32[]{:S(2)}) collective-permute-start(f32[2,4,256]{2,1,0:T(4,128)S(1)} %get-tuple-element.24), channel_id=1, source_target_pairs={{0,497},{1,496},{2,499},{3,498},{4,501},{5,500},{6,503},{7,502},{8... | collective-permute-start | bytes 24584 | tf_op jit(solution)/shard_map/ppermute | solution.py:40

commit v3 on v2

--- a/solution.py
+++ b/solution.py
@@ -123,9 +123,7 @@
     return jnp.where(last >= 0, base + last, N_TABLE - 1)
 
 
-def inner_kernel(reach_ref, loc_ref, own_ref, t_ref, h_ref, xs):
-    for w in range(8):
-        xs[w] = tile_of(own_ref, 32 * w + (16 if w >= 4 else 0))
+def table_kernel(loc_ref, t_ref):
     factor = SCALE / 255.0
     k = 0
     for d in range(W + 1):
@@ -144,37 +142,45 @@
             k += 1
     t_ref[k] = jnp.zeros(t_ref.shape[1:], jnp.float32)
 
-    def tile(w, start):
+
+def make_tables(loc_blocks):
+    return pl.pallas_call(
+        table_kernel,
+        out_shape=jax.ShapeDtypeStruct((N_TABLE, 256, 256), jnp.float32),
+        in_specs=[VM],
+        out_specs=VM,
+        compiler_params=params(14),
+        cost_estimate=pl.CostEstimate(
+            flops=25 * 2 * 256**3, bytes_accessed=7 * MIB, transcendentals=0
+        ),
+    )(loc_blocks)
+
+
+def inner_kernel(reach_ref, own_ref, t_ref, h_ref, xs):
+    for w in range(8):
+        xs[w] = tile_of(own_ref, 32 * w + (16 if w >= 4 else 0))
+    for w in range(8):
         rows = xs[w].T
         for shift in range(-W, W + 1):
-            other = w + shift
-
-            @pl.when((other >= 0) & (other < 8))
-            def _():
-                entry = table_entry(shift, reach_ref[w], reach_ref[other])
-                covariance = jnp.dot(rows, xs[other], preferred_element_type=jnp.float32)
-                h_ref[w * 8 + other] = covariance * t_ref[entry]
-
-        return start
-
-    lax.fori_loop(0, 8, tile, 0)
-
-
-def inner_blocks(reach, loc_blocks, own):
+            if (w, shift) not in INNER:
+                continue
+            entry = table_entry(shift, reach_ref[w], reach_ref[w + shift])
+            covariance = jnp.dot(rows, xs[w + shift], preferred_element_type=jnp.float32)
+            h_ref[INNER.index((w, shift))] = covariance * t_ref[entry]
+
+
+def inner_blocks(reach, own, table):
     return pl.pallas_call(
         inner_kernel,
-        out_shape=(
-            jax.ShapeDtypeStruct((N_TABLE, 256, 256), jnp.float32),
-            jax.ShapeDtypeStruct((64, 256, 256), jnp.float32),
+        out_shape=jax.ShapeDtypeStruct((len(INNER), 256, 256), jnp.float32),
+        in_specs=[SM, VM, VM],
+        out_specs=VM,
+        scratch_shapes=[pltpu.VMEM((8, 256, 256), jnp.bfloat16)],
+        compiler_params=params(26),
+        cost_estimate=pl.CostEstimate(
+            flops=52 * 2 * 256**3, bytes_accessed=20 * MIB, transcendentals=0
         ),
-        in_specs=[SM, VM, VM],
-        out_specs=(VM, VM),
-        scratch_shapes=[pltpu.VMEM((8, 256, 256), jnp.bfloat16)],
-        compiler_params=params(30),
-        cost_estimate=pl.CostEstimate(
-            flops=77 * 2 * 256**3, bytes_accessed=28 * MIB, transcendentals=0
-        ),
-    )(reach, loc_blocks, own)
+    )(reach, own, table)
 
 
 def add_products(acc, block, v_rows):
@@ -199,7 +205,7 @@
             for shift in range(-W, W + 1):
                 other = w + shift
                 if 0 <= other < 8:
-                    block = inner_ref[w * 8 + other, c : c + ROWS, :]
+                    block = inner_ref[INNER.index((w, shift)), c : c + ROWS, :]
                 else:
                     block = outer_ref[OUTER.index((w, shift)), c : c + ROWS, :]
                 rows = [v_ref[f, other + W : other + W + 1, :] for f in range(2)]
@@ -219,10 +225,10 @@
         b_ref[f] = jnp.where(even, low, high)
 
 
-def first_kernel(
-    reach_ref, own_ref, a_ref, b_ref, t_ref, inner_ref,
-    outer_ref, p0_ref, obs_ref, p1_ref, send_a_ref, send_b_ref,
-    xs, v, lines,
+def outer_kernel(
+    reach_ref, own_ref, a_ref, b_ref, t_ref,
+    outer_ref, p0_ref, obs_ref, field_a_ref, field_b_ref,
+    xs, lines,
 ):
     even = lax.axis_index("space") % 2 == 0
     a_low, b_low = jnp.where(even, 0, 16), jnp.where(even, 16, 0)
@@ -235,14 +241,6 @@
     b_at = pl.multiple_of(jnp.where(even, 0, 128), 16)
     lines[0] = a_ref[:, pl.ds(a_at, 16), :]
     lines[1] = b_ref[:, pl.ds(b_at, 16), :]
-    a_fields, b_fields = unpack_fields(lines[0]), unpack_fields(lines[1])
-    own_fields = unpack_fields(own_ref[:, FIELDS : FIELDS + 16, :])
-    for f in range(2):
-        v[f, :W] = jnp.where(even, b_fields[f], a_fields[f])[W:]
-        v[f, W : W + 8] = own_fields[f]
-        v[f, W + 8 :] = jnp.where(even, a_fields[f], b_fields[f])[:W]
-        p0_ref[f] = own_fields[f]
-    obs_ref[...] = own_fields[2]
 
     lane = lax.broadcasted_iota(jnp.int32, (1, 128), 1)
     reach_a = lines[0, 0, 9:10, :].astype(jnp.float32)
@@ -257,6 +255,13 @@
         return jnp.sum(jnp.where(lane == at, line, 0.0)).astype(jnp.int32)
 
     reach = {tile: reach_of(tile) for tile in range(-W, 8 + W)}
+    a_fields, b_fields = unpack_fields(lines[0]), unpack_fields(lines[1])
+    own_fields = unpack_fields(own_ref[:, FIELDS : FIELDS + 16, :])
+    for f in range(2):
+        field_a_ref[f] = jnp.where(even, a_fields[f][:W], a_fields[f][W:])
+        field_b_ref[f] = jnp.where(even, b_fields[f][W:], b_fields[f][:W])
+        p0_ref[f] = own_fields[f]
+    obs_ref[...] = own_fields[2]
     for w in range(8):
         rows = xs[w + W].T
         for shift in range(-W, W + 1):
@@ -265,34 +270,30 @@
             entry = table_entry(shift, reach[w], reach[w + shift])
             covariance = jnp.dot(rows, xs[w + shift + W], preferred_element_type=jnp.float32)
             outer_ref[OUTER.index((w, shift))] = covariance * t_ref[entry]
-    apply_blocks(inner_ref, outer_ref, v, obs_ref, p1_ref)
-    set_sends(even, p1_ref, send_a_ref, send_b_ref)
 
 
 FIELD = jax.ShapeDtypeStruct((2, 8, 256), jnp.float32)
 HALO = jax.ShapeDtypeStruct((2, W, 256), jnp.float32)
 
 
-def first_application(reach, own, a, b, table, inner):
-    return pl.pallas_call(
-        first_kernel,
+def outer_blocks(reach, own, a, b, table):
+    return pl.pallas_call(
+        outer_kernel,
         out_shape=(
             jax.ShapeDtypeStruct((len(OUTER), 256, 256), jnp.float32),
             FIELD,
             jax.ShapeDtypeStruct((8, 256), jnp.float32),
-            FIELD,
             HALO,
             HALO,
         ),
-        in_specs=[SM] + [VM] * 5,
-        out_specs=(VM,) * 6,
+        in_specs=[SM] + [VM] * 4,
+        out_specs=(VM,) * 5,
         scratch_shapes=[
             pltpu.VMEM((16, 256, 256), jnp.bfloat16),
-            pltpu.VMEM((2, 16, 256), jnp.float32),
             pltpu.VMEM((2, 16, 16, 128), jnp.bfloat16),
         ],
-        compiler_params=params(36),
-    )(reach, own, a, b, table, inner)
+        compiler_params=params(22),
+    )(reach, own, a, b, table)
 
 
 def fill_window(even, p_ref, a_ref, b_ref, v):
@@ -318,7 +319,7 @@
         in_specs=[VM] * 6,
         out_specs=(VM,) * 3,
         scratch_shapes=[pltpu.VMEM((2, 16, 256), jnp.float32)],
-        compiler_params=params(30),
+        compiler_params=params(24),
     )(p, a, b, obs, inner, outer)
 
 
@@ -388,7 +389,7 @@
         in_specs=[VM] * 8,
         out_specs=(VM,) * 2,
         scratch_shapes=[pltpu.VMEM((2, 16, 256), jnp.float32)],
-        compiler_params=params(30),
+        compiler_params=params(24),
     )(p, a, b, obs, inner, outer, p0, p1)
 
 
@@ -460,14 +461,16 @@
 
 
 def on_device(anomalies, loc_blocks, tile_reach, obs_var, innovations):
+    table = make_tables(loc_blocks)
     chunk = pack(anomalies, tile_reach, obs_var, innovations)
     own = lax.all_to_all(chunk, "member", 0, 0)
     odd = lax.axis_index("space") % 2
     to_a = lax.dynamic_slice_in_dim(own, 128 * (1 - odd), PART, 1)
     to_b = lax.dynamic_slice_in_dim(own, 128 * odd, PART, 1)
     a, b = pair_swap(to_a, 0), pair_swap(to_b, 1)
-    table, inner = inner_blocks(tile_reach, loc_blocks, own)
-    outer, p0, obs, p1, to_a, to_b = first_application(tile_reach, own, a, b, table, inner)
+    inner = inner_blocks(tile_reach, own, table)
+    outer, p0, obs, a, b = outer_blocks(tile_reach, own, a, b, table)
+    p1, to_a, to_b = next_application(p0, a, b, obs, inner, outer)
     a, b = pair_swap(to_a, 0), pair_swap(to_b, 1)
     p2, to_a, to_b = next_application(p1, a, b, obs, inner, outer)
     a, b = pair_swap(to_a, 0), pair_swap(to_b, 1)

time: 145 us -> 123 us (0.85)
  Pallas kernels: 38.1 us -> 19.1 us
  local copies, waits for them, and re-layouts: 8.72 us -> 2.95 us
  blocking collectives: 26.7 us -> 28.9 us
  starting transfers between devices: 37.3 us -> 38.8 us
    pallas_call x2 -> x3, Pallas kernels: 28.6 us -> 5.65 us  [the longest x1 2.52 us: inner_blocks(): pl.pallas_call(inner_kernel, out_shape=jax.ShapeDtypeStruct((len(INNER),...]
    unnamed x14 -> x12, local copies, waits for them, and re-layouts: 8.65 us -> 2.88 us
    pallas_call x1 -> x2, Pallas kernels: 3.08 us -> 6.77 us  [next_application(): pl.pallas_call(next_kernel, out_shape=(FIELD, HALO, HALO), in_specs=[VM]...]
    all_to_all x1, blocking collectives: 26.7 us -> 28.9 us  [on_device(): m = lax.all_to_all(m, 'space', 0, 0)]
    ppermute x6, starting transfers between devices: 23.5 us -> 25 us  [pair_swap(): return lax.ppermute(block, ('space', 'member'), route)]
  transfers between devices with their start and end apart: 7 -> 7, of which waited for: 3 -> 3; matrix products, arithmetic and copies ran while one was open for 0% -> 0% of each run, Pallas kernels for 12% -> 3%
where the time goes in v3:
time: 123 us
  starting transfers between devices  38.8 us (32%)
  waiting for transfers between devices  32.4 us (26%)
  blocking collectives  28.9 us (23%)
  Pallas kernels  19.1 us (16%)
  local copies, waits for them, and re-layouts  2.95 us (2%)
    all_to_all x1, blocking collectives, on_device(): m = lax.all_to_all(m, 'space', 0, 0)  28.9 us
    all_to_all x1, waiting for transfers between devices, on_device(): own = lax.all_to_all(chunk, 'member', 0, 0)  26.5 us
    ppermute x6, starting transfers between devices, pair_swap(): return lax.ppermute(block, ('space', 'member'), route)  25 us
    all_to_all x1, starting transfers between devices, on_device(): own = lax.all_to_all(chunk, 'member', 0, 0)  13.8 us
    pallas_call x2, Pallas kernels, next_application(): pl.pallas_call(next_kernel, out_shape=(FIELD, HALO, HALO), in_specs=[VM]...  6.77 us
    ppermute x6, waiting for transfers between devices, pair_swap(): return lax.ppermute(block, ('space', 'member'), route)  5.89 us
    pallas_call x1, Pallas kernels, last_application(): pl.pallas_call(last_kernel, out_shape=(FIELD, jax.ShapeDtypeStruct((32, 8...  3.95 us
    unnamed x12, local copies, waits for them, and re-layouts  2.88 us
  transfers between devices with their start and end apart: 7, of which 3 were waited for; matrix products, arithmetic and copies ran while one was open for 0% of the time, Pallas kernels for 3%

profile of v3, /device:TPU:129, one launch (start us, length us, event | category | flops | bytes accessed | tf_op | source)
XLA Modules:
  0.0 123.0 jit_solution(11406189728330958153)
XLA Ops:
  0.6 0.8 copy-done.1
  1.5 0.7 copy-done.2
  2.2 0.7 copy-done.3
  2.8 0.7 copy-done.5
  3.5 1.7 %shard_map.68 = bf16[16,272,128]{2,1,0:T(8,128)(2,1)} custom-call(bf16[16,8,256]{2,1,0:T(8,128)(2,1)S(1)} %copy-done.1, s32[8]{0:T(128)S(1)} %copy-done.3, f32[8,16]{1,0:T(8,128)S(1)} %copy-done.5, f32[2,8,16]{2,1,0:T(8,128)S(1)} %copy-done.2), custom_call_target="tpu_custom_call" | custom-call | tf_op jit(solution)/shard_map/pallas_call | solution.py:74
  5.2 13.8 %all-to-all-start = ((bf16[16,272,128]{2,1,0:T(8,128)(2,1)}), bf16[16,272,128]{2,1,0:T(8,128)(2,1)S(1)}, u32[]{:S(2)}, u32[]{:S(2)}) async-start(bf16[16,272,128]{2,1,0:T(8,128)(2,1)} %shard_map.68), calls=%async_computation | async-start | bytes 2228224 | tf_op jit(solution)/shard_map/all_to_all | solution.py:466
  19.0 26.5 %all-to-all-done.own_ref = bf16[16,272,128]{2,1,0:T(8,128)(2,1)S(1)} async-done(((bf16[16,272,128]{2,1,0:T(8,128)(2,1)}), bf16[16,272,128]{2,1,0:T(8,128)(2,1)S(1)}, u32[]{:S(2)}, u32[]{:S(2)}) %all-to-all-start) | async-done | bytes 1114144 | tf_op jit(solution)/shard_map/all_to_all | solution.py:466
  45.6 0.1 constant_dynamic-slice_fusion
  45.7 5.8 %collective-permute-start.1 = (bf16[16,144,128]{2,1,0:T(8,128)(2,1)S(1)}, bf16[16,144,128]{2,1,0:T(8,128)(2,1)S(1)}, u32[]{:S(2)}, u32[]{:S(2)}) collective-permute-start(bf16[16,144,128]{2,1,0:T(8,128)(2,1)S(1)} %get-tuple-element.28), channel_id=1, source_target_pairs={{0,497},{1,496},{2,499},{3,498},{4,501},{5,500},{6,503},{7,502},{8... | collective-permute-start | bytes 1769480 | tf_op jit(solution)/shard_map/ppermute | solution.py:40
  51.4 6.1 %collective-permute-start = (bf16[16,144,128]{2,1,0:T(8,128)(2,1)S(1)}, bf16[16,144,128]{2,1,0:T(8,128)(2,1)S(1)}, u32[]{:S(2)}, u32[]{:S(2)}) collective-permute-start(bf16[16,144,128]{2,1,0:T(8,128)(2,1)S(1)} %get-tuple-element.29), channel_id=1, source_target_pairs={{0,16},{1,17},{2,18},{3,19},{4,20},{5,21},{6,22},{7,23},{8,24},{9,... | collective-permute-start | bytes 1769480 | tf_op jit(solution)/shard_map/ppermute | solution.py:40
  57.6 1.1 shard_map.69.t_ref
  58.6 2.5 %shard_map.71.inner_ref = f32[52,256,256]{2,1,0:T(8,128)S(1)} custom-call(s32[8]{0:T(128)S(1)} %copy-done.4, bf16[16,272,128]{2,1,0:T(8,128)(2,1)S(1)} %all-to-all-done.own_ref, f32[26,256,256]{2,1,0:T(8,128)S(1)} %shard_map.69.t_ref), custom_call_target="tpu_custom_call" | custom-call | flops 1744830464 | bytes 20971520 | tf_op jit(solution)/shard_map/pallas_call | solution.py:173
  61.2 2.1 %shard_map.70 = (f32[20,256,256]{2,1,0:T(8,128)S(1)}, f32[2,8,256]{2,1,0:T(8,128)S(1)}, f32[8,256]{1,0:T(8,128)S(1)}, f32[2,4,256]{2,1,0:T(4,128)S(1)}, f32[2,4,256]{2,1,0:T(4,128)S(1)}) custom-call(s32[8]{0:T(128)S(1)} %copy-done.4, bf16[16,272,128]{2,1,0:T(8,128)(2,1)S(1)} %all-to-all-done.own_ref, bf16[16,144,128]{2,1,0:T(8,128)(2,1)S(1)} %collective-permute-done.a_ref, ...), custom_call_target="tpu_custom_call" | custom-call | tf_op jit(solution)/shard_map/pallas_call | solution.py:280
  63.3 3.4 %shard_map.72 = (f32[2,8,256]{2,1,0:T(8,128)S(1)}, f32[2,4,256]{2,1,0:T(4,128)S(1)}, f32[2,4,256]{2,1,0:T(4,128)S(1)}) custom-call(f32[2,8,256]{2,1,0:T(8,128)S(1)} %get-tuple-element.15.p_ref.p0_ref, f32[2,4,256]{2,1,0:T(4,128)S(1)} %get-tuple-element.16.a_ref, f32[2,4,256]{2,1,0:T(4,128)S(1)} %get-tuple-element.17.b_ref, ...), custom_call_target="tpu_custom_call" | custom-call | tf_op jit(solution)/shard_map/pallas_call | solution.py:316
  66.7 3.9 %collective-permute-start.2 = (f32[2,4,256]{2,1,0:T(4,128)S(1)}, f32[2,4,256]{2,1,0:T(4,128)S(1)}, u32[]{:S(2)}, u32[]{:S(2)}) collective-permute-start(f32[2,4,256]{2,1,0:T(4,128)S(1)} %get-tuple-element.21), channel_id=1, source_target_pairs={{0,16},{1,17},{2,18},{3,19},{4,20},{5,21},{6,22},{7,23},{8,24},{9,... | collective-permute-start | bytes 24584 | tf_op jit(solution)/shard_map/ppermute | solution.py:40
  70.6 1.9 %collective-permute-start.3 = (f32[2,4,256]{2,1,0:T(4,128)S(1)}, f32[2,4,256]{2,1,0:T(4,128)S(1)}, u32[]{:S(2)}, u32[]{:S(2)}) collective-permute-start(f32[2,4,256]{2,1,0:T(4,128)S(1)} %get-tuple-element.22), channel_id=1, source_target_pairs={{0,497},{1,496},{2,499},{3,498},{4,501},{5,500},{6,503},{7,502},{8... | collective-permute-start | bytes 24584 | tf_op jit(solution)/shard_map/ppermute | solution.py:40
  72.5 3.0 %collective-permute-done.3.b_ref = f32[2,4,256]{2,1,0:T(4,128)S(1)} collective-permute-done((f32[2,4,256]{2,1,0:T(4,128)S(1)}, f32[2,4,256]{2,1,0:T(4,128)S(1)}, u32[]{:S(2)}, u32[]{:S(2)}) %collective-permute-start.3) | collective-permute-done | bytes 8224 | tf_op jit(solution)/shard_map/ppermute | solution.py:40
  75.5 3.4 %shard_map.73 = (f32[2,8,256]{2,1,0:T(8,128)S(1)}, f32[2,4,256]{2,1,0:T(4,128)S(1)}, f32[2,4,256]{2,1,0:T(4,128)S(1)}) custom-call(f32[2,8,256]{2,1,0:T(8,128)S(1)} %get-tuple-element.20.p_ref.p1_ref, f32[2,4,256]{2,1,0:T(4,128)S(1)} %collective-permute-done.2.a_ref, f32[2,4,256]{2,1,0:T(4,128)S(1)} %collective-permute-done.3.b_ref, ...), custom_call_target="tpu_custom_call" | custom-call | tf_op jit(solution)/shard_map/pallas_call | solution.py:316
  78.9 5.2 %collective-permute-start.4 = (f32[2,4,256]{2,1,0:T(4,128)S(1)}, f32[2,4,256]{2,1,0:T(4,128)S(1)}, u32[]{:S(2)}, u32[]{:S(2)}) collective-permute-start(f32[2,4,256]{2,1,0:T(4,128)S(1)} %get-tuple-element.24), channel_id=1, source_target_pairs={{0,16},{1,17},{2,18},{3,19},{4,20},{5,21},{6,22},{7,23},{8,24},{9,... | collective-permute-start | bytes 24584 | tf_op jit(solution)/shard_map/ppermute | solution.py:40
  84.2 2.1 %collective-permute-start.5 = (f32[2,4,256]{2,1,0:T(4,128)S(1)}, f32[2,4,256]{2,1,0:T(4,128)S(1)}, u32[]{:S(2)}, u32[]{:S(2)}) collective-permute-start(f32[2,4,256]{2,1,0:T(4,128)S(1)} %get-tuple-element.25), channel_id=1, source_target_pairs={{0,497},{1,496},{2,499},{3,498},{4,501},{5,500},{6,503},{7,502},{8... | collective-permute-start | bytes 24584 | tf_op jit(solution)/shard_map/ppermute | solution.py:40
  86.3 2.9 %collective-permute-done.5.b_ref = f32[2,4,256]{2,1,0:T(4,128)S(1)} collective-permute-done((f32[2,4,256]{2,1,0:T(4,128)S(1)}, f32[2,4,256]{2,1,0:T(4,128)S(1)}, u32[]{:S(2)}, u32[]{:S(2)}) %collective-permute-start.5) | collective-permute-done | bytes 8224 | tf_op jit(solution)/shard_map/ppermute | solution.py:40
  89.1 4.0 %shard_map.74 = (f32[2,8,256]{2,1,0:T(8,128)S(1)}, f32[32,8,128]{2,1,0:T(8,128)S(1)}) custom-call(f32[2,8,256]{2,1,0:T(8,128)S(1)} %get-tuple-element.23.p_ref.p2_ref, f32[2,4,256]{2,1,0:T(4,128)S(1)} %collective-permute-done.4.a_ref, f32[2,4,256]{2,1,0:T(4,128)S(1)} %collective-permute-done.5.b_ref, f32[8,256]{1,0:T(8,128)S(1)} %get-tuple-element.18.obs_ref, ...), custom_call_target="tpu_custom_call" | custom-call | tf_op jit(solution)/shard_map/pallas_call | solution.py:386
  93.1 28.9 %all_to_all.10.m_ref = f32[32,8,128]{2,1,0:T(8,128)S(1)} all-to-all(f32[32,8,128]{2,1,0:T(8,128)S(1)} %get-tuple-element.26), channel_id=1, replica_groups=mesh['space'=32,'member'=16] {'space'}, dimensions={0} | all-to-all | bytes 262144 | tf_op jit(solution)/shard_map/all_to_all | solution.py:478
  122.0 1.0 shard_map.75
  (12 shorter events, 0.0 us)
Async XLA Ops:
  0.6 0.8 copy-start.1
  1.5 0.7 copy-start.2
  2.2 0.7 copy-start.3
  2.8 0.7 copy-start.5
  3.5 54.0 %copy-start = (bf16[5,256,256]{2,1,0:T(8,128)(2,1)S(1)}, bf16[5,256,256]{2,1,0:T(8,128)(2,1)}, u32[]{:S(2)}) copy-start(bf16[5,256,256]{2,1,0:T(8,128)(2,1)} %loc_ref.1) | copy-start | bytes 1966084
  5.2 40.3 %all-to-all-start = ((bf16[16,272,128]{2,1,0:T(8,128)(2,1)}), bf16[16,272,128]{2,1,0:T(8,128)(2,1)S(1)}, u32[]{:S(2)}, u32[]{:S(2)}) async-start(bf16[16,272,128]{2,1,0:T(8,128)(2,1)} %shard_map.68), calls=%async_computation | async-start | bytes 2228224 | tf_op jit(solution)/shard_map/all_to_all | solution.py:466
  19.0 39.6 %copy-start.4 = (s32[8]{0:T(128)S(1)}, s32[8]{0:T(128)}, u32[]{:S(2)}) copy-start(s32[8]{0:T(128)} %reach_ref.5) | copy-start | bytes 100
  45.7 15.5 %collective-permute-start.1 = (bf16[16,144,128]{2,1,0:T(8,128)(2,1)S(1)}, bf16[16,144,128]{2,1,0:T(8,128)(2,1)S(1)}, u32[]{:S(2)}, u32[]{:S(2)}) collective-permute-start(bf16[16,144,128]{2,1,0:T(8,128)(2,1)S(1)} %get-tuple-element.28), channel_id=1, source_target_pairs={{0,497},{1,496},{2,499},{3,498},{4,501},{5,500},{6,503},{7,502},{8... | collective-permute-start | bytes 1769480 | tf_op jit(solution)/shard_map/ppermute | solution.py:40
  51.4 9.7 %collective-permute-start = (bf16[16,144,128]{2,1,0:T(8,128)(2,1)S(1)}, bf16[16,144,128]{2,1,0:T(8,128)(2,1)S(1)}, u32[]{:S(2)}, u32[]{:S(2)}) collective-permute-start(bf16[16,144,128]{2,1,0:T(8,128)(2,1)S(1)} %get-tuple-element.29), channel_id=1, source_target_pairs={{0,16},{1,17},{2,18},{3,19},{4,20},{5,21},{6,22},{7,23},{8,24},{9,... | collective-permute-start | bytes 1769480 | tf_op jit(solution)/shard_map/ppermute | solution.py:40
  66.7 5.8 %collective-permute-start.2 = (f32[2,4,256]{2,1,0:T(4,128)S(1)}, f32[2,4,256]{2,1,0:T(4,128)S(1)}, u32[]{:S(2)}, u32[]{:S(2)}) collective-permute-start(f32[2,4,256]{2,1,0:T(4,128)S(1)} %get-tuple-element.21), channel_id=1, source_target_pairs={{0,16},{1,17},{2,18},{3,19},{4,20},{5,21},{6,22},{7,23},{8,24},{9,... | collective-permute-start | bytes 24584 | tf_op jit(solution)/shard_map/ppermute | solution.py:40
  70.6 5.0 %collective-permute-start.3 = (f32[2,4,256]{2,1,0:T(4,128)S(1)}, f32[2,4,256]{2,1,0:T(4,128)S(1)}, u32[]{:S(2)}, u32[]{:S(2)}) collective-permute-start(f32[2,4,256]{2,1,0:T(4,128)S(1)} %get-tuple-element.22), channel_id=1, source_target_pairs={{0,497},{1,496},{2,499},{3,498},{4,501},{5,500},{6,503},{7,502},{8... | collective-permute-start | bytes 24584 | tf_op jit(solution)/shard_map/ppermute | solution.py:40
  78.9 7.4 %collective-permute-start.4 = (f32[2,4,256]{2,1,0:T(4,128)S(1)}, f32[2,4,256]{2,1,0:T(4,128)S(1)}, u32[]{:S(2)}, u32[]{:S(2)}) collective-permute-start(f32[2,4,256]{2,1,0:T(4,128)S(1)} %get-tuple-element.24), channel_id=1, source_target_pairs={{0,16},{1,17},{2,18},{3,19},{4,20},{5,21},{6,22},{7,23},{8,24},{9,... | collective-permute-start | bytes 24584 | tf_op jit(solution)/shard_map/ppermute | solution.py:40
  84.2 5.0 %collective-permute-start.5 = (f32[2,4,256]{2,1,0:T(4,128)S(1)}, f32[2,4,256]{2,1,0:T(4,128)S(1)}, u32[]{:S(2)}, u32[]{:S(2)}) collective-permute-start(f32[2,4,256]{2,1,0:T(4,128)S(1)} %get-tuple-element.25), channel_id=1, source_target_pairs={{0,497},{1,496},{2,499},{3,498},{4,501},{5,500},{6,503},{7,502},{8... | collective-permute-start | bytes 24584 | tf_op jit(solution)/shard_map/ppermute | solution.py:40

commit v4 on v3

--- a/solution.py
+++ b/solution.py
@@ -13,6 +13,7 @@
 
 VM = pl.BlockSpec(memory_space=pltpu.VMEM)
 SM = pl.BlockSpec(memory_space=pltpu.SMEM)
+HBM = pl.BlockSpec(memory_space=pltpu.HBM)
 
 FIELDS = 128
 PART = 144
@@ -40,8 +41,16 @@
     return lax.ppermute(block, ("space", "member"), route)
 
 
-def pack_kernel(anomalies_ref, reach_ref, obs_ref, innovations_ref, chunk_ref):
-    x = anomalies_ref[...].astype(jnp.float32)
+def pack_kernel(
+    anomalies_hbm, reach_hbm, obs_hbm, innovations_hbm, chunk_ref, x_ref, reach_ref, obs_ref, inn_ref, sems
+):
+    moves = [(anomalies_hbm, x_ref), (innovations_hbm, inn_ref), (obs_hbm, obs_ref), (reach_hbm, reach_ref)]
+    copies = [pltpu.make_async_copy(x, y, sems.at[i]) for i, (x, y) in enumerate(moves)]
+    for copy in copies:
+        copy.start()
+    for copy in copies:
+        copy.wait()
+    x = x_ref[...].astype(jnp.float32)
     rows = []
     for t in range(8):
         tile = x[:, t, :]
@@ -49,7 +58,7 @@
     lane = lax.broadcasted_iota(jnp.int32, (1, 128), 1)
     lines = []
     for a in range(3):
-        block = innovations_ref[a] if a < 2 else obs_ref[...]
+        block = inn_ref[a] if a < 2 else obs_ref[...]
         wide = jnp.concatenate([block, jnp.zeros((8, 112), jnp.float32)], axis=1)
         line = wide[0:1]
         for t in range(1, 8):
@@ -65,19 +74,48 @@
     fields = jnp.concatenate(
         [high, middle, rest - middle, reach, jnp.zeros((6, 128), jnp.float32)], axis=0
     )
-    chunk = jnp.concatenate(rows[:8] + [fields] + rows[8:], axis=0).astype(jnp.bfloat16)
-    for k in range(16):
-        chunk_ref[k] = chunk
+    chunk_ref[...] = jnp.concatenate(rows[:8] + [fields] + rows[8:], axis=0).astype(jnp.bfloat16)
 
 
 def pack(anomalies, tile_reach, obs_var, innovations):
     return pl.pallas_call(
         pack_kernel,
-        out_shape=jax.ShapeDtypeStruct((16, CHUNK, 128), jnp.bfloat16),
-        in_specs=[VM, SM, VM, VM],
+        out_shape=jax.ShapeDtypeStruct((CHUNK, 128), jnp.bfloat16),
+        in_specs=[HBM] * 4,
+        out_specs=VM,
+        scratch_shapes=[
+            pltpu.VMEM(anomalies.shape, jnp.bfloat16),
+            pltpu.SMEM((8,), jnp.int32),
+            pltpu.VMEM(obs_var.shape, jnp.float32),
+            pltpu.VMEM(innovations.shape, jnp.float32),
+            pltpu.SemaphoreType.DMA((4,)),
+        ],
+        compiler_params=params(8),
+    )(anomalies, tile_reach, obs_var, innovations)
+
+
+def spread_kernel(mine_ref, other_ref, out_ref):
+    y = lax.axis_index("member") % 2 == 0
+    low = jnp.where(y, mine_ref[...], other_ref[...])
+    high = jnp.where(y, other_ref[...], mine_ref[...])
+    for k in range(8):
+        out_ref[k, :CHUNK] = low
+        out_ref[k, CHUNK:] = high
+
+
+def gather_members(chunk):
+    n, m = lax.axis_size("space"), lax.axis_size("member")
+    other = lax.ppermute(chunk, "member", [(k, k ^ 1) for k in range(m)])
+    both = pl.pallas_call(
+        spread_kernel,
+        out_shape=jax.ShapeDtypeStruct((8, 2 * CHUNK, 128), jnp.bfloat16),
+        in_specs=[VM, VM],
         out_specs=VM,
         compiler_params=params(8),
-    )(anomalies, tile_reach, obs_var, innovations)
+    )(chunk, other)
+    groups = [[2 * z + y for z in range(8)] for y in range(2)]
+    out = lax.all_to_all(both, "member", 0, 0, axis_index_groups=groups)
+    return out.reshape(16, CHUNK, 128)
 
 
 def swap_blocks(x):
@@ -156,9 +194,54 @@
     )(loc_blocks)
 
 
-def inner_kernel(reach_ref, own_ref, t_ref, h_ref, xs):
+FIELD = jax.ShapeDtypeStruct((2, 8, 256), jnp.float32)
+HALO = jax.ShapeDtypeStruct((2, W, 256), jnp.float32)
+ROWS = 64
+
+
+def apply_blocks(pairs, block_ref, field_row):
+    out = []
+    for w in range(8):
+        mine = [(k, w + shift) for k, (row, shift) in enumerate(pairs) if row == w]
+        done = [[], []]
+        for c in range(0, 256, ROWS):
+            acc = [None, None]
+            for k, other in mine:
+                block = block_ref[k, c : c + ROWS, :]
+                for f in range(2):
+                    p = block * field_row(f, other)
+                    p = p[:, :128] + p[:, 128:]
+                    acc[f] = p if acc[f] is None else acc[f] + p
+            for f in range(2):
+                done[f].append(acc[f])
+        for f in range(2):
+            total = jnp.sum(jnp.concatenate(done[f], axis=0).T, axis=0, keepdims=True)
+            out.append((f, w, total))
+    return out
+
+
+def apply_inner(inner_ref, p_ref, obs_ref, part_ref):
+    for f, w, total in apply_blocks(INNER, inner_ref, lambda f, t: p_ref[f, t : t + 1, :]):
+        own = (obs_ref[w : w + 1, :] * SCALE) * p_ref[f, w : w + 1, :]
+        part_ref[f, w : w + 1, :] = total + own
+
+
+def apply_outer(outer_ref, part_ref, halo, y_ref):
+    def row(f, t):
+        at = t + W if t < 0 else t - W
+        return halo[f, at : at + 1, :]
+
+    for f, w, total in apply_blocks(OUTER, outer_ref, row):
+        y_ref[f, w : w + 1, :] = total + part_ref[f, w : w + 1, :]
+
+
+def inner_kernel(reach_ref, own_ref, t_ref, h_ref, p0_ref, obs_ref, part_ref, xs):
     for w in range(8):
         xs[w] = tile_of(own_ref, 32 * w + (16 if w >= 4 else 0))
+    fields = unpack_fields(own_ref[:, FIELDS : FIELDS + 16, :])
+    for f in range(2):
+        p0_ref[f] = fields[f]
+    obs_ref[...] = fields[2]
     for w in range(8):
         rows = xs[w].T
         for shift in range(-W, W + 1):
@@ -167,55 +250,26 @@
             entry = table_entry(shift, reach_ref[w], reach_ref[w + shift])
             covariance = jnp.dot(rows, xs[w + shift], preferred_element_type=jnp.float32)
             h_ref[INNER.index((w, shift))] = covariance * t_ref[entry]
+    apply_inner(h_ref, p0_ref, obs_ref, part_ref)
 
 
 def inner_blocks(reach, own, table):
     return pl.pallas_call(
         inner_kernel,
-        out_shape=jax.ShapeDtypeStruct((len(INNER), 256, 256), jnp.float32),
+        out_shape=(
+            jax.ShapeDtypeStruct((len(INNER), 256, 256), jnp.float32),
+            FIELD,
+            jax.ShapeDtypeStruct((8, 256), jnp.float32),
+            FIELD,
+        ),
         in_specs=[SM, VM, VM],
-        out_specs=VM,
+        out_specs=(VM,) * 4,
         scratch_shapes=[pltpu.VMEM((8, 256, 256), jnp.bfloat16)],
         compiler_params=params(26),
         cost_estimate=pl.CostEstimate(
-            flops=52 * 2 * 256**3, bytes_accessed=20 * MIB, transcendentals=0
+            flops=100 * 2 * 256**3, bytes_accessed=20 * MIB, transcendentals=0
         ),
     )(reach, own, table)
-
-
-def add_products(acc, block, v_rows):
-    for f in range(2):
-        p = block * v_rows[f]
-        p = p[:, :128] + p[:, 128:]
-        acc[f] = p if acc[f] is None else acc[f] + p
-
-
-def row_sums(parts):
-    return jnp.sum(jnp.concatenate(parts, axis=0).T, axis=0, keepdims=True)
-
-
-ROWS = 64
-
-
-def apply_blocks(inner_ref, outer_ref, v_ref, obs_ref, y):
-    for w in range(8):
-        done = [[], []]
-        for c in range(0, 256, ROWS):
-            acc = [None, None]
-            for shift in range(-W, W + 1):
-                other = w + shift
-                if 0 <= other < 8:
-                    block = inner_ref[INNER.index((w, shift)), c : c + ROWS, :]
-                else:
-                    block = outer_ref[OUTER.index((w, shift)), c : c + ROWS, :]
-                rows = [v_ref[f, other + W : other + W + 1, :] for f in range(2)]
-                add_products(acc, block, rows)
-            for f in range(2):
-                done[f].append(acc[f])
-        for f in range(2):
-            y[f, w : w + 1, :] = row_sums(done[f]) + (obs_ref[w : w + 1, :] * SCALE) * v_ref[
-                f, w + W : w + W + 1, :
-            ]
 
 
 def set_sends(even, p, a_ref, b_ref):
@@ -225,10 +279,16 @@
         b_ref[f] = jnp.where(even, low, high)
 
 
+def fill_halo(even, a, b, halo):
+    for f in range(2):
+        halo[f, :W] = jnp.where(even, b[f], a[f])
+        halo[f, W:] = jnp.where(even, a[f], b[f])
+
+
 def outer_kernel(
-    reach_ref, own_ref, a_ref, b_ref, t_ref,
-    outer_ref, p0_ref, obs_ref, field_a_ref, field_b_ref,
-    xs, lines,
+    reach_ref, own_ref, a_ref, b_ref, t_ref, part_ref,
+    outer_ref, y_ref, send_a_ref, send_b_ref,
+    xs, lines, halo,
 ):
     even = lax.axis_index("space") % 2 == 0
     a_low, b_low = jnp.where(even, 0, 16), jnp.where(even, 16, 0)
@@ -256,12 +316,12 @@
 
     reach = {tile: reach_of(tile) for tile in range(-W, 8 + W)}
     a_fields, b_fields = unpack_fields(lines[0]), unpack_fields(lines[1])
-    own_fields = unpack_fields(own_ref[:, FIELDS : FIELDS + 16, :])
-    for f in range(2):
-        field_a_ref[f] = jnp.where(even, a_fields[f][:W], a_fields[f][W:])
-        field_b_ref[f] = jnp.where(even, b_fields[f][W:], b_fields[f][:W])
-        p0_ref[f] = own_fields[f]
-    obs_ref[...] = own_fields[2]
+    fill_halo(
+        even,
+        [jnp.where(even, x[:W], x[W:]) for x in a_fields[:2]],
+        [jnp.where(even, x[W:], x[:W]) for x in b_fields[:2]],
+        halo,
+    )
     for w in range(8):
         rows = xs[w + W].T
         for shift in range(-W, W + 1):
@@ -270,57 +330,59 @@
             entry = table_entry(shift, reach[w], reach[w + shift])
             covariance = jnp.dot(rows, xs[w + shift + W], preferred_element_type=jnp.float32)
             outer_ref[OUTER.index((w, shift))] = covariance * t_ref[entry]
-
-
-FIELD = jax.ShapeDtypeStruct((2, 8, 256), jnp.float32)
-HALO = jax.ShapeDtypeStruct((2, W, 256), jnp.float32)
-
-
-def outer_blocks(reach, own, a, b, table):
+    apply_outer(outer_ref, part_ref, halo, y_ref)
+    set_sends(even, y_ref, send_a_ref, send_b_ref)
+
+
+def outer_blocks(reach, own, a, b, table, part):
     return pl.pallas_call(
         outer_kernel,
         out_shape=(
             jax.ShapeDtypeStruct((len(OUTER), 256, 256), jnp.float32),
             FIELD,
-            jax.ShapeDtypeStruct((8, 256), jnp.float32),
             HALO,
             HALO,
         ),
-        in_specs=[SM] + [VM] * 4,
-        out_specs=(VM,) * 5,
+        in_specs=[SM] + [VM] * 5,
+        out_specs=(VM,) * 4,
         scratch_shapes=[
             pltpu.VMEM((16, 256, 256), jnp.bfloat16),
             pltpu.VMEM((2, 16, 16, 128), jnp.bfloat16),
+            pltpu.VMEM((2, 8, 256), jnp.float32),
         ],
         compiler_params=params(22),
-    )(reach, own, a, b, table)
-
-
-def fill_window(even, p_ref, a_ref, b_ref, v):
-    for f in range(2):
-        v[f, :W] = jnp.where(even, b_ref[f], a_ref[f])
-        v[f, W : W + 8] = p_ref[f]
-        v[f, W + 8 :] = jnp.where(even, a_ref[f], b_ref[f])
-
-
-def next_kernel(
-    p_ref, a_ref, b_ref, obs_ref, inner_ref, outer_ref, y_ref, send_a_ref, send_b_ref, v
-):
+    )(reach, own, a, b, table, part)
+
+
+def next_inner(p, obs, inner):
+    return pl.pallas_call(
+        lambda p_ref, obs_ref, inner_ref, part_ref: apply_inner(inner_ref, p_ref, obs_ref, part_ref),
+        out_shape=FIELD,
+        in_specs=[VM] * 3,
+        out_specs=VM,
+        compiler_params=params(18),
+        cost_estimate=pl.CostEstimate(
+            flops=50 * 2 * 256**3, bytes_accessed=14 * MIB, transcendentals=0
+        ),
+    )(p, obs, inner)
+
+
+def next_kernel(part_ref, a_ref, b_ref, outer_ref, y_ref, send_a_ref, send_b_ref, halo):
     even = lax.axis_index("space") % 2 == 0
-    fill_window(even, p_ref, a_ref, b_ref, v)
-    apply_blocks(inner_ref, outer_ref, v, obs_ref, y_ref)
+    fill_halo(even, a_ref, b_ref, halo)
+    apply_outer(outer_ref, part_ref, halo, y_ref)
     set_sends(even, y_ref, send_a_ref, send_b_ref)
 
 
-def next_application(p, a, b, obs, inner, outer):
+def next_outer(part, a, b, outer):
     return pl.pallas_call(
         next_kernel,
         out_shape=(FIELD, HALO, HALO),
-        in_specs=[VM] * 6,
+        in_specs=[VM] * 4,
         out_specs=(VM,) * 3,
-        scratch_shapes=[pltpu.VMEM((2, 16, 256), jnp.float32)],
-        compiler_params=params(24),
-    )(p, a, b, obs, inner, outer)
+        scratch_shapes=[pltpu.VMEM((2, 8, 256), jnp.float32)],
+        compiler_params=params(10),
+    )(part, a, b, outer)
 
 
 def two_sum(a, b):
@@ -354,13 +416,11 @@
     return p, e + (x[0] * y[1] + x[1] * y[0])
 
 
-def last_kernel(
-    p_ref, a_ref, b_ref, obs_ref, inner_ref, outer_ref, p0_ref, p1_ref, y_ref, m_ref, v
-):
+def last_kernel(part_ref, a_ref, b_ref, outer_ref, p0_ref, p1_ref, p2_ref, y_ref, m_ref, halo):
     even = lax.axis_index("space") % 2 == 0
-    fill_window(even, p_ref, a_ref, b_ref, v)
-    apply_blocks(inner_ref, outer_ref, v, obs_ref, y_ref)
-    powers = [p0_ref, p1_ref, p_ref, y_ref]
+    fill_halo(even, a_ref, b_ref, halo)
+    apply_outer(outer_ref, part_ref, halo, y_ref)
+    powers = [p0_ref, p1_ref, p2_ref, y_ref]
     row = lax.broadcasted_iota(jnp.int32, (8, 128), 0)
     lane = lax.broadcasted_iota(jnp.int32, (8, 128), 1)
     sums = []
@@ -382,15 +442,15 @@
         m_ref[k] = out
 
 
-def last_application(p, a, b, obs, inner, outer, p0, p1):
+def last_outer(part, a, b, outer, p0, p1, p2):
     return pl.pallas_call(
         last_kernel,
         out_shape=(FIELD, jax.ShapeDtypeStruct((32, 8, 128), jnp.float32)),
-        in_specs=[VM] * 8,
+        in_specs=[VM] * 7,
         out_specs=(VM,) * 2,
-        scratch_shapes=[pltpu.VMEM((2, 16, 256), jnp.float32)],
-        compiler_params=params(24),
-    )(p, a, b, obs, inner, outer, p0, p1)
+        scratch_shapes=[pltpu.VMEM((2, 8, 256), jnp.float32)],
+        compiler_params=params(10),
+    )(part, a, b, outer, p0, p1, p2)
 
 
 def square_dot(poly, moment):
@@ -462,19 +522,19 @@
 
 def on_device(anomalies, loc_blocks, tile_reach, obs_var, innovations):
     table = make_tables(loc_blocks)
-    chunk = pack(anomalies, tile_reach, obs_var, innovations)
-    own = lax.all_to_all(chunk, "member", 0, 0)
+    own = gather_members(pack(anomalies, tile_reach, obs_var, innovations))
     odd = lax.axis_index("space") % 2
     to_a = lax.dynamic_slice_in_dim(own, 128 * (1 - odd), PART, 1)
     to_b = lax.dynamic_slice_in_dim(own, 128 * odd, PART, 1)
     a, b = pair_swap(to_a, 0), pair_swap(to_b, 1)
-    inner = inner_blocks(tile_reach, own, table)
-    outer, p0, obs, a, b = outer_blocks(tile_reach, own, a, b, table)
-    p1, to_a, to_b = next_application(p0, a, b, obs, inner, outer)
+    inner, p0, obs, part = inner_blocks(tile_reach, own, table)
+    outer, p1, to_a, to_b = outer_blocks(tile_reach, own, a, b, table, part)
     a, b = pair_swap(to_a, 0), pair_swap(to_b, 1)
-    p2, to_a, to_b = next_application(p1, a, b, obs, inner, outer)
+    part = next_inner(p1, obs, inner)
+    p2, to_a, to_b = next_outer(part, a, b, outer)
     a, b = pair_swap(to_a, 0), pair_swap(to_b, 1)
-    p3, m = last_application(p2, a, b, obs, inner, outer, p0, p1)
+    part = next_inner(p2, obs, inner)
+    p3, m = last_outer(part, a, b, outer, p0, p1, p2)
     m = lax.all_to_all(m, "space", 0, 0)
     return finish(m, [p0, p1, p2, p3])
 

time: 123 us -> 113 us (0.919)
  the two profiles are of different devices: /device:TPU:129 before, /device:TPU:1 now
where the time goes in v4:
time: 113 us
  starting transfers between devices  43.2 us (38%)
  waiting for transfers between devices  32.6 us (29%)
  Pallas kernels  18.2 us (16%)
  blocking collectives  15.2 us (13%)
  local copies, waits for them, and re-layouts  2.95 us (3%)
    all_to_all x1, waiting for transfers between devices, gather_members(): out = lax.all_to_all(both, 'member', 0, 0, axis_index_groups=groups)  28.8 us
    ppermute x6, starting transfers between devices, pair_swap(): return lax.ppermute(block, ('space', 'member'), route)  24.9 us
    all_to_all x1, blocking collectives, on_device(): m = lax.all_to_all(m, 'space', 0, 0)  15.2 us
    all_to_all x1, starting transfers between devices, gather_members(): out = lax.all_to_all(both, 'member', 0, 0, axis_index_groups=groups)  10 us
    ppermute x1, starting transfers between devices, gather_members(): other = lax.ppermute(chunk, 'member', [(k, k ^ 1) for k in range(m)])  8.28 us
    pallas_call x1, Pallas kernels, inner_blocks(): pl.pallas_call(inner_kernel, out_shape=(jax.ShapeDtypeStruct((len(INNER),...  4.99 us
    pallas_call x2, Pallas kernels, next_inner(): pl.pallas_call(lambda p_ref, obs_ref, inner_ref, part_ref: apply_inner(in...  3.88 us
    pallas_call x1, Pallas kernels, outer_blocks(): pl.pallas_call(outer_kernel, out_shape=(jax.ShapeDtypeStruct((len(OUTER),...  2.89 us
  transfers between devices with their start and end apart: 8, of which 4 were waited for; matrix products, arithmetic and copies ran while one was open for 0% of the time, Pallas kernels for 9%

profile of v4, /device:TPU:1, one launch (start us, length us, event | category | flops | bytes accessed | tf_op | source)
XLA Modules:
  0.0 113.0 jit_solution(2505401891239374528)
XLA Ops:
  0.6 0.8 copy-done.1
  3.5 0.7 shard_map.68.mine_ref
  4.3 8.3 %collective-permute-start = (bf16[272,128]{1,0:T(8,128)(2,1)S(1)}, bf16[272,128]{1,0:T(8,128)(2,1)S(1)}, u32[]{:S(2)}, u32[]{:S(2)}) collective-permute-start(bf16[272,128]{1,0:T(8,128)(2,1)S(1)} %shard_map.68.mine_ref), channel_id=1, source_target_pairs={{0,1},{1,0},{2,3},{3,2},{4,5},{5,4},{6,7},{7,6},{8,9},{9,8},{10,11... | collective-permute-start | bytes 208904 | tf_op jit(solution)/shard_map/ppermute | solution.py:108
  12.6 1.8 %collective-permute-done.other_ref = bf16[272,128]{1,0:T(8,128)(2,1)S(1)} collective-permute-done((bf16[272,128]{1,0:T(8,128)(2,1)S(1)}, bf16[272,128]{1,0:T(8,128)(2,1)S(1)}, u32[]{:S(2)}, u32[]{:S(2)}) %collective-permute-start) | collective-permute-done | bytes 69664 | tf_op jit(solution)/shard_map/ppermute | solution.py:108
  14.3 1.2 %shard_map.69 = bf16[8,544,128]{2,1,0:T(8,128)(2,1)} custom-call(bf16[272,128]{1,0:T(8,128)(2,1)S(1)} %shard_map.68.mine_ref, bf16[272,128]{1,0:T(8,128)(2,1)S(1)} %collective-permute-done.other_ref), custom_call_target="tpu_custom_call" | custom-call | tf_op jit(solution)/shard_map/pallas_call | solution.py:109
  15.5 10.0 %all-to-all-start = ((bf16[8,544,128]{2,1,0:T(8,128)(2,1)}), bf16[8,544,128]{2,1,0:T(8,128)(2,1)S(1)}, u32[]{:S(2)}, u32[]{:S(2)}) async-start(bf16[8,544,128]{2,1,0:T(8,128)(2,1)} %shard_map.69), calls=%async_computation | async-start | bytes 2228224 | tf_op jit(solution)/shard_map/all_to_all | solution.py:117
  25.6 28.8 %all-to-all-done = bf16[8,544,128]{2,1,0:T(8,128)(2,1)S(1)} async-done(((bf16[8,544,128]{2,1,0:T(8,128)(2,1)}), bf16[8,544,128]{2,1,0:T(8,128)(2,1)S(1)}, u32[]{:S(2)}, u32[]{:S(2)}) %all-to-all-start) | async-done | bytes 1114144 | tf_op jit(solution)/shard_map/all_to_all | solution.py:117
  54.4 5.3 %collective-permute-start.2 = (bf16[16,144,128]{2,1,0:T(8,128)(2,1)S(1)}, bf16[16,144,128]{2,1,0:T(8,128)(2,1)S(1)}, u32[]{:S(2)}, u32[]{:S(2)}) collective-permute-start(bf16[16,144,128]{2,1,0:T(8,128)(2,1)S(1)} %get-tuple-element.28), channel_id=1, source_target_pairs={{0,497},{1,496},{2,499},{3,498},{4,501},{5,500},{6,503},{7,502},{8... | collective-permute-start | bytes 1769480 | tf_op jit(solution)/shard_map/ppermute | solution.py:41
  59.7 8.0 %collective-permute-start.1 = (bf16[16,144,128]{2,1,0:T(8,128)(2,1)S(1)}, bf16[16,144,128]{2,1,0:T(8,128)(2,1)S(1)}, u32[]{:S(2)}, u32[]{:S(2)}) collective-permute-start(bf16[16,144,128]{2,1,0:T(8,128)(2,1)S(1)} %get-tuple-element.29), channel_id=1, source_target_pairs={{0,16},{1,17},{2,18},{3,19},{4,20},{5,21},{6,22},{7,23},{8,24},{9,... | collective-permute-start | bytes 1769480 | tf_op jit(solution)/shard_map/ppermute | solution.py:41
  67.7 1.1 shard_map.70.t_ref
  68.8 5.0 %shard_map.71 = (f32[52,256,256]{2,1,0:T(8,128)S(1)}, f32[2,8,256]{2,1,0:T(8,128)S(1)}, f32[8,256]{1,0:T(8,128)S(1)}, f32[2,8,256]{2,1,0:T(8,128)S(1)}) custom-call(s32[8]{0:T(128)S(1)} %copy-done.5, bf16[16,272,128]{2,1,0:T(8,128)(2,1)S(1)} %bitcast.2, f32[26,256,256]{2,1,0:T(8,128)S(1)} %shard_map.70.t_ref), custom_call_target="tpu_custom_call" | custom-call | flops 3355443200 | bytes 20971520 | tf_op jit(solution)/shard_map/pallas_call | solution.py:257
  73.8 2.9 %shard_map.72 = (f32[20,256,256]{2,1,0:T(8,128)S(1)}, f32[2,8,256]{2,1,0:T(8,128)S(1)}, f32[2,4,256]{2,1,0:T(4,128)S(1)}, f32[2,4,256]{2,1,0:T(4,128)S(1)}) custom-call(s32[8]{0:T(128)S(1)} %copy-done.5, bf16[16,272,128]{2,1,0:T(8,128)(2,1)S(1)} %bitcast.3, bf16[16,144,128]{2,1,0:T(8,128)(2,1)S(1)} %collective-permute-done.1.a_ref, ...), custom_call_target="tpu_custom_call" | custom-call | tf_op jit(solution)/shard_map/pallas_call | solution.py:338
  76.7 1.9 %collective-permute-start.3 = (f32[2,4,256]{2,1,0:T(4,128)S(1)}, f32[2,4,256]{2,1,0:T(4,128)S(1)}, u32[]{:S(2)}, u32[]{:S(2)}) collective-permute-start(f32[2,4,256]{2,1,0:T(4,128)S(1)} %get-tuple-element.19), channel_id=1, source_target_pairs={{0,16},{1,17},{2,18},{3,19},{4,20},{5,21},{6,22},{7,23},{8,24},{9,... | collective-permute-start | bytes 24584 | tf_op jit(solution)/shard_map/ppermute | solution.py:41
  78.6 1.9 %collective-permute-start.4 = (f32[2,4,256]{2,1,0:T(4,128)S(1)}, f32[2,4,256]{2,1,0:T(4,128)S(1)}, u32[]{:S(2)}, u32[]{:S(2)}) collective-permute-start(f32[2,4,256]{2,1,0:T(4,128)S(1)} %get-tuple-element.20), channel_id=1, source_target_pairs={{0,497},{1,496},{2,499},{3,498},{4,501},{5,500},{6,503},{7,502},{8... | collective-permute-start | bytes 24584 | tf_op jit(solution)/shard_map/ppermute | solution.py:41
  80.5 1.9 %shard_map.73.part_ref = f32[2,8,256]{2,1,0:T(8,128)S(1)} custom-call(f32[2,8,256]{2,1,0:T(8,128)S(1)} %get-tuple-element.16.p_ref.p1_ref, f32[8,256]{1,0:T(8,128)S(1)} %get-tuple-element.17.obs_ref, f32[52,256,256]{2,1,0:T(8,128)S(1)} %get-tuple-element.18.inner_ref), custom_call_target="tpu_custom_call" | custom-call | flops 1677721600 | bytes 14680064 | tf_op jit(solution)/shard_map/pallas_call | solution.py:358
  82.4 1.1 %collective-permute-done.4.b_ref = f32[2,4,256]{2,1,0:T(4,128)S(1)} collective-permute-done((f32[2,4,256]{2,1,0:T(4,128)S(1)}, f32[2,4,256]{2,1,0:T(4,128)S(1)}, u32[]{:S(2)}, u32[]{:S(2)}) %collective-permute-start.4) | collective-permute-done | bytes 8224 | tf_op jit(solution)/shard_map/ppermute | solution.py:41
  83.6 1.0 shard_map.74
  84.5 5.7 %collective-permute-start.5 = (f32[2,4,256]{2,1,0:T(4,128)S(1)}, f32[2,4,256]{2,1,0:T(4,128)S(1)}, u32[]{:S(2)}, u32[]{:S(2)}) collective-permute-start(f32[2,4,256]{2,1,0:T(4,128)S(1)} %get-tuple-element.23), channel_id=1, source_target_pairs={{0,16},{1,17},{2,18},{3,19},{4,20},{5,21},{6,22},{7,23},{8,24},{9,... | collective-permute-start | bytes 24584 | tf_op jit(solution)/shard_map/ppermute | solution.py:41
  90.3 2.1 %collective-permute-start.6 = (f32[2,4,256]{2,1,0:T(4,128)S(1)}, f32[2,4,256]{2,1,0:T(4,128)S(1)}, u32[]{:S(2)}, u32[]{:S(2)}) collective-permute-start(f32[2,4,256]{2,1,0:T(4,128)S(1)} %get-tuple-element.24), channel_id=1, source_target_pairs={{0,497},{1,496},{2,499},{3,498},{4,501},{5,500},{6,503},{7,502},{8... | collective-permute-start | bytes 24584 | tf_op jit(solution)/shard_map/ppermute | solution.py:41
  92.4 2.0 %shard_map.75.part_ref = f32[2,8,256]{2,1,0:T(8,128)S(1)} custom-call(f32[2,8,256]{2,1,0:T(8,128)S(1)} %get-tuple-element.22.p_ref.p2_ref, f32[8,256]{1,0:T(8,128)S(1)} %get-tuple-element.17.obs_ref, f32[52,256,256]{2,1,0:T(8,128)S(1)} %get-tuple-element.18.inner_ref), custom_call_target="tpu_custom_call" | custom-call | flops 1677721600 | bytes 14680064 | tf_op jit(solution)/shard_map/pallas_call | solution.py:358
  94.4 0.9 collective-permute-done.6.b_ref
  95.2 1.6 %shard_map.76 = (f32[2,8,256]{2,1,0:T(8,128)S(1)}, f32[32,8,128]{2,1,0:T(8,128)S(1)}) custom-call(f32[2,8,256]{2,1,0:T(8,128)S(1)} %shard_map.75.part_ref, f32[2,4,256]{2,1,0:T(4,128)S(1)} %collective-permute-done.5.a_ref, f32[2,4,256]{2,1,0:T(4,128)S(1)} %collective-permute-done.6.b_ref, f32[20,256,256]{2,1,0:T(8,128)S(1)} %get-tuple-element.21.outer_ref, ...), custom_call_target="tpu_custom_call" | custom-call | tf_op jit(solution)/shard_map/pallas_call | solution.py:446
  96.8 15.2 %all_to_all.10.m_ref = f32[32,8,128]{2,1,0:T(8,128)S(1)} all-to-all(f32[32,8,128]{2,1,0:T(8,128)S(1)} %get-tuple-element.26), channel_id=1, replica_groups=mesh['space'=32,'member'=16] {'space'}, dimensions={0} | all-to-all | bytes 262144 | tf_op jit(solution)/shard_map/all_to_all | solution.py:538
  112.0 1.0 shard_map.77
  (16 shorter events, 2.1 us)
Async XLA Ops:
  0.6 0.8 copy-start.1
  1.5 0.7 copy-start.2
  2.2 0.7 copy-start.3
  2.9 0.7 copy-start.4
  3.5 64.2 %copy-start = (bf16[5,256,256]{2,1,0:T(8,128)(2,1)S(1)}, bf16[5,256,256]{2,1,0:T(8,128)(2,1)}, u32[]{:S(2)}) copy-start(bf16[5,256,256]{2,1,0:T(8,128)(2,1)} %loc_ref.1) | copy-start | bytes 1966084
  4.3 10.1 %collective-permute-start = (bf16[272,128]{1,0:T(8,128)(2,1)S(1)}, bf16[272,128]{1,0:T(8,128)(2,1)S(1)}, u32[]{:S(2)}, u32[]{:S(2)}) collective-permute-start(bf16[272,128]{1,0:T(8,128)(2,1)S(1)} %shard_map.68.mine_ref), channel_id=1, source_target_pairs={{0,1},{1,0},{2,3},{3,2},{4,5},{5,4},{6,7},{7,6},{8,9},{9,8},{10,11... | collective-permute-start | bytes 208904 | tf_op jit(solution)/shard_map/ppermute | solution.py:108
  15.5 38.9 %all-to-all-start = ((bf16[8,544,128]{2,1,0:T(8,128)(2,1)}), bf16[8,544,128]{2,1,0:T(8,128)(2,1)S(1)}, u32[]{:S(2)}, u32[]{:S(2)}) async-start(bf16[8,544,128]{2,1,0:T(8,128)(2,1)} %shard_map.69), calls=%async_computation | async-start | bytes 2228224 | tf_op jit(solution)/shard_map/all_to_all | solution.py:117
  25.5 43.2 %copy-start.5 = (s32[8]{0:T(128)S(1)}, s32[8]{0:T(128)}, u32[]{:S(2)}) copy-start(s32[8]{0:T(128)} %reach_ref.3) | copy-start | bytes 100
  54.4 19.3 %collective-permute-start.2 = (bf16[16,144,128]{2,1,0:T(8,128)(2,1)S(1)}, bf16[16,144,128]{2,1,0:T(8,128)(2,1)S(1)}, u32[]{:S(2)}, u32[]{:S(2)}) collective-permute-start(bf16[16,144,128]{2,1,0:T(8,128)(2,1)S(1)} %get-tuple-element.28), channel_id=1, source_target_pairs={{0,497},{1,496},{2,499},{3,498},{4,501},{5,500},{6,503},{7,502},{8... | collective-permute-start | bytes 1769480 | tf_op jit(solution)/shard_map/ppermute | solution.py:41
  59.7 14.1 %collective-permute-start.1 = (bf16[16,144,128]{2,1,0:T(8,128)(2,1)S(1)}, bf16[16,144,128]{2,1,0:T(8,128)(2,1)S(1)}, u32[]{:S(2)}, u32[]{:S(2)}) collective-permute-start(bf16[16,144,128]{2,1,0:T(8,128)(2,1)S(1)} %get-tuple-element.29), channel_id=1, source_target_pairs={{0,16},{1,17},{2,18},{3,19},{4,20},{5,21},{6,22},{7,23},{8,24},{9,... | collective-permute-start | bytes 1769480 | tf_op jit(solution)/shard_map/ppermute | solution.py:41
  76.7 5.7 %collective-permute-start.3 = (f32[2,4,256]{2,1,0:T(4,128)S(1)}, f32[2,4,256]{2,1,0:T(4,128)S(1)}, u32[]{:S(2)}, u32[]{:S(2)}) collective-permute-start(f32[2,4,256]{2,1,0:T(4,128)S(1)} %get-tuple-element.19), channel_id=1, source_target_pairs={{0,16},{1,17},{2,18},{3,19},{4,20},{5,21},{6,22},{7,23},{8,24},{9,... | collective-permute-start | bytes 24584 | tf_op jit(solution)/shard_map/ppermute | solution.py:41
  78.6 5.0 %collective-permute-start.4 = (f32[2,4,256]{2,1,0:T(4,128)S(1)}, f32[2,4,256]{2,1,0:T(4,128)S(1)}, u32[]{:S(2)}, u32[]{:S(2)}) collective-permute-start(f32[2,4,256]{2,1,0:T(4,128)S(1)} %get-tuple-element.20), channel_id=1, source_target_pairs={{0,497},{1,496},{2,499},{3,498},{4,501},{5,500},{6,503},{7,502},{8... | collective-permute-start | bytes 24584 | tf_op jit(solution)/shard_map/ppermute | solution.py:41
  84.5 9.8 %collective-permute-start.5 = (f32[2,4,256]{2,1,0:T(4,128)S(1)}, f32[2,4,256]{2,1,0:T(4,128)S(1)}, u32[]{:S(2)}, u32[]{:S(2)}) collective-permute-start(f32[2,4,256]{2,1,0:T(4,128)S(1)} %get-tuple-element.23), channel_id=1, source_target_pairs={{0,16},{1,17},{2,18},{3,19},{4,20},{5,21},{6,22},{7,23},{8,24},{9,... | collective-permute-start | bytes 24584 | tf_op jit(solution)/shard_map/ppermute | solution.py:41
  90.3 5.0 %collective-permute-start.6 = (f32[2,4,256]{2,1,0:T(4,128)S(1)}, f32[2,4,256]{2,1,0:T(4,128)S(1)}, u32[]{:S(2)}, u32[]{:S(2)}) collective-permute-start(f32[2,4,256]{2,1,0:T(4,128)S(1)} %get-tuple-element.24), channel_id=1, source_target_pairs={{0,497},{1,496},{2,499},{3,498},{4,501},{5,500},{6,503},{7,502},{8... | collective-permute-start | bytes 24584 | tf_op jit(solution)/shard_map/ppermute | solution.py:41

commit v5 on v4

--- a/solution.py
+++ b/solution.py
@@ -10,6 +10,7 @@
 EPSILON = 1e-6
 SCALE = 2.0**-8
 MIB = 1 << 20
+PACK_MIB = 63
 
 VM = pl.BlockSpec(memory_space=pltpu.VMEM)
 SM = pl.BlockSpec(memory_space=pltpu.SMEM)
@@ -90,7 +91,7 @@
             pltpu.VMEM(innovations.shape, jnp.float32),
             pltpu.SemaphoreType.DMA((4,)),
         ],
-        compiler_params=params(8),
+        compiler_params=params(PACK_MIB),
     )(anomalies, tile_reach, obs_var, innovations)
 
 
@@ -161,7 +162,7 @@
     return jnp.where(last >= 0, base + last, N_TABLE - 1)
 
 
-def table_kernel(loc_ref, t_ref):
+def fill_table(loc_ref, t_ref):
     factor = SCALE / 255.0
     k = 0
     for d in range(W + 1):
@@ -179,19 +180,6 @@
             t_ref[k] = total * factor
             k += 1
     t_ref[k] = jnp.zeros(t_ref.shape[1:], jnp.float32)
-
-
-def make_tables(loc_blocks):
-    return pl.pallas_call(
-        table_kernel,
-        out_shape=jax.ShapeDtypeStruct((N_TABLE, 256, 256), jnp.float32),
-        in_specs=[VM],
-        out_specs=VM,
-        compiler_params=params(14),
-        cost_estimate=pl.CostEstimate(
-            flops=25 * 2 * 256**3, bytes_accessed=7 * MIB, transcendentals=0
-        ),
-    )(loc_blocks)
 
 
 FIELD = jax.ShapeDtypeStruct((2, 8, 256), jnp.float32)
@@ -235,7 +223,8 @@
         y_ref[f, w : w + 1, :] = total + part_ref[f, w : w + 1, :]
 
 
-def inner_kernel(reach_ref, own_ref, t_ref, h_ref, p0_ref, obs_ref, part_ref, xs):
+def inner_kernel(reach_ref, loc_ref, own_ref, t_ref, h_ref, p0_ref, obs_ref, part_ref, xs):
+    fill_table(loc_ref, t_ref)
     for w in range(8):
         xs[w] = tile_of(own_ref, 32 * w + (16 if w >= 4 else 0))
     fields = unpack_fields(own_ref[:, FIELDS : FIELDS + 16, :])
@@ -253,23 +242,24 @@
     apply_inner(h_ref, p0_ref, obs_ref, part_ref)
 
 
-def inner_blocks(reach, own, table):
+def inner_blocks(reach, loc_blocks, own):
     return pl.pallas_call(
         inner_kernel,
         out_shape=(
+            jax.ShapeDtypeStruct((N_TABLE, 256, 256), jnp.float32),
             jax.ShapeDtypeStruct((len(INNER), 256, 256), jnp.float32),
             FIELD,
             jax.ShapeDtypeStruct((8, 256), jnp.float32),
             FIELD,
         ),
         in_specs=[SM, VM, VM],
-        out_specs=(VM,) * 4,
+        out_specs=(VM,) * 5,
         scratch_shapes=[pltpu.VMEM((8, 256, 256), jnp.bfloat16)],
-        compiler_params=params(26),
+        compiler_params=params(12),
         cost_estimate=pl.CostEstimate(
             flops=100 * 2 * 256**3, bytes_accessed=20 * MIB, transcendentals=0
         ),
-    )(reach, own, table)
+    )(reach, loc_blocks, own)
 
 
 def set_sends(even, p, a_ref, b_ref):
@@ -350,7 +340,7 @@
             pltpu.VMEM((2, 16, 16, 128), jnp.bfloat16),
             pltpu.VMEM((2, 8, 256), jnp.float32),
         ],
-        compiler_params=params(22),
+        compiler_params=params(12),
     )(reach, own, a, b, table, part)
 
 
@@ -360,7 +350,7 @@
         out_shape=FIELD,
         in_specs=[VM] * 3,
         out_specs=VM,
-        compiler_params=params(18),
+        compiler_params=params(6),
         cost_estimate=pl.CostEstimate(
             flops=50 * 2 * 256**3, bytes_accessed=14 * MIB, transcendentals=0
         ),
@@ -381,7 +371,7 @@
         in_specs=[VM] * 4,
         out_specs=(VM,) * 3,
         scratch_shapes=[pltpu.VMEM((2, 8, 256), jnp.float32)],
-        compiler_params=params(10),
+        compiler_params=params(6),
     )(part, a, b, outer)
 
 
@@ -437,7 +427,10 @@
         sums.append(packed)
     high = jnp.where(lane < 32, sums[0][0], sums[1][0])
     low = jnp.where(lane < 96, sums[0][1], sums[1][1])
-    out = jnp.where(lane < 64, high, low)
+    out = jnp.where((lane & 7) == row, jnp.where(lane < 64, high, low), 0.0)
+    for shift in (4, 2, 1):
+        out = out + pltpu.roll(out, shift, 0)
+    out = out[0:1]
     for k in range(32):
         m_ref[k] = out
 
@@ -445,11 +438,11 @@
 def last_outer(part, a, b, outer, p0, p1, p2):
     return pl.pallas_call(
         last_kernel,
-        out_shape=(FIELD, jax.ShapeDtypeStruct((32, 8, 128), jnp.float32)),
+        out_shape=(FIELD, jax.ShapeDtypeStruct((32, 1, 128), jnp.float32)),
         in_specs=[VM] * 7,
         out_specs=(VM,) * 2,
         scratch_shapes=[pltpu.VMEM((2, 8, 256), jnp.float32)],
-        compiler_params=params(10),
+        compiler_params=params(6),
     )(part, a, b, outer, p0, p1, p2)
 
 
@@ -472,13 +465,15 @@
 
 def finish_kernel(m_ref, p0_ref, p1_ref, p2_ref, p3_ref, inc_ref, res_ref):
     member = lax.axis_index("member")
-    s = m_ref[0]
-    e = jnp.zeros((8, 128), jnp.float32)
-    for k in range(1, 32):
-        s, t = two_sum(s, m_ref[k])
-        e = e + t
+    sums = [(m_ref[k], jnp.zeros((1, 128), jnp.float32)) for k in range(32)]
+    while len(sums) > 1:
+        pairs = [(two_sum(x[0], y[0]), x[1] + y[1]) for x, y in zip(sums[::2], sums[1::2])]
+        sums = [(p[0], p[1] + e) for p, e in pairs]
+    s, e = sums[0]
     low = e + pltpu.roll(s, 64, 1)
-    moment = [(s[k : k + 1], low[k : k + 1]) for k in range(2 * ITERS)]
+    moment = [(s, low)]
+    for k in range(1, 2 * ITERS):
+        moment.append((pltpu.roll(s, 128 - k, 1), pltpu.roll(low, 128 - k, 1)))
     one = jnp.ones((1, 128), jnp.float32)
     residual, direction, increment = [one], [one], []
     norm_now = moment[0][0] + moment[0][1]
@@ -521,13 +516,12 @@
 
 
 def on_device(anomalies, loc_blocks, tile_reach, obs_var, innovations):
-    table = make_tables(loc_blocks)
     own = gather_members(pack(anomalies, tile_reach, obs_var, innovations))
     odd = lax.axis_index("space") % 2
     to_a = lax.dynamic_slice_in_dim(own, 128 * (1 - odd), PART, 1)
     to_b = lax.dynamic_slice_in_dim(own, 128 * odd, PART, 1)
     a, b = pair_swap(to_a, 0), pair_swap(to_b, 1)
-    inner, p0, obs, part = inner_blocks(tile_reach, own, table)
+    table, inner, p0, obs, part = inner_blocks(tile_reach, loc_blocks, own)
     outer, p1, to_a, to_b = outer_blocks(tile_reach, own, a, b, table, part)
     a, b = pair_swap(to_a, 0), pair_swap(to_b, 1)
     part = next_inner(p1, obs, inner)

time: 113 us -> 111 us (0.982)
  local copies, waits for them, and re-layouts: 2.95 us -> 0.97 us
    unnamed x12 -> x6, local copies, waits for them, and re-layouts: 2.88 us -> 0.89 us
    pallas_call x3 -> x2, Pallas kernels: 7.6 us -> 6.47 us  [the longest x1 5.01 us: inner_blocks(): pl.pallas_call(inner_kernel, out_shape=(jax.ShapeDtypeStruct((N_TABLE, 25...]
  transfers between devices with their start and end apart: 8 -> 8, of which waited for: 4 -> 4; matrix products, arithmetic and copies ran while one was open for 0% -> 0% of each run, Pallas kernels for 9% -> 8%
where the time goes in v5:
time: 111 us; the launch traced here: 110 us
  starting transfers between devices  44 us (40%)
  waiting for transfers between devices  32.8 us (30%)
  Pallas kernels  17.5 us (16%)
  blocking collectives  14.3 us (13%)
    all_to_all x1, waiting for transfers between devices, gather_members(): out = lax.all_to_all(both, 'member', 0, 0, axis_index_groups=groups)  28.7 us
    ppermute x6, starting transfers between devices, pair_swap(): return lax.ppermute(block, ('space', 'member'), route)  25.7 us
    all_to_all x1, blocking collectives, on_device(): m = lax.all_to_all(m, 'space', 0, 0)  14.3 us
    all_to_all x1, starting transfers between devices, gather_members(): out = lax.all_to_all(both, 'member', 0, 0, axis_index_groups=groups)  10 us
    ppermute x1, starting transfers between devices, gather_members(): other = lax.ppermute(chunk, 'member', [(k, k ^ 1) for k in range(m)])  8.28 us
    pallas_call x1, Pallas kernels, inner_blocks(): pl.pallas_call(inner_kernel, out_shape=(jax.ShapeDtypeStruct((N_TABLE, 25...  5.01 us
    pallas_call x2, Pallas kernels, next_inner(): pl.pallas_call(lambda p_ref, obs_ref, inner_ref, part_ref: apply_inner(in...  3.79 us
    pallas_call x1, Pallas kernels, outer_blocks(): pl.pallas_call(outer_kernel, out_shape=(jax.ShapeDtypeStruct((len(OUTER),...  2.6 us
  transfers between devices with their start and end apart: 8, of which 4 were waited for; matrix products, arithmetic and copies ran while one was open for 0% of the time, Pallas kernels for 8%

profile of v5, /device:TPU:1, one launch (start us, length us, event | category | flops | bytes accessed | tf_op | source)
XLA Modules:
  0.0 110.4 jit_solution(2860891476658798306)
XLA Ops:
  0.6 1.6 %shard_map.68.mine_ref = bf16[272,128]{1,0:T(8,128)(2,1)} custom-call(bf16[16,8,256]{2,1,0:T(8,128)(2,1)} %anomalies_hbm.1, s32[8]{0:T(128)} %reach_ref.3, f32[8,16]{1,0:T(8,128)} %obs_hbm.1, f32[2,8,16]{2,1,0:T(8,128)} %innovations_hbm.1), custom_call_target="tpu_custom_call" | custom-call | tf_op jit(solution)/shard_map/pallas_call | solution.py:82
  2.3 8.3 %collective-permute-start = (bf16[272,128]{1,0:T(8,128)(2,1)}, bf16[272,128]{1,0:T(8,128)(2,1)S(1)}, u32[]{:S(2)}, u32[]{:S(2)}) collective-permute-start(bf16[272,128]{1,0:T(8,128)(2,1)} %shard_map.68.mine_ref), channel_id=1, source_target_pairs={{0,1},{1,0},{2,3},{3,2},{4,5},{5,4},{6,7},{7,6},{8,9},{9,8},{10,11... | collective-permute-start | bytes 208904 | tf_op jit(solution)/shard_map/ppermute | solution.py:109
  10.6 2.0 %collective-permute-done.other_ref = bf16[272,128]{1,0:T(8,128)(2,1)S(1)} collective-permute-done((bf16[272,128]{1,0:T(8,128)(2,1)}, bf16[272,128]{1,0:T(8,128)(2,1)S(1)}, u32[]{:S(2)}, u32[]{:S(2)}) %collective-permute-start) | collective-permute-done | bytes 69664 | tf_op jit(solution)/shard_map/ppermute | solution.py:109
  12.5 0.9 copy-done
  13.4 1.2 %shard_map.69 = bf16[8,544,128]{2,1,0:T(8,128)(2,1)} custom-call(bf16[272,128]{1,0:T(8,128)(2,1)S(1)} %copy-done, bf16[272,128]{1,0:T(8,128)(2,1)S(1)} %collective-permute-done.other_ref), custom_call_target="tpu_custom_call" | custom-call | tf_op jit(solution)/shard_map/pallas_call | solution.py:110
  14.6 10.0 %all-to-all-start = ((bf16[8,544,128]{2,1,0:T(8,128)(2,1)}), bf16[8,544,128]{2,1,0:T(8,128)(2,1)S(1)}, u32[]{:S(2)}, u32[]{:S(2)}) async-start(bf16[8,544,128]{2,1,0:T(8,128)(2,1)} %shard_map.69), calls=%async_computation | async-start | bytes 2228224 | tf_op jit(solution)/shard_map/all_to_all | solution.py:118
  24.6 28.7 %all-to-all-done = bf16[8,544,128]{2,1,0:T(8,128)(2,1)S(1)} async-done(((bf16[8,544,128]{2,1,0:T(8,128)(2,1)}), bf16[8,544,128]{2,1,0:T(8,128)(2,1)S(1)}, u32[]{:S(2)}, u32[]{:S(2)}) %all-to-all-start) | async-done | bytes 1114144 | tf_op jit(solution)/shard_map/all_to_all | solution.py:118
  53.4 0.1 constant_dynamic-slice_fusion
  53.4 5.4 %collective-permute-start.2 = (bf16[16,144,128]{2,1,0:T(8,128)(2,1)S(1)}, bf16[16,144,128]{2,1,0:T(8,128)(2,1)S(1)}, u32[]{:S(2)}, u32[]{:S(2)}) collective-permute-start(bf16[16,144,128]{2,1,0:T(8,128)(2,1)S(1)} %get-tuple-element.30), channel_id=1, source_target_pairs={{0,497},{1,496},{2,499},{3,498},{4,501},{5,500},{6,503},{7,502},{8... | collective-permute-start | bytes 1769480 | tf_op jit(solution)/shard_map/ppermute | solution.py:42
  58.8 8.0 %collective-permute-start.1 = (bf16[16,144,128]{2,1,0:T(8,128)(2,1)S(1)}, bf16[16,144,128]{2,1,0:T(8,128)(2,1)S(1)}, u32[]{:S(2)}, u32[]{:S(2)}) collective-permute-start(bf16[16,144,128]{2,1,0:T(8,128)(2,1)S(1)} %get-tuple-element.31), channel_id=1, source_target_pairs={{0,16},{1,17},{2,18},{3,19},{4,20},{5,21},{6,22},{7,23},{8,24},{9,... | collective-permute-start | bytes 1769480 | tf_op jit(solution)/shard_map/ppermute | solution.py:42
  66.8 5.0 %shard_map.70 = (f32[26,256,256]{2,1,0:T(8,128)S(1)}, f32[52,256,256]{2,1,0:T(8,128)S(1)}, f32[2,8,256]{2,1,0:T(8,128)S(1)}, f32[8,256]{1,0:T(8,128)S(1)}, f32[2,8,256]{2,1,0:T(8,128)S(1)}) custom-call(s32[8]{0:T(128)S(1)} %copy-done.1, bf16[5,256,256]{2,1,0:T(8,128)(2,1)S(1)} %copy-done.2, bf16[16,272,128]{2,1,0:T(8,128)(2,1)S(1)} %bitcast.2), custom_call_target="tpu_custom_call" | custom-call | flops 3355443200 | bytes 20971520 | tf_op jit(solution)/shard_map/pallas_call | solution.py:246
  71.8 2.6 %shard_map.71 = (f32[20,256,256]{2,1,0:T(8,128)S(1)}, f32[2,8,256]{2,1,0:T(8,128)S(1)}, f32[2,4,256]{2,1,0:T(4,128)S(1)}, f32[2,4,256]{2,1,0:T(4,128)S(1)}) custom-call(s32[8]{0:T(128)S(1)} %copy-done.1, bf16[16,272,128]{2,1,0:T(8,128)(2,1)S(1)} %bitcast.3, bf16[16,144,128]{2,1,0:T(8,128)(2,1)S(1)} %collective-permute-done.1.a_ref, ...), custom_call_target="tpu_custom_call" | custom-call | tf_op jit(solution)/shard_map/pallas_call | solution.py:328
  74.4 2.5 %collective-permute-start.3 = (f32[2,4,256]{2,1,0:T(4,128)S(1)}, f32[2,4,256]{2,1,0:T(4,128)S(1)}, u32[]{:S(2)}, u32[]{:S(2)}) collective-permute-start(f32[2,4,256]{2,1,0:T(4,128)S(1)} %get-tuple-element.21), channel_id=1, source_target_pairs={{0,16},{1,17},{2,18},{3,19},{4,20},{5,21},{6,22},{7,23},{8,24},{9,... | collective-permute-start | bytes 24584 | tf_op jit(solution)/shard_map/ppermute | solution.py:42
  76.9 1.9 %collective-permute-start.4 = (f32[2,4,256]{2,1,0:T(4,128)S(1)}, f32[2,4,256]{2,1,0:T(4,128)S(1)}, u32[]{:S(2)}, u32[]{:S(2)}) collective-permute-start(f32[2,4,256]{2,1,0:T(4,128)S(1)} %get-tuple-element.22), channel_id=1, source_target_pairs={{0,497},{1,496},{2,499},{3,498},{4,501},{5,500},{6,503},{7,502},{8... | collective-permute-start | bytes 24584 | tf_op jit(solution)/shard_map/ppermute | solution.py:42
  78.9 1.9 %shard_map.72.part_ref = f32[2,8,256]{2,1,0:T(8,128)S(1)} custom-call(f32[2,8,256]{2,1,0:T(8,128)S(1)} %get-tuple-element.18.p_ref.p1_ref, f32[8,256]{1,0:T(8,128)S(1)} %get-tuple-element.19.obs_ref, f32[52,256,256]{2,1,0:T(8,128)S(1)} %get-tuple-element.20.inner_ref), custom_call_target="tpu_custom_call" | custom-call | flops 1677721600 | bytes 14680064 | tf_op jit(solution)/shard_map/pallas_call | solution.py:348
  80.8 1.1 %collective-permute-done.4.b_ref = f32[2,4,256]{2,1,0:T(4,128)S(1)} collective-permute-done((f32[2,4,256]{2,1,0:T(4,128)S(1)}, f32[2,4,256]{2,1,0:T(4,128)S(1)}, u32[]{:S(2)}, u32[]{:S(2)}) %collective-permute-start.4) | collective-permute-done | bytes 8224 | tf_op jit(solution)/shard_map/ppermute | solution.py:42
  81.9 0.9 shard_map.73
  82.8 5.8 %collective-permute-start.5 = (f32[2,4,256]{2,1,0:T(4,128)S(1)}, f32[2,4,256]{2,1,0:T(4,128)S(1)}, u32[]{:S(2)}, u32[]{:S(2)}) collective-permute-start(f32[2,4,256]{2,1,0:T(4,128)S(1)} %get-tuple-element.25), channel_id=1, source_target_pairs={{0,16},{1,17},{2,18},{3,19},{4,20},{5,21},{6,22},{7,23},{8,24},{9,... | collective-permute-start | bytes 24584 | tf_op jit(solution)/shard_map/ppermute | solution.py:42
  88.6 2.1 %collective-permute-start.6 = (f32[2,4,256]{2,1,0:T(4,128)S(1)}, f32[2,4,256]{2,1,0:T(4,128)S(1)}, u32[]{:S(2)}, u32[]{:S(2)}) collective-permute-start(f32[2,4,256]{2,1,0:T(4,128)S(1)} %get-tuple-element.26), channel_id=1, source_target_pairs={{0,497},{1,496},{2,499},{3,498},{4,501},{5,500},{6,503},{7,502},{8... | collective-permute-start | bytes 24584 | tf_op jit(solution)/shard_map/ppermute | solution.py:42
  90.7 1.9 %shard_map.74.part_ref = f32[2,8,256]{2,1,0:T(8,128)S(1)} custom-call(f32[2,8,256]{2,1,0:T(8,128)S(1)} %get-tuple-element.24.p_ref.p2_ref, f32[8,256]{1,0:T(8,128)S(1)} %get-tuple-element.19.obs_ref, f32[52,256,256]{2,1,0:T(8,128)S(1)} %get-tuple-element.20.inner_ref), custom_call_target="tpu_custom_call" | custom-call | flops 1677721600 | bytes 14680064 | tf_op jit(solution)/shard_map/pallas_call | solution.py:348
  92.6 1.0 collective-permute-done.6.b_ref
  93.6 1.5 %shard_map.75 = (f32[2,8,256]{2,1,0:T(8,128)S(1)}, f32[32,1,128]{2,1,0:T(1,128)S(1)}) custom-call(f32[2,8,256]{2,1,0:T(8,128)S(1)} %shard_map.74.part_ref, f32[2,4,256]{2,1,0:T(4,128)S(1)} %collective-permute-done.5.a_ref, f32[2,4,256]{2,1,0:T(4,128)S(1)} %collective-permute-done.6.b_ref, f32[20,256,256]{2,1,0:T(8,128)S(1)} %get-tuple-element.23.outer_ref, ...), custom_call_target="tpu_custom_call" | custom-call | tf_op jit(solution)/shard_map/pallas_call | solution.py:439
  95.0 14.3 %all_to_all.10.m_ref = f32[32,1,128]{2,1,0:T(1,128)S(1)} all-to-all(f32[32,1,128]{2,1,0:T(1,128)S(1)} %get-tuple-element.28), channel_id=1, replica_groups=mesh['space'=32,'member'=16] {'space'}, dimensions={0} | all-to-all | bytes 32768 | tf_op jit(solution)/shard_map/all_to_all | solution.py:532
  109.4 1.0 shard_map.76
  (9 shorter events, 0.0 us)
Async XLA Ops:
  0.6 66.2 %copy-start.1 = (s32[8]{0:T(128)S(1)}, s32[8]{0:T(128)}, u32[]{:S(2)}) copy-start(s32[8]{0:T(128)} %reach_ref.3) | copy-start | bytes 100
  2.3 10.3 %collective-permute-start = (bf16[272,128]{1,0:T(8,128)(2,1)}, bf16[272,128]{1,0:T(8,128)(2,1)S(1)}, u32[]{:S(2)}, u32[]{:S(2)}) collective-permute-start(bf16[272,128]{1,0:T(8,128)(2,1)} %shard_map.68.mine_ref), channel_id=1, source_target_pairs={{0,1},{1,0},{2,3},{3,2},{4,5},{5,4},{6,7},{7,6},{8,9},{9,8},{10,11... | collective-permute-start | bytes 208904 | tf_op jit(solution)/shard_map/ppermute | solution.py:109
  12.5 0.9 copy-start
  13.4 53.4 %copy-start.2 = (bf16[5,256,256]{2,1,0:T(8,128)(2,1)S(1)}, bf16[5,256,256]{2,1,0:T(8,128)(2,1)}, u32[]{:S(2)}) copy-start(bf16[5,256,256]{2,1,0:T(8,128)(2,1)} %loc_ref.1) | copy-start | bytes 1966084
  14.6 38.8 %all-to-all-start = ((bf16[8,544,128]{2,1,0:T(8,128)(2,1)}), bf16[8,544,128]{2,1,0:T(8,128)(2,1)S(1)}, u32[]{:S(2)}, u32[]{:S(2)}) async-start(bf16[8,544,128]{2,1,0:T(8,128)(2,1)} %shard_map.69), calls=%async_computation | async-start | bytes 2228224 | tf_op jit(solution)/shard_map/all_to_all | solution.py:118
  53.4 18.4 %collective-permute-start.2 = (bf16[16,144,128]{2,1,0:T(8,128)(2,1)S(1)}, bf16[16,144,128]{2,1,0:T(8,128)(2,1)S(1)}, u32[]{:S(2)}, u32[]{:S(2)}) collective-permute-start(bf16[16,144,128]{2,1,0:T(8,128)(2,1)S(1)} %get-tuple-element.30), channel_id=1, source_target_pairs={{0,497},{1,496},{2,499},{3,498},{4,501},{5,500},{6,503},{7,502},{8... | collective-permute-start | bytes 1769480 | tf_op jit(solution)/shard_map/ppermute | solution.py:42
  58.8 13.0 %collective-permute-start.1 = (bf16[16,144,128]{2,1,0:T(8,128)(2,1)S(1)}, bf16[16,144,128]{2,1,0:T(8,128)(2,1)S(1)}, u32[]{:S(2)}, u32[]{:S(2)}) collective-permute-start(bf16[16,144,128]{2,1,0:T(8,128)(2,1)S(1)} %get-tuple-element.31), channel_id=1, source_target_pairs={{0,16},{1,17},{2,18},{3,19},{4,20},{5,21},{6,22},{7,23},{8,24},{9,... | collective-permute-start | bytes 1769480 | tf_op jit(solution)/shard_map/ppermute | solution.py:42
  74.4 6.3 %collective-permute-start.3 = (f32[2,4,256]{2,1,0:T(4,128)S(1)}, f32[2,4,256]{2,1,0:T(4,128)S(1)}, u32[]{:S(2)}, u32[]{:S(2)}) collective-permute-start(f32[2,4,256]{2,1,0:T(4,128)S(1)} %get-tuple-element.21), channel_id=1, source_target_pairs={{0,16},{1,17},{2,18},{3,19},{4,20},{5,21},{6,22},{7,23},{8,24},{9,... | collective-permute-start | bytes 24584 | tf_op jit(solution)/shard_map/ppermute | solution.py:42
  76.9 5.0 %collective-permute-start.4 = (f32[2,4,256]{2,1,0:T(4,128)S(1)}, f32[2,4,256]{2,1,0:T(4,128)S(1)}, u32[]{:S(2)}, u32[]{:S(2)}) collective-permute-start(f32[2,4,256]{2,1,0:T(4,128)S(1)} %get-tuple-element.22), channel_id=1, source_target_pairs={{0,497},{1,496},{2,499},{3,498},{4,501},{5,500},{6,503},{7,502},{8... | collective-permute-start | bytes 24584 | tf_op jit(solution)/shard_map/ppermute | solution.py:42
  82.8 9.8 %collective-permute-start.5 = (f32[2,4,256]{2,1,0:T(4,128)S(1)}, f32[2,4,256]{2,1,0:T(4,128)S(1)}, u32[]{:S(2)}, u32[]{:S(2)}) collective-permute-start(f32[2,4,256]{2,1,0:T(4,128)S(1)} %get-tuple-element.25), channel_id=1, source_target_pairs={{0,16},{1,17},{2,18},{3,19},{4,20},{5,21},{6,22},{7,23},{8,24},{9,... | collective-permute-start | bytes 24584 | tf_op jit(solution)/shard_map/ppermute | solution.py:42
  88.6 5.0 %collective-permute-start.6 = (f32[2,4,256]{2,1,0:T(4,128)S(1)}, f32[2,4,256]{2,1,0:T(4,128)S(1)}, u32[]{:S(2)}, u32[]{:S(2)}) collective-permute-start(f32[2,4,256]{2,1,0:T(4,128)S(1)} %get-tuple-element.26), channel_id=1, source_target_pairs={{0,497},{1,496},{2,499},{3,498},{4,501},{5,500},{6,503},{7,502},{8... | collective-permute-start | bytes 24584 | tf_op jit(solution)/shard_map/ppermute | solution.py:42

commit v6 on v5

--- a/solution.py
+++ b/solution.py
@@ -95,25 +95,46 @@
     )(anomalies, tile_reach, obs_var, innovations)
 
 
-def spread_kernel(mine_ref, other_ref, out_ref):
-    y = lax.axis_index("member") % 2 == 0
-    low = jnp.where(y, mine_ref[...], other_ref[...])
-    high = jnp.where(y, other_ref[...], mine_ref[...])
-    for k in range(8):
-        out_ref[k, :CHUNK] = low
-        out_ref[k, CHUNK:] = high
+def send_copies(source, target, half, sems):
+    rows = pl.ds(pl.multiple_of(half * CHUNK, 16), CHUNK)
+    moves = [pltpu.make_async_copy(source, target.at[k, rows], sems.at[k]) for k in range(8)]
+    for move in moves:
+        move.start()
+    for move in moves:
+        move.wait()
+
+
+def own_half_kernel(chunk_ref, out_ref, sems):
+    send_copies(chunk_ref, out_ref, lax.axis_index("member") % 2, sems)
+
+
+def other_half_kernel(chunk_ref, same_ref, out_ref, sems):
+    send_copies(chunk_ref, out_ref, 1 - lax.axis_index("member") % 2, sems)
 
 
 def gather_members(chunk):
-    n, m = lax.axis_size("space"), lax.axis_size("member")
+    m = lax.axis_size("member")
     other = lax.ppermute(chunk, "member", [(k, k ^ 1) for k in range(m)])
+    shape = jax.ShapeDtypeStruct((8, 2 * CHUNK, 128), jnp.bfloat16)
+    scratch = [pltpu.SemaphoreType.DMA((8,))]
+    half = pl.pallas_call(
+        own_half_kernel,
+        out_shape=shape,
+        in_specs=[HBM],
+        out_specs=HBM,
+        scratch_shapes=scratch,
+        compiler_params=params(4),
+        cost_estimate=pl.CostEstimate(flops=0, bytes_accessed=2 * MIB, transcendentals=0),
+    )(chunk)
     both = pl.pallas_call(
-        spread_kernel,
-        out_shape=jax.ShapeDtypeStruct((8, 2 * CHUNK, 128), jnp.bfloat16),
-        in_specs=[VM, VM],
-        out_specs=VM,
-        compiler_params=params(8),
-    )(chunk, other)
+        other_half_kernel,
+        out_shape=shape,
+        in_specs=[VM, HBM],
+        out_specs=HBM,
+        scratch_shapes=scratch,
+        input_output_aliases={1: 0},
+        compiler_params=params(4),
+    )(other, half)
     groups = [[2 * z + y for z in range(8)] for y in range(2)]
     out = lax.all_to_all(both, "member", 0, 0, axis_index_groups=groups)
     return out.reshape(16, CHUNK, 128)
@@ -223,7 +244,9 @@
         y_ref[f, w : w + 1, :] = total + part_ref[f, w : w + 1, :]
 
 
-def inner_kernel(reach_ref, loc_ref, own_ref, t_ref, h_ref, p0_ref, obs_ref, part_ref, xs):
+def inner_kernel(
+    reach_ref, loc_ref, own_ref, t_ref, h_ref, xt_ref, p0_ref, obs_ref, part_ref, xs
+):
     fill_table(loc_ref, t_ref)
     for w in range(8):
         xs[w] = tile_of(own_ref, 32 * w + (16 if w >= 4 else 0))
@@ -233,6 +256,7 @@
     obs_ref[...] = fields[2]
     for w in range(8):
         rows = xs[w].T
+        xt_ref[w] = rows
         for shift in range(-W, W + 1):
             if (w, shift) not in INNER:
                 continue
@@ -248,12 +272,13 @@
         out_shape=(
             jax.ShapeDtypeStruct((N_TABLE, 256, 256), jnp.float32),
             jax.ShapeDtypeStruct((len(INNER), 256, 256), jnp.float32),
+            jax.ShapeDtypeStruct((8, 256, 256), jnp.bfloat16),
             FIELD,
             jax.ShapeDtypeStruct((8, 256), jnp.float32),
             FIELD,
         ),
         in_specs=[SM, VM, VM],
-        out_specs=(VM,) * 5,
+        out_specs=(VM,) * 6,
         scratch_shapes=[pltpu.VMEM((8, 256, 256), jnp.bfloat16)],
         compiler_params=params(12),
         cost_estimate=pl.CostEstimate(
@@ -276,17 +301,15 @@
 
 
 def outer_kernel(
-    reach_ref, own_ref, a_ref, b_ref, t_ref, part_ref,
+    reach_ref, xt_ref, a_ref, b_ref, t_ref, part_ref,
     outer_ref, y_ref, send_a_ref, send_b_ref,
     xs, lines, halo,
 ):
     even = lax.axis_index("space") % 2 == 0
     a_low, b_low = jnp.where(even, 0, 16), jnp.where(even, 16, 0)
-    for w in range(8):
-        xs[w + W] = tile_of(own_ref, 32 * w + (16 if w >= 4 else 0))
     for w in range(W):
-        xs[jnp.where(even, 12, 0) + w] = tile_of(a_ref, pl.multiple_of(a_low + 32 * w, 16))
-        xs[jnp.where(even, 0, 12) + w] = tile_of(b_ref, pl.multiple_of(b_low + 32 * w, 16))
+        xs[jnp.where(even, W, 0) + w] = tile_of(a_ref, pl.multiple_of(a_low + 32 * w, 16))
+        xs[jnp.where(even, 0, W) + w] = tile_of(b_ref, pl.multiple_of(b_low + 32 * w, 16))
     a_at = pl.multiple_of(jnp.where(even, 128, 0), 16)
     b_at = pl.multiple_of(jnp.where(even, 0, 128), 16)
     lines[0] = a_ref[:, pl.ds(a_at, 16), :]
@@ -313,18 +336,20 @@
         halo,
     )
     for w in range(8):
-        rows = xs[w + W].T
+        rows = xt_ref[w]
         for shift in range(-W, W + 1):
             if (w, shift) not in OUTER:
                 continue
-            entry = table_entry(shift, reach[w], reach[w + shift])
-            covariance = jnp.dot(rows, xs[w + shift + W], preferred_element_type=jnp.float32)
+            other = w + shift
+            entry = table_entry(shift, reach[w], reach[other])
+            tile = xs[other + W if other < 0 else other - W]
+            covariance = jnp.dot(rows, tile, preferred_element_type=jnp.float32)
             outer_ref[OUTER.index((w, shift))] = covariance * t_ref[entry]
     apply_outer(outer_ref, part_ref, halo, y_ref)
     set_sends(even, y_ref, send_a_ref, send_b_ref)
 
 
-def outer_blocks(reach, own, a, b, table, part):
+def outer_blocks(reach, xt, a, b, table, part):
     return pl.pallas_call(
         outer_kernel,
         out_shape=(
@@ -336,12 +361,12 @@
         in_specs=[SM] + [VM] * 5,
         out_specs=(VM,) * 4,
         scratch_shapes=[
-            pltpu.VMEM((16, 256, 256), jnp.bfloat16),
+            pltpu.VMEM((8, 256, 256), jnp.bfloat16),
             pltpu.VMEM((2, 16, 16, 128), jnp.bfloat16),
             pltpu.VMEM((2, 8, 256), jnp.float32),
         ],
         compiler_params=params(12),
-    )(reach, own, a, b, table, part)
+    )(reach, xt, a, b, table, part)
 
 
 def next_inner(p, obs, inner):
@@ -517,12 +542,14 @@
 
 def on_device(anomalies, loc_blocks, tile_reach, obs_var, innovations):
     own = gather_members(pack(anomalies, tile_reach, obs_var, innovations))
+    own, loc_blocks, tile_reach = lax.optimization_barrier((own, loc_blocks, tile_reach))
     odd = lax.axis_index("space") % 2
     to_a = lax.dynamic_slice_in_dim(own, 128 * (1 - odd), PART, 1)
     to_b = lax.dynamic_slice_in_dim(own, 128 * odd, PART, 1)
-    a, b = pair_swap(to_a, 0), pair_swap(to_b, 1)
-    table, inner, p0, obs, part = inner_blocks(tile_reach, loc_blocks, own)
-    outer, p1, to_a, to_b = outer_blocks(tile_reach, own, a, b, table, part)
+    b = pair_swap(to_b, 1)
+    a = pair_swap(to_a, 0)
+    table, inner, xt, p0, obs, part = inner_blocks(tile_reach, loc_blocks, own)
+    outer, p1, to_a, to_b = outer_blocks(tile_reach, xt, a, b, table, part)
     a, b = pair_swap(to_a, 0), pair_swap(to_b, 1)
     part = next_inner(p1, obs, inner)
     p2, to_a, to_b = next_outer(part, a, b, outer)

time: 111 us -> 109 us (0.982)
  waiting for transfers between devices: 32.8 us -> 31 us
    ppermute x1, waiting for transfers between devices: 1.97 us -> 0.18 us  [gather_members(): other = lax.ppermute(chunk, 'member', [(k, k ^ 1) for k in range(m)])]
  transfers between devices with their start and end apart: 8 -> 8, of which waited for: 4 -> 4; matrix products, arithmetic and copies ran while one was open for 0% -> 0% of each run, Pallas kernels for 8% -> 9%
where the time goes in v6:
time: 109 us
  starting transfers between devices  44.1 us (40%)
  waiting for transfers between devices  31 us (28%)
  Pallas kernels  17.8 us (16%)
  blocking collectives  14.3 us (13%)
    all_to_all x1, waiting for transfers between devices, gather_members(): out = lax.all_to_all(both, 'member', 0, 0, axis_index_groups=groups)  28.7 us
    ppermute x6, starting transfers between devices, pair_swap(): return lax.ppermute(block, ('space', 'member'), route)  25.8 us
    all_to_all x1, blocking collectives, on_device(): m = lax.all_to_all(m, 'space', 0, 0)  14.3 us
    all_to_all x1, starting transfers between devices, gather_members(): out = lax.all_to_all(both, 'member', 0, 0, axis_index_groups=groups)  10 us
    ppermute x1, starting transfers between devices, gather_members(): other = lax.ppermute(chunk, 'member', [(k, k ^ 1) for k in range(m)])  8.28 us
    pallas_call x1, Pallas kernels, inner_blocks(): pl.pallas_call(inner_kernel, out_shape=(jax.ShapeDtypeStruct((N_TABLE, 25...  5.07 us
    pallas_call x2, Pallas kernels, next_inner(): pl.pallas_call(lambda p_ref, obs_ref, inner_ref, part_ref: apply_inner(in...  3.79 us
    pallas_call x1, Pallas kernels, outer_blocks(): pl.pallas_call(outer_kernel, out_shape=(jax.ShapeDtypeStruct((len(OUTER),...  2.24 us
  transfers between devices with their start and end apart: 8, of which 4 were waited for; matrix products, arithmetic and copies ran while one was open for 0% of the time, Pallas kernels for 9%

profile of v6, /device:TPU:1, one launch (start us, length us, event | category | flops | bytes accessed | tf_op | source)
XLA Modules:
  0.0 109.0 jit_solution(5852497852958201290)
XLA Ops:
  0.6 1.6 %shard_map.68.chunk_ref = bf16[272,128]{1,0:T(8,128)(2,1)} custom-call(bf16[16,8,256]{2,1,0:T(8,128)(2,1)} %anomalies_hbm.1, s32[8]{0:T(128)} %reach_ref.1, f32[8,16]{1,0:T(8,128)} %obs_hbm.1, f32[2,8,16]{2,1,0:T(8,128)} %innovations_hbm.1), custom_call_target="tpu_custom_call" | custom-call | tf_op jit(solution)/shard_map/pallas_call | solution.py:82
  2.3 8.3 %collective-permute-start = (bf16[272,128]{1,0:T(8,128)(2,1)}, bf16[272,128]{1,0:T(8,128)(2,1)S(1)}, u32[]{:S(2)}, u32[]{:S(2)}) collective-permute-start(bf16[272,128]{1,0:T(8,128)(2,1)} %shard_map.68.chunk_ref), channel_id=1, source_target_pairs={{0,1},{1,0},{2,3},{3,2},{4,5},{5,4},{6,7},{7,6},{8,9},{9,8},{10,11... | collective-permute-start | bytes 208904 | tf_op jit(solution)/shard_map/ppermute | solution.py:117
  10.6 0.9 copy-done
  11.4 0.9 shard_map.69.same_ref
  12.3 0.2 collective-permute-done.chunk_ref
  12.5 0.9 shard_map.70
  13.4 10.0 %all-to-all-start = ((bf16[8,544,128]{2,1,0:T(8,128)(2,1)}), bf16[8,544,128]{2,1,0:T(8,128)(2,1)S(1)}, u32[]{:S(2)}, u32[]{:S(2)}) async-start(bf16[8,544,128]{2,1,0:T(8,128)(2,1)} %shard_map.70), calls=%async_computation | async-start | bytes 2228224 | tf_op jit(solution)/shard_map/all_to_all | solution.py:139
  23.4 28.7 %all-to-all-done = bf16[8,544,128]{2,1,0:T(8,128)(2,1)S(1)} async-done(((bf16[8,544,128]{2,1,0:T(8,128)(2,1)}), bf16[8,544,128]{2,1,0:T(8,128)(2,1)S(1)}, u32[]{:S(2)}, u32[]{:S(2)}) %all-to-all-start) | async-done | bytes 1114144 | tf_op jit(solution)/shard_map/all_to_all | solution.py:139
  52.3 5.5 %collective-permute-start.2 = (bf16[16,144,128]{2,1,0:T(8,128)(2,1)S(1)}, bf16[16,144,128]{2,1,0:T(8,128)(2,1)S(1)}, u32[]{:S(2)}, u32[]{:S(2)}) collective-permute-start(bf16[16,144,128]{2,1,0:T(8,128)(2,1)S(1)} %get-tuple-element.38), channel_id=1, source_target_pairs={{0,497},{1,496},{2,499},{3,498},{4,501},{5,500},{6,503},{7,502},{8... | collective-permute-start | bytes 1769480 | tf_op jit(solution)/shard_map/ppermute | solution.py:42
  57.8 8.0 %collective-permute-start.1 = (bf16[16,144,128]{2,1,0:T(8,128)(2,1)S(1)}, bf16[16,144,128]{2,1,0:T(8,128)(2,1)S(1)}, u32[]{:S(2)}, u32[]{:S(2)}) collective-permute-start(bf16[16,144,128]{2,1,0:T(8,128)(2,1)S(1)} %get-tuple-element.39), channel_id=1, source_target_pairs={{0,16},{1,17},{2,18},{3,19},{4,20},{5,21},{6,22},{7,23},{8,24},{9,... | collective-permute-start | bytes 1769480 | tf_op jit(solution)/shard_map/ppermute | solution.py:42
  65.8 5.1 %shard_map.71 = (f32[26,256,256]{2,1,0:T(8,128)S(1)}, f32[52,256,256]{2,1,0:T(8,128)S(1)}, bf16[8,256,256]{2,1,0:T(8,128)(2,1)S(1)}, f32[2,8,256]{2,1,0:T(8,128)...) custom-call(s32[8]{0:T(128)S(1)} %copy-done.1, bf16[5,256,256]{2,1,0:T(8,128)(2,1)S(1)} %copy-done.2, ...), custom_call_target="tpu_custom_call" | custom-call | flops 3355443200 | bytes 20971520 | tf_op jit(solution)/shard_map/pallas_call | solution.py:270
  70.9 2.2 %shard_map.72 = (f32[20,256,256]{2,1,0:T(8,128)S(1)}, f32[2,8,256]{2,1,0:T(8,128)S(1)}, f32[2,4,256]{2,1,0:T(4,128)S(1)}, f32[2,4,256]{2,1,0:T(4,128)S(1)}) custom-call(s32[8]{0:T(128)S(1)} %copy-done.1, bf16[8,256,256]{2,1,0:T(8,128)(2,1)S(1)} %get-tuple-element.23.xt_ref, bf16[16,144,128]{2,1,0:T(8,128)(2,1)S(1)} %collective-permute-done.1.a_ref, ...), custom_call_target="tpu_custom_call" | custom-call | tf_op jit(solution)/shard_map/pallas_call | solution.py:353
  73.1 2.4 %collective-permute-start.3 = (f32[2,4,256]{2,1,0:T(4,128)S(1)}, f32[2,4,256]{2,1,0:T(4,128)S(1)}, u32[]{:S(2)}, u32[]{:S(2)}) collective-permute-start(f32[2,4,256]{2,1,0:T(4,128)S(1)} %get-tuple-element.29), channel_id=1, source_target_pairs={{0,16},{1,17},{2,18},{3,19},{4,20},{5,21},{6,22},{7,23},{8,24},{9,... | collective-permute-start | bytes 24584 | tf_op jit(solution)/shard_map/ppermute | solution.py:42
  75.5 1.9 %collective-permute-start.4 = (f32[2,4,256]{2,1,0:T(4,128)S(1)}, f32[2,4,256]{2,1,0:T(4,128)S(1)}, u32[]{:S(2)}, u32[]{:S(2)}) collective-permute-start(f32[2,4,256]{2,1,0:T(4,128)S(1)} %get-tuple-element.30), channel_id=1, source_target_pairs={{0,497},{1,496},{2,499},{3,498},{4,501},{5,500},{6,503},{7,502},{8... | collective-permute-start | bytes 24584 | tf_op jit(solution)/shard_map/ppermute | solution.py:42
  77.5 1.9 %shard_map.73.part_ref = f32[2,8,256]{2,1,0:T(8,128)S(1)} custom-call(f32[2,8,256]{2,1,0:T(8,128)S(1)} %get-tuple-element.26.p_ref.p1_ref, f32[8,256]{1,0:T(8,128)S(1)} %get-tuple-element.27.obs_ref, f32[52,256,256]{2,1,0:T(8,128)S(1)} %get-tuple-element.28.inner_ref), custom_call_target="tpu_custom_call" | custom-call | flops 1677721600 | bytes 14680064 | tf_op jit(solution)/shard_map/pallas_call | solution.py:373
  79.4 1.1 %collective-permute-done.4.b_ref = f32[2,4,256]{2,1,0:T(4,128)S(1)} collective-permute-done((f32[2,4,256]{2,1,0:T(4,128)S(1)}, f32[2,4,256]{2,1,0:T(4,128)S(1)}, u32[]{:S(2)}, u32[]{:S(2)}) %collective-permute-start.4) | collective-permute-done | bytes 8224 | tf_op jit(solution)/shard_map/ppermute | solution.py:42
  80.5 0.9 shard_map.74
  81.4 5.8 %collective-permute-start.5 = (f32[2,4,256]{2,1,0:T(4,128)S(1)}, f32[2,4,256]{2,1,0:T(4,128)S(1)}, u32[]{:S(2)}, u32[]{:S(2)}) collective-permute-start(f32[2,4,256]{2,1,0:T(4,128)S(1)} %get-tuple-element.33), channel_id=1, source_target_pairs={{0,16},{1,17},{2,18},{3,19},{4,20},{5,21},{6,22},{7,23},{8,24},{9,... | collective-permute-start | bytes 24584 | tf_op jit(solution)/shard_map/ppermute | solution.py:42
  87.2 2.1 %collective-permute-start.6 = (f32[2,4,256]{2,1,0:T(4,128)S(1)}, f32[2,4,256]{2,1,0:T(4,128)S(1)}, u32[]{:S(2)}, u32[]{:S(2)}) collective-permute-start(f32[2,4,256]{2,1,0:T(4,128)S(1)} %get-tuple-element.34), channel_id=1, source_target_pairs={{0,497},{1,496},{2,499},{3,498},{4,501},{5,500},{6,503},{7,502},{8... | collective-permute-start | bytes 24584 | tf_op jit(solution)/shard_map/ppermute | solution.py:42
  89.3 1.9 %shard_map.75.part_ref = f32[2,8,256]{2,1,0:T(8,128)S(1)} custom-call(f32[2,8,256]{2,1,0:T(8,128)S(1)} %get-tuple-element.32.p_ref.p2_ref, f32[8,256]{1,0:T(8,128)S(1)} %get-tuple-element.27.obs_ref, f32[52,256,256]{2,1,0:T(8,128)S(1)} %get-tuple-element.28.inner_ref), custom_call_target="tpu_custom_call" | custom-call | flops 1677721600 | bytes 14680064 | tf_op jit(solution)/shard_map/pallas_call | solution.py:373
  91.2 1.0 collective-permute-done.6.b_ref
  92.2 1.5 %shard_map.76 = (f32[2,8,256]{2,1,0:T(8,128)S(1)}, f32[32,1,128]{2,1,0:T(1,128)S(1)}) custom-call(f32[2,8,256]{2,1,0:T(8,128)S(1)} %shard_map.75.part_ref, f32[2,4,256]{2,1,0:T(4,128)S(1)} %collective-permute-done.5.a_ref, f32[2,4,256]{2,1,0:T(4,128)S(1)} %collective-permute-done.6.b_ref, f32[20,256,256]{2,1,0:T(8,128)S(1)} %get-tuple-element.31.outer_ref, ...), custom_call_target="tpu_custom_call" | custom-call | tf_op jit(solution)/shard_map/pallas_call | solution.py:464
  93.7 14.3 %all_to_all.10.m_ref = f32[32,1,128]{2,1,0:T(1,128)S(1)} all-to-all(f32[32,1,128]{2,1,0:T(1,128)S(1)} %get-tuple-element.36), channel_id=1, replica_groups=mesh['space'=32,'member'=16] {'space'}, dimensions={0} | all-to-all | bytes 32768 | tf_op jit(solution)/shard_map/all_to_all | solution.py:559
  108.0 1.0 shard_map.77
  (10 shorter events, 0.1 us)
Async XLA Ops:
  2.3 10.3 %collective-permute-start = (bf16[272,128]{1,0:T(8,128)(2,1)}, bf16[272,128]{1,0:T(8,128)(2,1)S(1)}, u32[]{:S(2)}, u32[]{:S(2)}) collective-permute-start(bf16[272,128]{1,0:T(8,128)(2,1)} %shard_map.68.chunk_ref), channel_id=1, source_target_pairs={{0,1},{1,0},{2,3},{3,2},{4,5},{5,4},{6,7},{7,6},{8,9},{9,8},{10,11... | collective-permute-start | bytes 208904 | tf_op jit(solution)/shard_map/ppermute | solution.py:117
  10.5 0.9 copy-start
  13.4 38.8 %all-to-all-start = ((bf16[8,544,128]{2,1,0:T(8,128)(2,1)}), bf16[8,544,128]{2,1,0:T(8,128)(2,1)S(1)}, u32[]{:S(2)}, u32[]{:S(2)}) async-start(bf16[8,544,128]{2,1,0:T(8,128)(2,1)} %shard_map.70), calls=%async_computation | async-start | bytes 2228224 | tf_op jit(solution)/shard_map/all_to_all | solution.py:139
  52.2 13.6 %copy-start.1 = (s32[8]{0:T(128)S(1)}, s32[8]{0:T(128)}, u32[]{:S(2)}) copy-start(s32[8]{0:T(128)} %reach_ref.1) | copy-start | bytes 100
  52.2 13.6 %copy-start.2 = (bf16[5,256,256]{2,1,0:T(8,128)(2,1)S(1)}, bf16[5,256,256]{2,1,0:T(8,128)(2,1)}, u32[]{:S(2)}) copy-start(bf16[5,256,256]{2,1,0:T(8,128)(2,1)} %loc_ref) | copy-start | bytes 1966084
  52.3 18.6 %collective-permute-start.2 = (bf16[16,144,128]{2,1,0:T(8,128)(2,1)S(1)}, bf16[16,144,128]{2,1,0:T(8,128)(2,1)S(1)}, u32[]{:S(2)}, u32[]{:S(2)}) collective-permute-start(bf16[16,144,128]{2,1,0:T(8,128)(2,1)S(1)} %get-tuple-element.38), channel_id=1, source_target_pairs={{0,497},{1,496},{2,499},{3,498},{4,501},{5,500},{6,503},{7,502},{8... | collective-permute-start | bytes 1769480 | tf_op jit(solution)/shard_map/ppermute | solution.py:42
  57.8 13.1 %collective-permute-start.1 = (bf16[16,144,128]{2,1,0:T(8,128)(2,1)S(1)}, bf16[16,144,128]{2,1,0:T(8,128)(2,1)S(1)}, u32[]{:S(2)}, u32[]{:S(2)}) collective-permute-start(bf16[16,144,128]{2,1,0:T(8,128)(2,1)S(1)} %get-tuple-element.39), channel_id=1, source_target_pairs={{0,16},{1,17},{2,18},{3,19},{4,20},{5,21},{6,22},{7,23},{8,24},{9,... | collective-permute-start | bytes 1769480 | tf_op jit(solution)/shard_map/ppermute | solution.py:42
  73.1 6.3 %collective-permute-start.3 = (f32[2,4,256]{2,1,0:T(4,128)S(1)}, f32[2,4,256]{2,1,0:T(4,128)S(1)}, u32[]{:S(2)}, u32[]{:S(2)}) collective-permute-start(f32[2,4,256]{2,1,0:T(4,128)S(1)} %get-tuple-element.29), channel_id=1, source_target_pairs={{0,16},{1,17},{2,18},{3,19},{4,20},{5,21},{6,22},{7,23},{8,24},{9,... | collective-permute-start | bytes 24584 | tf_op jit(solution)/shard_map/ppermute | solution.py:42
  75.5 5.0 %collective-permute-start.4 = (f32[2,4,256]{2,1,0:T(4,128)S(1)}, f32[2,4,256]{2,1,0:T(4,128)S(1)}, u32[]{:S(2)}, u32[]{:S(2)}) collective-permute-start(f32[2,4,256]{2,1,0:T(4,128)S(1)} %get-tuple-element.30), channel_id=1, source_target_pairs={{0,497},{1,496},{2,499},{3,498},{4,501},{5,500},{6,503},{7,502},{8... | collective-permute-start | bytes 24584 | tf_op jit(solution)/shard_map/ppermute | solution.py:42
  81.4 9.9 %collective-permute-start.5 = (f32[2,4,256]{2,1,0:T(4,128)S(1)}, f32[2,4,256]{2,1,0:T(4,128)S(1)}, u32[]{:S(2)}, u32[]{:S(2)}) collective-permute-start(f32[2,4,256]{2,1,0:T(4,128)S(1)} %get-tuple-element.33), channel_id=1, source_target_pairs={{0,16},{1,17},{2,18},{3,19},{4,20},{5,21},{6,22},{7,23},{8,24},{9,... | collective-permute-start | bytes 24584 | tf_op jit(solution)/shard_map/ppermute | solution.py:42
  87.2 5.0 %collective-permute-start.6 = (f32[2,4,256]{2,1,0:T(4,128)S(1)}, f32[2,4,256]{2,1,0:T(4,128)S(1)}, u32[]{:S(2)}, u32[]{:S(2)}) collective-permute-start(f32[2,4,256]{2,1,0:T(4,128)S(1)} %get-tuple-element.34), channel_id=1, source_target_pairs={{0,497},{1,496},{2,499},{3,498},{4,501},{5,500},{6,503},{7,502},{8... | collective-permute-start | bytes 24584 | tf_op jit(solution)/shard_map/ppermute | solution.py:42

commit v7 on v6

--- a/solution.py
+++ b/solution.py
@@ -382,7 +382,7 @@
     )(p, obs, inner)
 
 
-def next_kernel(part_ref, a_ref, b_ref, outer_ref, y_ref, send_a_ref, send_b_ref, halo):
+def next_kernel(part_ref, b_ref, a_ref, outer_ref, y_ref, send_a_ref, send_b_ref, halo):
     even = lax.axis_index("space") % 2 == 0
     fill_halo(even, a_ref, b_ref, halo)
     apply_outer(outer_ref, part_ref, halo, y_ref)
@@ -397,7 +397,7 @@
         out_specs=(VM,) * 3,
         scratch_shapes=[pltpu.VMEM((2, 8, 256), jnp.float32)],
         compiler_params=params(6),
-    )(part, a, b, outer)
+    )(part, b, a, outer)
 
 
 def two_sum(a, b):
@@ -431,7 +431,7 @@
     return p, e + (x[0] * y[1] + x[1] * y[0])
 
 
-def last_kernel(part_ref, a_ref, b_ref, outer_ref, p0_ref, p1_ref, p2_ref, y_ref, m_ref, halo):
+def last_kernel(part_ref, b_ref, a_ref, outer_ref, p0_ref, p1_ref, p2_ref, y_ref, m_ref, halo):
     even = lax.axis_index("space") % 2 == 0
     fill_halo(even, a_ref, b_ref, halo)
     apply_outer(outer_ref, part_ref, halo, y_ref)
@@ -468,7 +468,7 @@
         out_specs=(VM,) * 2,
         scratch_shapes=[pltpu.VMEM((2, 8, 256), jnp.float32)],
         compiler_params=params(6),
-    )(part, a, b, outer, p0, p1, p2)
+    )(part, b, a, outer, p0, p1, p2)
 
 
 def square_dot(poly, moment):

time: 109 us -> 107 us (0.982)
  blocking collectives: 14.3 us -> 10.1 us
  starting transfers between devices: 44.1 us -> 47.7 us
  waiting for transfers between devices: 31 us -> 28.9 us
    all_to_all x1, blocking collectives: 14.3 us -> 10.1 us  [on_device(): m = lax.all_to_all(m, 'space', 0, 0)]
    ppermute x6, starting transfers between devices: 25.8 us -> 29.4 us  [pair_swap(): return lax.ppermute(block, ('space', 'member'), route)]
    ppermute x6, waiting for transfers between devices: 2.1 us -> 0.02 us  [pair_swap(): return lax.ppermute(block, ('space', 'member'), route)]
  transfers between devices with their start and end apart: 8 -> 8, of which waited for: 4 -> 2; matrix products, arithmetic and copies ran while one was open for 0% -> 0% of each run, Pallas kernels for 9% -> 9%
where the time goes in v7:
time: 107 us; the launch traced here: 106 us
  starting transfers between devices  47.7 us (45%)
  waiting for transfers between devices  28.9 us (27%)
  Pallas kernels  17.8 us (17%)
  blocking collectives  10.1 us (9%)
    ppermute x6, starting transfers between devices, pair_swap(): return lax.ppermute(block, ('space', 'member'), route)  29.4 us
    all_to_all x1, waiting for transfers between devices, gather_members(): out = lax.all_to_all(both, 'member', 0, 0, axis_index_groups=groups)  28.7 us
    all_to_all x1, blocking collectives, on_device(): m = lax.all_to_all(m, 'space', 0, 0)  10.1 us
    all_to_all x1, starting transfers between devices, gather_members(): out = lax.all_to_all(both, 'member', 0, 0, axis_index_groups=groups)  10 us
    ppermute x1, starting transfers between devices, gather_members(): other = lax.ppermute(chunk, 'member', [(k, k ^ 1) for k in range(m)])  8.28 us
    pallas_call x1, Pallas kernels, inner_blocks(): pl.pallas_call(inner_kernel, out_shape=(jax.ShapeDtypeStruct((N_TABLE, 25...  5.07 us
    pallas_call x2, Pallas kernels, next_inner(): pl.pallas_call(lambda p_ref, obs_ref, inner_ref, part_ref: apply_inner(in...  3.79 us
    pallas_call x1, Pallas kernels, outer_blocks(): pl.pallas_call(outer_kernel, out_shape=(jax.ShapeDtypeStruct((len(OUTER),...  2.24 us
  transfers between devices with their start and end apart: 8, of which 2 were waited for; matrix products, arithmetic and copies ran while one was open for 0% of the time, Pallas kernels for 9%

profile of v7, /device:TPU:1, one launch (start us, length us, event | category | flops | bytes accessed | tf_op | source)
XLA Modules:
  0.0 106.3 jit_solution(1018928418997334661)
XLA Ops:
  0.6 1.6 %shard_map.68.chunk_ref = bf16[272,128]{1,0:T(8,128)(2,1)} custom-call(bf16[16,8,256]{2,1,0:T(8,128)(2,1)} %anomalies_hbm.1, s32[8]{0:T(128)} %reach_ref.1, f32[8,16]{1,0:T(8,128)} %obs_hbm.1, f32[2,8,16]{2,1,0:T(8,128)} %innovations_hbm.1), custom_call_target="tpu_custom_call" | custom-call | tf_op jit(solution)/shard_map/pallas_call | solution.py:82
  2.3 8.3 %collective-permute-start = (bf16[272,128]{1,0:T(8,128)(2,1)}, bf16[272,128]{1,0:T(8,128)(2,1)S(1)}, u32[]{:S(2)}, u32[]{:S(2)}) collective-permute-start(bf16[272,128]{1,0:T(8,128)(2,1)} %shard_map.68.chunk_ref), channel_id=1, source_target_pairs={{0,1},{1,0},{2,3},{3,2},{4,5},{5,4},{6,7},{7,6},{8,9},{9,8},{10,11... | collective-permute-start | bytes 208904 | tf_op jit(solution)/shard_map/ppermute | solution.py:117
  10.6 0.9 copy-done
  11.4 0.9 shard_map.69.same_ref
  12.3 0.2 collective-permute-done.chunk_ref
  12.5 0.9 shard_map.70
  13.4 10.0 %all-to-all-start = ((bf16[8,544,128]{2,1,0:T(8,128)(2,1)}), bf16[8,544,128]{2,1,0:T(8,128)(2,1)S(1)}, u32[]{:S(2)}, u32[]{:S(2)}) async-start(bf16[8,544,128]{2,1,0:T(8,128)(2,1)} %shard_map.70), calls=%async_computation | async-start | bytes 2228224 | tf_op jit(solution)/shard_map/all_to_all | solution.py:139
  23.4 28.7 %all-to-all-done = bf16[8,544,128]{2,1,0:T(8,128)(2,1)S(1)} async-done(((bf16[8,544,128]{2,1,0:T(8,128)(2,1)}), bf16[8,544,128]{2,1,0:T(8,128)(2,1)S(1)}, u32[]{:S(2)}, u32[]{:S(2)}) %all-to-all-start) | async-done | bytes 1114144 | tf_op jit(solution)/shard_map/all_to_all | solution.py:139
  52.2 0.1 constant_dynamic-slice_fusion
  52.3 5.5 %collective-permute-start.2 = (bf16[16,144,128]{2,1,0:T(8,128)(2,1)S(1)}, bf16[16,144,128]{2,1,0:T(8,128)(2,1)S(1)}, u32[]{:S(2)}, u32[]{:S(2)}) collective-permute-start(bf16[16,144,128]{2,1,0:T(8,128)(2,1)S(1)} %get-tuple-element.38), channel_id=1, source_target_pairs={{0,497},{1,496},{2,499},{3,498},{4,501},{5,500},{6,503},{7,502},{8... | collective-permute-start | bytes 1769480 | tf_op jit(solution)/shard_map/ppermute | solution.py:42
  57.8 8.0 %collective-permute-start.1 = (bf16[16,144,128]{2,1,0:T(8,128)(2,1)S(1)}, bf16[16,144,128]{2,1,0:T(8,128)(2,1)S(1)}, u32[]{:S(2)}, u32[]{:S(2)}) collective-permute-start(bf16[16,144,128]{2,1,0:T(8,128)(2,1)S(1)} %get-tuple-element.39), channel_id=1, source_target_pairs={{0,16},{1,17},{2,18},{3,19},{4,20},{5,21},{6,22},{7,23},{8,24},{9,... | collective-permute-start | bytes 1769480 | tf_op jit(solution)/shard_map/ppermute | solution.py:42
  65.8 5.1 %shard_map.71 = (f32[26,256,256]{2,1,0:T(8,128)S(1)}, f32[52,256,256]{2,1,0:T(8,128)S(1)}, bf16[8,256,256]{2,1,0:T(8,128)(2,1)S(1)}, f32[2,8,256]{2,1,0:T(8,128)...) custom-call(s32[8]{0:T(128)S(1)} %copy-done.1, bf16[5,256,256]{2,1,0:T(8,128)(2,1)S(1)} %copy-done.2, ...), custom_call_target="tpu_custom_call" | custom-call | flops 3355443200 | bytes 20971520 | tf_op jit(solution)/shard_map/pallas_call | solution.py:270
  70.8 0.0 collective-permute-done.2.b_ref
  70.9 2.2 %shard_map.72 = (f32[20,256,256]{2,1,0:T(8,128)S(1)}, f32[2,8,256]{2,1,0:T(8,128)S(1)}, f32[2,4,256]{2,1,0:T(4,128)S(1)}, f32[2,4,256]{2,1,0:T(4,128)S(1)}) custom-call(s32[8]{0:T(128)S(1)} %copy-done.1, bf16[8,256,256]{2,1,0:T(8,128)(2,1)S(1)} %get-tuple-element.23.xt_ref, bf16[16,144,128]{2,1,0:T(8,128)(2,1)S(1)} %collective-permute-done.1.a_ref, ...), custom_call_target="tpu_custom_call" | custom-call | tf_op jit(solution)/shard_map/pallas_call | solution.py:353
  73.1 1.9 %collective-permute-start.3 = (f32[2,4,256]{2,1,0:T(4,128)S(1)}, f32[2,4,256]{2,1,0:T(4,128)S(1)}, u32[]{:S(2)}, u32[]{:S(2)}) collective-permute-start(f32[2,4,256]{2,1,0:T(4,128)S(1)} %get-tuple-element.29), channel_id=1, source_target_pairs={{0,497},{1,496},{2,499},{3,498},{4,501},{5,500},{6,503},{7,502},{8... | collective-permute-start | bytes 24584 | tf_op jit(solution)/shard_map/ppermute | solution.py:42
  75.0 7.5 %collective-permute-start.4 = (f32[2,4,256]{2,1,0:T(4,128)S(1)}, f32[2,4,256]{2,1,0:T(4,128)S(1)}, u32[]{:S(2)}, u32[]{:S(2)}) collective-permute-start(f32[2,4,256]{2,1,0:T(4,128)S(1)} %get-tuple-element.30), channel_id=1, source_target_pairs={{0,16},{1,17},{2,18},{3,19},{4,20},{5,21},{6,22},{7,23},{8,24},{9,... | collective-permute-start | bytes 24584 | tf_op jit(solution)/shard_map/ppermute | solution.py:42
  82.5 1.9 %shard_map.73.part_ref = f32[2,8,256]{2,1,0:T(8,128)S(1)} custom-call(f32[2,8,256]{2,1,0:T(8,128)S(1)} %get-tuple-element.26.p_ref.p1_ref, f32[8,256]{1,0:T(8,128)S(1)} %get-tuple-element.27.obs_ref, f32[52,256,256]{2,1,0:T(8,128)S(1)} %get-tuple-element.28.inner_ref), custom_call_target="tpu_custom_call" | custom-call | flops 1677721600 | bytes 14680064 | tf_op jit(solution)/shard_map/pallas_call | solution.py:373
  84.4 0.9 shard_map.74
  85.3 1.9 %collective-permute-start.5 = (f32[2,4,256]{2,1,0:T(4,128)S(1)}, f32[2,4,256]{2,1,0:T(4,128)S(1)}, u32[]{:S(2)}, u32[]{:S(2)}) collective-permute-start(f32[2,4,256]{2,1,0:T(4,128)S(1)} %get-tuple-element.33), channel_id=1, source_target_pairs={{0,497},{1,496},{2,499},{3,498},{4,501},{5,500},{6,503},{7,502},{8... | collective-permute-start | bytes 24584 | tf_op jit(solution)/shard_map/ppermute | solution.py:42
  87.2 4.6 %collective-permute-start.6 = (f32[2,4,256]{2,1,0:T(4,128)S(1)}, f32[2,4,256]{2,1,0:T(4,128)S(1)}, u32[]{:S(2)}, u32[]{:S(2)}) collective-permute-start(f32[2,4,256]{2,1,0:T(4,128)S(1)} %get-tuple-element.34), channel_id=1, source_target_pairs={{0,16},{1,17},{2,18},{3,19},{4,20},{5,21},{6,22},{7,23},{8,24},{9,... | collective-permute-start | bytes 24584 | tf_op jit(solution)/shard_map/ppermute | solution.py:42
  91.8 1.9 %shard_map.75.part_ref = f32[2,8,256]{2,1,0:T(8,128)S(1)} custom-call(f32[2,8,256]{2,1,0:T(8,128)S(1)} %get-tuple-element.32.p_ref.p2_ref, f32[8,256]{1,0:T(8,128)S(1)} %get-tuple-element.27.obs_ref, f32[52,256,256]{2,1,0:T(8,128)S(1)} %get-tuple-element.28.inner_ref), custom_call_target="tpu_custom_call" | custom-call | flops 1677721600 | bytes 14680064 | tf_op jit(solution)/shard_map/pallas_call | solution.py:373
  93.8 1.5 %shard_map.76 = (f32[2,8,256]{2,1,0:T(8,128)S(1)}, f32[32,1,128]{2,1,0:T(1,128)S(1)}) custom-call(f32[2,8,256]{2,1,0:T(8,128)S(1)} %shard_map.75.part_ref, f32[2,4,256]{2,1,0:T(4,128)S(1)} %collective-permute-done.5.b_ref, f32[2,4,256]{2,1,0:T(4,128)S(1)} %collective-permute-done.6.a_ref, f32[20,256,256]{2,1,0:T(8,128)S(1)} %get-tuple-element.31.outer_ref, ...), custom_call_target="tpu_custom_call" | custom-call | tf_op jit(solution)/shard_map/pallas_call | solution.py:464
  95.2 10.1 %all_to_all.10.m_ref = f32[32,1,128]{2,1,0:T(1,128)S(1)} all-to-all(f32[32,1,128]{2,1,0:T(1,128)S(1)} %get-tuple-element.36), channel_id=1, replica_groups=mesh['space'=32,'member'=16] {'space'}, dimensions={0} | all-to-all | bytes 32768 | tf_op jit(solution)/shard_map/all_to_all | solution.py:559
  105.3 1.0 shard_map.77
  (10 shorter events, 0.0 us)
Async XLA Ops:
  2.3 10.3 %collective-permute-start = (bf16[272,128]{1,0:T(8,128)(2,1)}, bf16[272,128]{1,0:T(8,128)(2,1)S(1)}, u32[]{:S(2)}, u32[]{:S(2)}) collective-permute-start(bf16[272,128]{1,0:T(8,128)(2,1)} %shard_map.68.chunk_ref), channel_id=1, source_target_pairs={{0,1},{1,0},{2,3},{3,2},{4,5},{5,4},{6,7},{7,6},{8,9},{9,8},{10,11... | collective-permute-start | bytes 208904 | tf_op jit(solution)/shard_map/ppermute | solution.py:117
  10.5 0.9 copy-start
  13.4 38.8 %all-to-all-start = ((bf16[8,544,128]{2,1,0:T(8,128)(2,1)}), bf16[8,544,128]{2,1,0:T(8,128)(2,1)S(1)}, u32[]{:S(2)}, u32[]{:S(2)}) async-start(bf16[8,544,128]{2,1,0:T(8,128)(2,1)} %shard_map.70), calls=%async_computation | async-start | bytes 2228224 | tf_op jit(solution)/shard_map/all_to_all | solution.py:139
  52.2 13.6 %copy-start.1 = (s32[8]{0:T(128)S(1)}, s32[8]{0:T(128)}, u32[]{:S(2)}) copy-start(s32[8]{0:T(128)} %reach_ref.1) | copy-start | bytes 100
  52.2 13.6 %copy-start.2 = (bf16[5,256,256]{2,1,0:T(8,128)(2,1)S(1)}, bf16[5,256,256]{2,1,0:T(8,128)(2,1)}, u32[]{:S(2)}) copy-start(bf16[5,256,256]{2,1,0:T(8,128)(2,1)} %loc_ref) | copy-start | bytes 1966084
  52.3 18.6 %collective-permute-start.2 = (bf16[16,144,128]{2,1,0:T(8,128)(2,1)S(1)}, bf16[16,144,128]{2,1,0:T(8,128)(2,1)S(1)}, u32[]{:S(2)}, u32[]{:S(2)}) collective-permute-start(bf16[16,144,128]{2,1,0:T(8,128)(2,1)S(1)} %get-tuple-element.38), channel_id=1, source_target_pairs={{0,497},{1,496},{2,499},{3,498},{4,501},{5,500},{6,503},{7,502},{8... | collective-permute-start | bytes 1769480 | tf_op jit(solution)/shard_map/ppermute | solution.py:42
  57.8 13.1 %collective-permute-start.1 = (bf16[16,144,128]{2,1,0:T(8,128)(2,1)S(1)}, bf16[16,144,128]{2,1,0:T(8,128)(2,1)S(1)}, u32[]{:S(2)}, u32[]{:S(2)}) collective-permute-start(bf16[16,144,128]{2,1,0:T(8,128)(2,1)S(1)} %get-tuple-element.39), channel_id=1, source_target_pairs={{0,16},{1,17},{2,18},{3,19},{4,20},{5,21},{6,22},{7,23},{8,24},{9,... | collective-permute-start | bytes 1769480 | tf_op jit(solution)/shard_map/ppermute | solution.py:42
  73.1 11.3 %collective-permute-start.3 = (f32[2,4,256]{2,1,0:T(4,128)S(1)}, f32[2,4,256]{2,1,0:T(4,128)S(1)}, u32[]{:S(2)}, u32[]{:S(2)}) collective-permute-start(f32[2,4,256]{2,1,0:T(4,128)S(1)} %get-tuple-element.29), channel_id=1, source_target_pairs={{0,497},{1,496},{2,499},{3,498},{4,501},{5,500},{6,503},{7,502},{8... | collective-permute-start | bytes 24584 | tf_op jit(solution)/shard_map/ppermute | solution.py:42
  75.0 9.4 %collective-permute-start.4 = (f32[2,4,256]{2,1,0:T(4,128)S(1)}, f32[2,4,256]{2,1,0:T(4,128)S(1)}, u32[]{:S(2)}, u32[]{:S(2)}) collective-permute-start(f32[2,4,256]{2,1,0:T(4,128)S(1)} %get-tuple-element.30), channel_id=1, source_target_pairs={{0,16},{1,17},{2,18},{3,19},{4,20},{5,21},{6,22},{7,23},{8,24},{9,... | collective-permute-start | bytes 24584 | tf_op jit(solution)/shard_map/ppermute | solution.py:42
  85.3 8.4 %collective-permute-start.5 = (f32[2,4,256]{2,1,0:T(4,128)S(1)}, f32[2,4,256]{2,1,0:T(4,128)S(1)}, u32[]{:S(2)}, u32[]{:S(2)}) collective-permute-start(f32[2,4,256]{2,1,0:T(4,128)S(1)} %get-tuple-element.33), channel_id=1, source_target_pairs={{0,497},{1,496},{2,499},{3,498},{4,501},{5,500},{6,503},{7,502},{8... | collective-permute-start | bytes 24584 | tf_op jit(solution)/shard_map/ppermute | solution.py:42
  87.2 6.5 %collective-permute-start.6 = (f32[2,4,256]{2,1,0:T(4,128)S(1)}, f32[2,4,256]{2,1,0:T(4,128)S(1)}, u32[]{:S(2)}, u32[]{:S(2)}) collective-permute-start(f32[2,4,256]{2,1,0:T(4,128)S(1)} %get-tuple-element.34), channel_id=1, source_target_pairs={{0,16},{1,17},{2,18},{3,19},{4,20},{5,21},{6,22},{7,23},{8,24},{9,... | collective-permute-start | bytes 24584 | tf_op jit(solution)/shard_map/ppermute | solution.py:42
